TPU v7x, 32 devices: a whole 2x2x4 slice. The times are simulated.
32 devices in a mesh: section: 4 (over y, core), dp: 8 (over z, x).
Axes of the slice: x: 2, y: 2, z: 4, core: 2. Of those that a mesh axis runs over, the one named last changes fastest.
Arguments:
- patches: bfloat16 [2048, 192], P('dp'), may hold values from -6 to 6
- var_ids: int32 [48], replicated, may hold values from 0 to 47, each once
- segment_ids: int32 [16, 128], P('dp'), may hold values from 0 to 7, never falling along the last dimension, each value on 1 to 32 neighbouring positions
- embed_weight: bfloat16 [1024, 192], P('dp'), may hold values from -3 to 3
- var_embed: float32 [48, 1024], replicated, may hold values from -3 to 3
- agg_query: float32 [1024], replicated, may hold values from -6 to 6
- agg_wq: bfloat16 [1024, 1024], P('dp'), may hold values from -0.1875 to 0.1875
- agg_bq: float32 [1024], replicated, may hold values from -3 to 3
- agg_wk: bfloat16 [1024, 1024], P('dp'), may hold values from -0.1875 to 0.1875
- agg_wv: bfloat16 [1024, 1024], P('dp'), may hold values from -0.1875 to 0.1875
- agg_bv: float32 [1024], replicated, may hold values from -2 to 2
- agg_wo: bfloat16 [1024, 1024], P('dp'), may hold values from -0.1875 to 0.1875
- agg_bo: float32 [1024], replicated, may hold values from -2 to 2
- attn_norm_gain: float32 [1024], replicated, may hold values from 0.1 to 1.9
- attn_norm_bias: float32 [1024], replicated, may hold values from -2 to 2
- attn_wqkv: bfloat16 [1024, 3072], P('dp'), may hold values from -0.1875 to 0.1875
- attn_bq: float32 [1024], replicated, may hold values from -2 to 2
- attn_bv: float32 [1024], replicated, may hold values from -2 to 2
- attn_wo: bfloat16 [1024, 1024], P('dp'), may hold values from -1 to 1
- attn_bo: float32 [1024], replicated, may hold values from -2 to 2
- mlp_norm_gain: float32 [1024], replicated, may hold values from 0.1 to 1.9
- mlp_norm_bias: float32 [1024], replicated, may hold values from -2 to 2
- mlp_up: bfloat16 [1024, 4096], P('dp'), may hold values from -0.1875 to 0.1875
- mlp_bup: float32 [4096], replicated, may hold values from -2 to 2
- mlp_down: bfloat16 [1024, 4096], P('dp'), may hold values from -0.125 to 0.125
- mlp_bdown: float32 [1024], replicated, may hold values from -2 to 2
- cotangent: bfloat16 [2048, 1024], P('dp', 'section'), may hold values from -8 to 8
Outputs:
- activations: bfloat16 [2048, 1024], P('dp', 'section')
- patches_grad: bfloat16 [2048, 192], P('dp', 'section')
- embed_weight_grad: float32 [1024, 192], P('dp')
- var_embed_grad: float32 [48, 1024], P(None, 'dp')
- agg_query_grad: float32 [1024], P('dp')
- agg_wq_grad: float32 [1024, 1024], P('dp')
- agg_bq_grad: float32 [1024], P('dp')
- agg_wk_grad: float32 [1024, 1024], P('dp')
- agg_wv_grad: float32 [1024, 1024], P('dp')
- agg_bv_grad: float32 [1024], P('dp')
- agg_wo_grad: float32 [1024, 1024], P('dp')
- agg_bo_grad: float32 [1024], P('dp')
- attn_norm_gain_grad: float32 [1024], P('dp')
- attn_norm_bias_grad: float32 [1024], P('dp')
- attn_wqkv_grad: float32 [1024, 3072], P('dp')
- attn_bq_grad: float32 [1024], P('dp')
- attn_bv_grad: float32 [1024], P('dp')
- attn_wo_grad: float32 [1024, 1024], P('dp')
- attn_bo_grad: float32 [1024], P('dp')
- mlp_norm_gain_grad: float32 [1024], P('dp')
- mlp_norm_bias_grad: float32 [1024], P('dp')
- mlp_up_grad: float32 [1024, 4096], P('dp')
- mlp_bup_grad: float32 [4096], P('dp')
- mlp_down_grad: float32 [1024, 4096], P('dp')
- mlp_bdown_grad: float32 [1024], P('dp')
Inputs may be any that keep to these rules, and one draw needn't show every extreme that they name: `segment_ids`: in every sequence the ids never decrease, each of the 8 subgrids holds one to a quarter of 128 patches, and one holds exactly a quarter. `var_ids`: each of the 48 variables belongs to exactly one input channel.
All inputs are finite; a program needn't handle non-finite values.
Results may differ from a plain program's by a relative error of at most 0.028.
Values may be sent and summed in bfloat16 or wider, within the bound.
A program may use at most 320 MiB of HBM per device.

v0:
```python
from functools import partial

import jax
import jax.numpy as jnp
from jax import lax
from jax.sharding import PartitionSpec as P

D = 1024
HEADS = 16
HEAD = 64
FF = 4096
VARS = 48
PIX = 4
LEN = 128
MB = 2


highest = lax.Precision.HIGHEST
blocked = -1000000000.0
epsilon = 1e-05


def shortened(x):
    return jax.tree.map(lambda a: a.astype(jnp.bfloat16) if a.dtype == jnp.float32 else a, x)


def shifted(x, axis, by):
    count = lax.axis_size(axis)
    pairs = [(i, i + by) for i in range(count) if 0 <= i + by < count]
    return lax.ppermute(x, axis, pairs)


def project(row_block, matrix):
    return jnp.dot(row_block, matrix, preferred_element_type=jnp.float32)


def project_back(row_block, matrix):
    return jnp.einsum("ta,ba->tb", row_block, matrix, preferred_element_type=jnp.float32)


def outer_sum(left_rows, right_rows):
    return jnp.einsum("ta,tb->ab", left_rows, right_rows, preferred_element_type=jnp.float32)


def layer_norm(row_block, norm_gain, shift_vec):
    averaged = jnp.mean(row_block, axis=-1, keepdims=True)
    centred = row_block - averaged
    variance = jnp.mean(centred * centred, axis=-1, keepdims=True)
    return centred * lax.rsqrt(variance + epsilon) * norm_gain + shift_vec


def embed_rows(patch_rows, picked_weight, picked_embed):
    grouped = patch_rows.reshape(patch_rows.shape[0], VARS, PIX)
    embedded = jnp.einsum(
        "tcp,dcp->tcd", grouped, picked_weight, preferred_element_type=jnp.float32
    )
    return (embedded + picked_embed[None]).astype(jnp.bfloat16)


def embed_back(patch_rows, grad_embedded, picked_weight, chosen_float):
    grouped = patch_rows.reshape(patch_rows.shape[0], VARS, PIX)
    grad_patch = jnp.einsum(
        "tcd,dcp->tcp", grad_embedded, picked_weight, preferred_element_type=jnp.float32
    )
    grad_patch = grad_patch.reshape(patch_rows.shape[0], VARS * PIX).astype(jnp.bfloat16)
    grad_picked = jnp.einsum(
        "tcd,tcp->dcp", grad_embedded, grouped, preferred_element_type=jnp.float32
    )
    grad_weight = jnp.einsum("dcp,cv->dvp", grad_picked, chosen_float, precision=highest).reshape(
        D, VARS * PIX
    )
    grad_var = jnp.dot(
        chosen_float.T, jnp.sum(grad_embedded, axis=0, dtype=jnp.float32), precision=highest
    )
    return (grad_patch, grad_weight, grad_var)


def aggregate_parts(embedded, key_query):
    scores = jnp.einsum("tcd,dh->tch", embedded, key_query, preferred_element_type=jnp.float32)
    weights = jax.nn.softmax(scores, axis=1)
    weights_low = weights.astype(jnp.bfloat16)
    mixture = jnp.einsum("tch,tcd->thd", weights_low, embedded, preferred_element_type=jnp.float32)
    return (weights, weights_low, mixture.astype(jnp.bfloat16))


def context_rows(mixture, value_w, value_b):
    context = jnp.einsum(
        "thd,dhj->thj", mixture, value_w.reshape(D, HEADS, HEAD), preferred_element_type=jnp.float32
    )
    return (context.reshape(mixture.shape[0], D) + value_b).astype(jnp.bfloat16)


def aggregate_rows(embedded, key_query, value_w, value_b, out_w, out_b):
    weights, weights_low, mixture = aggregate_parts(embedded, key_query)
    context = context_rows(mixture, value_w, value_b)
    return (project(context, out_w) + out_b).astype(jnp.bfloat16)


def aggregate_back(embedded, key_query, value_w, value_b, out_w, grad_rows):
    weights, weights_low, mixture = aggregate_parts(embedded, key_query)
    context = context_rows(mixture, value_w, value_b)
    grad_out_w = outer_sum(context, grad_rows)
    grad_out_b = jnp.sum(grad_rows, axis=0, dtype=jnp.float32)
    grad_context = project_back(grad_rows, out_w).astype(jnp.bfloat16)
    grad_value_b = jnp.sum(grad_context, axis=0, dtype=jnp.float32)
    context_heads = grad_context.reshape(grad_context.shape[0], HEADS, HEAD)
    grad_value_w = jnp.einsum(
        "thd,thj->dhj", mixture, context_heads, preferred_element_type=jnp.float32
    ).reshape(D, D)
    grad_mixture = jnp.einsum(
        "thj,dhj->thd",
        context_heads,
        value_w.reshape(D, HEADS, HEAD),
        preferred_element_type=jnp.float32,
    )
    grad_mixture = grad_mixture.astype(jnp.bfloat16)
    grad_weights = jnp.einsum(
        "thd,tcd->tch", grad_mixture, embedded, preferred_element_type=jnp.float32
    )
    grad_scores = weights * (grad_weights - jnp.sum(weights * grad_weights, axis=1, keepdims=True))
    grad_scores = grad_scores.astype(jnp.bfloat16)
    grad_embedded = jnp.einsum(
        "tch,thd->tcd", weights_low, grad_mixture, preferred_element_type=jnp.float32
    )
    grad_embedded = grad_embedded + jnp.einsum(
        "tch,dh->tcd", grad_scores, key_query, preferred_element_type=jnp.float32
    )
    grad_key_query = jnp.einsum(
        "tcd,tch->dh", embedded, grad_scores, preferred_element_type=jnp.float32
    )
    return (
        grad_embedded.astype(jnp.bfloat16),
        grad_key_query,
        grad_value_w,
        grad_value_b,
        grad_out_w,
        grad_out_b,
    )


def query_back(grad_key_query, query_low, query_proj, query_w, key_w):
    score_scale = HEAD ** (-0.5)
    key_heads = key_w.reshape(D, HEADS, HEAD).astype(jnp.float32)
    grad_proj = (
        jnp.einsum("dhj,dh->hj", key_heads, grad_key_query, precision=highest).reshape(D)
        * score_scale
    )
    grad_key_w = (grad_key_query[:, :, None] * query_proj.reshape(HEADS, HEAD)[None]).reshape(
        D, D
    ) * score_scale
    grad_query_w = query_low.astype(jnp.float32)[:, None] * grad_proj[None, :]
    grad_query = jnp.dot(query_w.astype(jnp.float32), grad_proj, precision=highest)
    return (grad_query_w, grad_key_w, grad_proj, grad_query)


def attention_parts(normed, segments, qkv_w, query_b, value_b):
    projected = project(normed, qkv_w)
    shaped = (normed.shape[0], HEADS, HEAD)
    queries = (projected[:, :D] + query_b).astype(jnp.bfloat16).reshape(shaped)
    keys_rows = projected[:, D : 2 * D].astype(jnp.bfloat16).reshape(shaped)
    values = (projected[:, 2 * D :] + value_b).astype(jnp.bfloat16).reshape(shaped)
    scores = jnp.einsum(
        "thj,uhj->htu", queries, keys_rows, preferred_element_type=jnp.float32
    ) * HEAD ** (-0.5)
    same_segment = segments[:, None] == segments[None, :]
    return (queries, keys_rows, values, jnp.where(same_segment[None], scores, blocked))


def attention_rows(inputs, segments, norm_gain, shift_vec, qkv_w, query_b, value_b, out_w, out_b):
    inputs_float = inputs.astype(jnp.float32)
    normed = layer_norm(inputs_float, norm_gain, shift_vec).astype(jnp.bfloat16)
    queries, keys_rows, values, scores = attention_parts(normed, segments, qkv_w, query_b, value_b)
    row_peak = jnp.max(scores, axis=-1, keepdims=True)
    row_total = jnp.sum(jnp.exp(scores - row_peak), axis=-1, keepdims=True)
    log_totals = row_peak + jnp.log(row_total)
    prob_rows = jnp.exp(scores - log_totals).astype(jnp.bfloat16)
    attended = jnp.einsum("htu,uhj->thj", prob_rows, values, preferred_element_type=jnp.float32)
    attended = attended.reshape(inputs.shape[0], D).astype(jnp.bfloat16)
    result = inputs_float + project(attended, out_w) + out_b
    return (result.astype(jnp.bfloat16), log_totals[:, :, 0])


def attention_back(
    inputs, segments, log_totals, grad_rows, norm_gain, shift_vec, qkv_w, query_b, value_b, out_w
):
    inputs_float = inputs.astype(jnp.float32)
    normed_float, norm_pull = jax.vjp(layer_norm, inputs_float, norm_gain, shift_vec)
    normed = normed_float.astype(jnp.bfloat16)
    queries, keys_rows, values, scores = attention_parts(normed, segments, qkv_w, query_b, value_b)
    prob_float = jnp.exp(scores - log_totals[:, :, None])
    prob_rows = prob_float.astype(jnp.bfloat16)
    attended = jnp.einsum("htu,uhj->thj", prob_rows, values, preferred_element_type=jnp.float32)
    attended = attended.reshape(inputs.shape[0], D).astype(jnp.bfloat16)
    grad_out_w = outer_sum(attended, grad_rows)
    grad_out_b = jnp.sum(grad_rows, axis=0, dtype=jnp.float32)
    grad_attended = (
        project_back(grad_rows, out_w).astype(jnp.bfloat16).reshape(inputs.shape[0], HEADS, HEAD)
    )
    grad_values = jnp.einsum(
        "htu,thj->uhj", prob_rows, grad_attended, preferred_element_type=jnp.float32
    ).astype(jnp.bfloat16)
    grad_probs = jnp.einsum(
        "thj,uhj->htu", grad_attended, values, preferred_element_type=jnp.float32
    )
    grad_scores = prob_float * (
        grad_probs - jnp.sum(prob_float * grad_probs, axis=-1, keepdims=True)
    )
    grad_scores = grad_scores.astype(jnp.bfloat16)
    score_scale = HEAD ** (-0.5)
    grad_queries = (
        jnp.einsum("htu,uhj->thj", grad_scores, keys_rows, preferred_element_type=jnp.float32)
        * score_scale
    )
    grad_keys = (
        jnp.einsum("htu,thj->uhj", grad_scores, queries, preferred_element_type=jnp.float32)
        * score_scale
    )
    grad_queries = grad_queries.astype(jnp.bfloat16).reshape(inputs.shape[0], D)
    grad_keys = grad_keys.astype(jnp.bfloat16).reshape(inputs.shape[0], D)
    grad_values = grad_values.reshape(inputs.shape[0], D)
    grad_query_b = jnp.sum(grad_queries, axis=0, dtype=jnp.float32)
    grad_value_b = jnp.sum(grad_values, axis=0, dtype=jnp.float32)
    grad_proj = jnp.concatenate([grad_queries, grad_keys, grad_values], axis=1)
    grad_qkv_w = outer_sum(normed, grad_proj)
    grad_normed = project_back(grad_proj, qkv_w)
    grad_inputs, grad_gain, grad_shift = norm_pull(grad_normed)
    grad_inputs = (grad_rows.astype(jnp.float32) + grad_inputs).astype(jnp.bfloat16)
    return (
        grad_inputs,
        grad_gain,
        grad_shift,
        grad_qkv_w,
        grad_query_b,
        grad_value_b,
        grad_out_w,
        grad_out_b,
    )


def mlp_rows(inputs, norm_gain, shift_vec, up_w, up_b, down_w, down_b):
    inputs_float = inputs.astype(jnp.float32)
    normed = layer_norm(inputs_float, norm_gain, shift_vec).astype(jnp.bfloat16)
    hidden = project(normed, up_w) + up_b
    activated = jax.nn.gelu(hidden, approximate=False).astype(jnp.bfloat16)
    return (inputs_float + project_back(activated, down_w) + down_b).astype(jnp.bfloat16)


def mlp_back(inputs, grad_rows, norm_gain, shift_vec, up_w, up_b, down_w):
    inputs_float = inputs.astype(jnp.float32)
    normed_float, norm_pull = jax.vjp(layer_norm, inputs_float, norm_gain, shift_vec)
    normed = normed_float.astype(jnp.bfloat16)
    hidden = project(normed, up_w) + up_b
    activated_float, gelu_pull = jax.vjp(partial(jax.nn.gelu, approximate=False), hidden)
    activated = activated_float.astype(jnp.bfloat16)
    grad_down = outer_sum(grad_rows, activated)
    grad_down_b = jnp.sum(grad_rows, axis=0, dtype=jnp.float32)
    grad_activated = project(grad_rows, down_w)
    grad_hidden = gelu_pull(grad_activated)[0].astype(jnp.bfloat16)
    grad_up_b = jnp.sum(grad_hidden, axis=0, dtype=jnp.float32)
    grad_up = outer_sum(normed, grad_hidden)
    grad_normed = project_back(grad_hidden, up_w)
    grad_inputs, grad_gain, grad_shift = norm_pull(grad_normed)
    grad_inputs = (grad_rows.astype(jnp.float32) + grad_inputs).astype(jnp.bfloat16)
    return (grad_inputs, grad_gain, grad_shift, grad_up, grad_up_b, grad_down, grad_down_b)


def on_device(
    patches,
    var_ids,
    segment_ids,
    embed_weight,
    var_embed,
    agg_query,
    agg_wq,
    agg_bq,
    agg_wk,
    agg_wv,
    agg_bv,
    agg_wo,
    agg_bo,
    attn_norm_gain,
    attn_norm_bias,
    attn_wqkv,
    attn_bq,
    attn_bv,
    attn_wo,
    attn_bo,
    mlp_norm_gain,
    mlp_norm_bias,
    mlp_up,
    mlp_bup,
    mlp_down,
    mlp_bdown,
    cotangent,
):
    section_id = lax.axis_index("section")
    dp_count = lax.axis_size("dp")
    flat_width = 2 * FF
    patch_cols = VARS * PIX
    up_rows = FF // D

    def padded(pieces):
        joined = jnp.concatenate(pieces, axis=1)
        return jnp.pad(joined, ((0, 0), (0, flat_width - joined.shape[1])))

    candidates = [
        padded([embed_weight]),
        padded([agg_wq, agg_wk, agg_wv, agg_wo]),
        padded([attn_wqkv, attn_wo]),
        padded([mlp_up, mlp_down]),
    ]
    packed = lax.dynamic_index_in_dim(jnp.stack(candidates), section_id, 0, keepdims=False)
    weights = lax.all_gather(packed, "dp", axis=0, tiled=True)
    embed_full = weights[:, 0:patch_cols].reshape(D, VARS, PIX)
    chosen = var_ids[:, None] == jnp.arange(VARS, dtype=jnp.int32)[None, :]
    chosen_float = chosen.astype(jnp.float32)
    picked_weight = jnp.einsum(
        "dvp,cv->dcp", embed_full, chosen.astype(jnp.bfloat16), preferred_element_type=jnp.float32
    )
    picked_weight = picked_weight.astype(jnp.bfloat16)
    picked_embed = jnp.dot(chosen_float, var_embed, precision=highest)
    query_w = weights[:, 0:D]
    key_w = weights[:, D : 2 * D]
    value_w = weights[:, 2 * D : 3 * D]
    agg_out_w = weights[:, 3 * D : 4 * D]
    query_low = agg_query.astype(jnp.bfloat16)
    query_proj = jnp.dot(query_low, query_w, preferred_element_type=jnp.float32) + agg_bq
    key_query = jnp.einsum(
        "dhj,hj->dh",
        key_w.reshape(D, HEADS, HEAD).astype(jnp.float32),
        query_proj.reshape(HEADS, HEAD),
        precision=highest,
    )
    key_query = (key_query * HEAD ** (-0.5)).astype(jnp.bfloat16)
    qkv_w = weights[:, : 3 * D]
    attn_out_w = weights[:, 3 * D : 4 * D]
    up_w = weights[:, :FF]
    down_w = weights[:, FF:]
    grads_cols = lax.all_gather(cotangent, "section", axis=1, tiled=True)
    patch_blocks = patches.reshape(MB, LEN, patch_cols)
    zero_rows = jnp.zeros((LEN, D), jnp.bfloat16)
    zero_total = jnp.zeros((HEADS, LEN), jnp.float32)
    zero_big = jnp.zeros((LEN, VARS, D), jnp.bfloat16)
    zero_thin = jnp.zeros((LEN, 1, D), jnp.bfloat16)
    zero_patch = jnp.zeros((LEN, patch_cols), jnp.bfloat16)
    big_in = {}
    rows_in = {}
    totals_kept = {}
    rows_kept = {}
    tick_count = MB + 3

    def forward_branch(section_index, micro_batch, tick_index, with_big):
        live_now = 0 <= micro_batch < MB

        def branch():
            rows_out, total_out = (zero_rows, zero_total)
            big_out = zero_big if with_big else zero_thin
            if live_now and section_index == 0:
                big_out = embed_rows(patch_blocks[micro_batch], picked_weight, picked_embed)
            if live_now and section_index == 1:
                rows_out = aggregate_rows(
                    big_in[micro_batch], key_query, value_w, agg_bv, agg_out_w, agg_bo
                )
            if live_now and section_index == 2:
                rows_out, total_out = attention_rows(
                    rows_in[tick_index - 1],
                    segment_ids[micro_batch],
                    attn_norm_gain,
                    attn_norm_bias,
                    qkv_w,
                    attn_bq,
                    attn_bv,
                    attn_out_w,
                    attn_bo,
                )
            if live_now and section_index == 3:
                rows_out = mlp_rows(
                    rows_in[tick_index - 1],
                    mlp_norm_gain,
                    mlp_norm_bias,
                    up_w,
                    mlp_bup,
                    down_w,
                    mlp_bdown,
                )
            return (rows_out, total_out, big_out)

        return branch

    for tick_index in range(tick_count):
        with_big = tick_index < MB
        branches = [
            forward_branch(section_index, tick_index - section_index, tick_index, with_big)
            for section_index in range(4)
        ]
        outputs = lax.switch(section_id, branches)
        rows_kept[tick_index] = outputs[0]
        totals_kept[tick_index] = outputs[1]
        if tick_index <= MB + 1:
            rows_in[tick_index], big_in[tick_index] = shifted(
                (shortened(outputs[0]), shortened(outputs[2])), "section", 1
            )
    flat_grads = jnp.zeros((D, flat_width), jnp.float32)
    small_grads = jnp.zeros((VARS + 4, D), jnp.float32)
    early_flat = None
    early_small = None
    grads_in = {}
    big_grads_in = {}
    patch_grads = {}

    def backward_branch(
        section_index, micro_batch, tick_index, big_back, patch_back, flat_now, small_now
    ):
        live_now = 0 <= micro_batch < MB

        def branch():
            flat_next, small_next = (flat_now, small_now)
            rows_out, patch_out = (zero_rows, zero_patch)
            big_out = zero_big if big_back else zero_thin
            if live_now and section_index == 3:
                grad_y = grads_cols[micro_batch * LEN : (micro_batch + 1) * LEN]
                rows_out, grad_gain, grad_shift, grad_up, grad_up_b, grad_down, grad_down_b = (
                    mlp_back(
                        rows_in[micro_batch + 2],
                        grad_y,
                        mlp_norm_gain,
                        mlp_norm_bias,
                        up_w,
                        mlp_bup,
                        down_w,
                    )
                )
                flat_next = flat_next + jnp.concatenate([grad_up, grad_down], axis=1)
                bup_rows = (
                    grad_up_b.reshape(dp_count, up_rows, D // dp_count)
                    .transpose(1, 0, 2)
                    .reshape(up_rows, D)
                )
                small_next = (
                    small_next.at[0:3]
                    .add(jnp.stack([grad_gain, grad_shift, grad_down_b]))
                    .at[3 : 3 + up_rows]
                    .add(bup_rows)
                )
            if live_now and section_index == 2:
                (
                    rows_out,
                    grad_gain,
                    grad_shift,
                    grad_qkv_w,
                    grad_query_b,
                    grad_value_b,
                    grad_out_w,
                    grad_out_b,
                ) = attention_back(
                    rows_in[micro_batch + 1],
                    segment_ids[micro_batch],
                    totals_kept[micro_batch + 2],
                    grads_in[tick_index - 1],
                    attn_norm_gain,
                    attn_norm_bias,
                    qkv_w,
                    attn_bq,
                    attn_bv,
                    attn_out_w,
                )
                flat_next = flat_next.at[:, 0 : 4 * D].add(
                    jnp.concatenate([grad_qkv_w, grad_out_w], axis=1)
                )
                small_next = small_next.at[0:5].add(
                    jnp.stack([grad_gain, grad_shift, grad_query_b, grad_value_b, grad_out_b])
                )
            if live_now and section_index == 1:
                (
                    grad_embedded,
                    grad_key_query,
                    grad_value_w,
                    grad_value_b,
                    grad_out_w,
                    grad_out_b,
                ) = aggregate_back(
                    big_in[micro_batch],
                    key_query,
                    value_w,
                    agg_bv,
                    agg_out_w,
                    grads_in[tick_index - 1],
                )
                grad_query_w, grad_key_w, grad_proj, grad_query = query_back(
                    grad_key_query, query_low, query_proj, query_w, key_w
                )
                flat_next = flat_next.at[:, 0 : 4 * D].add(
                    jnp.concatenate([grad_query_w, grad_key_w, grad_value_w, grad_out_w], axis=1)
                )
                small_next = small_next.at[0:4].add(
                    jnp.stack([grad_query, grad_proj, grad_value_b, grad_out_b])
                )
                big_out = grad_embedded
            if live_now and section_index == 0:
                patch_out, grad_weight, grad_var = embed_back(
                    patch_blocks[micro_batch],
                    big_grads_in[tick_index - 1],
                    picked_weight,
                    chosen_float,
                )
                flat_next = flat_next.at[:, 0:patch_cols].add(grad_weight)
                small_next = small_next.at[0:VARS].add(grad_var)
            result = [flat_next, small_next, rows_out, big_out]
            if patch_back:
                result.append(patch_out)
            return tuple(result)

        return branch

    for tick_index in range(tick_count):
        big_back = 2 <= tick_index <= MB + 1
        embed_micro = tick_index - 3
        patch_back = 0 <= embed_micro < MB
        branches = [
            backward_branch(
                section_index,
                tick_index - 3 + section_index,
                tick_index,
                big_back,
                patch_back,
                flat_grads,
                small_grads,
            )
            for section_index in range(4)
        ]
        outputs = lax.switch(section_id, branches)
        flat_grads, small_grads = (outputs[0], outputs[1])
        if tick_index <= MB + 1:
            grads_in[tick_index], big_grads_in[tick_index] = shifted(
                (shortened(outputs[2]), shortened(outputs[3])), "section", -1
            )
        if patch_back:
            patch_grads[embed_micro] = outputs[-1]
    reduced_flat, reduced_small = (
        lax.psum_scatter(flat_grads, "dp", scatter_dimension=0, tiled=True),
        lax.psum_scatter(small_grads, "dp", scatter_dimension=1, tiled=True),
    )

    def owned_by(block_part, owner_section):
        return jnp.where(section_id == owner_section, block_part, jnp.zeros_like(block_part))

    gradient_terms = (
        owned_by(reduced_flat[:, 0:patch_cols], 0),
        owned_by(reduced_small[0:VARS], 0),
        owned_by(reduced_small[0], 1),
        owned_by(reduced_flat[:, 0:D], 1),
        owned_by(reduced_small[1], 1),
        owned_by(reduced_flat[:, D : 2 * D], 1),
        owned_by(reduced_flat[:, 2 * D : 3 * D], 1),
        owned_by(reduced_small[2], 1),
        owned_by(reduced_flat[:, 3 * D : 4 * D], 1),
        owned_by(reduced_small[3], 1),
        owned_by(reduced_small[0], 2),
        owned_by(reduced_small[1], 2),
        owned_by(reduced_flat[:, 0 : 3 * D], 2),
        owned_by(reduced_small[2], 2),
        owned_by(reduced_small[3], 2),
        owned_by(reduced_flat[:, 3 * D : 4 * D], 2),
        owned_by(reduced_small[4], 2),
        owned_by(reduced_small[0], 3),
        owned_by(reduced_small[1], 3),
        owned_by(reduced_flat[:, 0:FF], 3),
        owned_by(reduced_small[3 : 3 + up_rows].reshape(-1), 3),
        owned_by(reduced_flat[:, FF : 2 * FF], 3),
        owned_by(reduced_small[2], 3),
    )
    summed = (
        lax.psum(gradient_terms[0].astype(jnp.bfloat16), "section").astype(jnp.float32),
        lax.psum(gradient_terms[1].astype(jnp.bfloat16), "section").astype(jnp.float32),
        lax.psum(gradient_terms[2].astype(jnp.bfloat16), "section").astype(jnp.float32),
        lax.psum(gradient_terms[3].astype(jnp.bfloat16), "section").astype(jnp.float32),
        lax.psum(gradient_terms[4].astype(jnp.bfloat16), "section").astype(jnp.float32),
        lax.psum(gradient_terms[5].astype(jnp.bfloat16), "section").astype(jnp.float32),
        lax.psum(gradient_terms[6].astype(jnp.bfloat16), "section").astype(jnp.float32),
        lax.psum(gradient_terms[7].astype(jnp.bfloat16), "section").astype(jnp.float32),
        lax.psum(gradient_terms[8].astype(jnp.bfloat16), "section").astype(jnp.float32),
        lax.psum(gradient_terms[9].astype(jnp.bfloat16), "section").astype(jnp.float32),
        lax.psum(gradient_terms[10].astype(jnp.bfloat16), "section").astype(jnp.float32),
        lax.psum(gradient_terms[11].astype(jnp.bfloat16), "section").astype(jnp.float32),
        lax.psum(gradient_terms[12].astype(jnp.bfloat16), "section").astype(jnp.float32),
        lax.psum(gradient_terms[13].astype(jnp.bfloat16), "section").astype(jnp.float32),
        lax.psum(gradient_terms[14].astype(jnp.bfloat16), "section").astype(jnp.float32),
        lax.psum(gradient_terms[15].astype(jnp.bfloat16), "section").astype(jnp.float32),
        lax.psum(gradient_terms[16].astype(jnp.bfloat16), "section").astype(jnp.float32),
        lax.psum(gradient_terms[17].astype(jnp.bfloat16), "section").astype(jnp.float32),
        lax.psum(gradient_terms[18].astype(jnp.bfloat16), "section").astype(jnp.float32),
        lax.psum(gradient_terms[19].astype(jnp.bfloat16), "section").astype(jnp.float32),
        lax.psum(gradient_terms[20].astype(jnp.bfloat16), "section").astype(jnp.float32),
        lax.psum(gradient_terms[21].astype(jnp.bfloat16), "section").astype(jnp.float32),
        lax.psum(gradient_terms[22].astype(jnp.bfloat16), "section").astype(jnp.float32),
    )
    final_rows = jnp.concatenate([rows_kept[micro_batch + 3] for micro_batch in range(MB)], axis=0)
    grads_patch = jnp.concatenate([patch_grads[micro_batch] for micro_batch in range(MB)], axis=0)
    rows_cols, patch_out_cols = (
        lax.psum_scatter(
            owned_by(final_rows.astype(jnp.float32), 3).astype(jnp.bfloat16),
            "section",
            scatter_dimension=1,
            tiled=True,
        ).astype(jnp.float32),
        lax.psum_scatter(
            owned_by(grads_patch.astype(jnp.float32), 0).astype(jnp.bfloat16),
            "section",
            scatter_dimension=1,
            tiled=True,
        ).astype(jnp.float32),
    )
    return (rows_cols.astype(jnp.bfloat16), patch_out_cols.astype(jnp.bfloat16)) + tuple(summed)


def solution(mesh):
    in_specs = (
        P("dp", None),
        P(),
        P("dp", None),
        P("dp", None),
        P(),
        P(),
        P("dp", None),
        P(),
        P("dp", None),
        P("dp", None),
        P(),
        P("dp", None),
        P(),
        P(),
        P(),
        P("dp", None),
        P(),
        P(),
        P("dp", None),
        P(),
        P(),
        P(),
        P("dp", None),
        P(),
        P("dp", None),
        P(),
        P("dp", "section"),
    )
    out_specs = (
        P("dp", "section"),
        P("dp", "section"),
        P("dp", None),
        P(None, "dp"),
        P("dp"),
        P("dp", None),
        P("dp"),
        P("dp", None),
        P("dp", None),
        P("dp"),
        P("dp", None),
        P("dp"),
        P("dp"),
        P("dp"),
        P("dp", None),
        P("dp"),
        P("dp"),
        P("dp", None),
        P("dp"),
        P("dp"),
        P("dp"),
        P("dp", None),
        P("dp"),
        P("dp", None),
        P("dp"),
    )
    return jax.shard_map(
        on_device, mesh=mesh, in_specs=in_specs, out_specs=out_specs, check_vma=False
    )
```

profile of v0, /device:TPU:0, one launch (start us, length us, event | category | flops | bytes accessed | tf_op | source)
XLA Modules:
  0.0 2214.4 jit_solution(13762230561027469113)
XLA Ops:
  19.8 12.8 fusion.437
  36.7 229.4 %all-gather.3.cloned.1.call-done = bf16[1,1024,8192]{1,2,0:T(8,128)(2,1)} async-done(((bf16[1,128,8192]{1,2,0:T(8,128)(2,1)}), bf16[1,1024,8192]{1,2,0:T(8,128)(2,1)}) %all-gather.3.cloned.1.call-update) | async-done | bytes 16777232 | tf_op jit(solution)/shard_map/all_gather | solution.py:313
  267.6 12.8 conditional.10
  267.7 12.6 fusion
  280.5 16.5 copy.421
  317.5 38.1 %conditional.11 = (bf16[128,1024]{1,0:T(8,128)(2,1)}, bf16[128,48,1024]{2,1,0:T(8,128)(2,1)}) conditional(s32[]{:T(128)} %clamp.2, (bf16[2,128,192]{1,0,2:T(2,128)(2,1)S(1)}, bf16[1024,48,4]{0,1,2:T(8,128)(2,1)S(1)}, f32[48,1024]{1,0:T(8,128)S(1)}) %tuple.263, (bf16[128,48,1024]{2,1,0:T(8,128)(2,1)}, ...), branch_computations={%region_4.5_spmd, %region_5.8_spmd, %region_8.9_spmd, %region_9.10... | conditional | flops 942639232 | bytes 53403664 | solution.py:396
  330.2 16.4 copy.358
  355.6 117.4 %collective-permute-start.1 = (bf16[128,48,1024]{2,1,0:T(8,128)(2,1)}, bf16[128,48,1024]{2,1,0:T(8,128)(2,1)}, u32[]{:S(2)}, u32[]{:S(2)}) collective-permute-start(bf16[128,48,1024]{2,1,0:T(8,128)(2,1)} %get-tuple-element.682), channel_id=1, source_target_pairs={{0,8},{8,16},{16,24},{1,9},{9,17},{17,25},{2,10},{10,18},{18,26},{... | collective-permute-start | bytes 37748744 | tf_op jit(solution)/shard_map/ppermute | solution.py:30
  474.3 15.0 all_gather.7
  503.7 153.3 %collective-permute-start.3 = (bf16[128,1024]{1,0:T(8,128)(2,1)S(1)}, bf16[128,1024]{1,0:T(8,128)(2,1)S(1)}, u32[]{:S(2)}, u32[]{:S(2)}) collective-permute-start(bf16[128,1024]{1,0:T(8,128)(2,1)S(1)} %get-tuple-element.684), channel_id=1, source_target_pairs={{0,8},{8,16},{16,24},{1,9},{9,17},{17,25},{2,10},{10,18},{18,26},{... | collective-permute-start | bytes 786440 | tf_op jit(solution)/shard_map/ppermute | solution.py:30
  672.1 19.4 conditional.15
  713.9 18.5 conditional.17
  747.2 242.9 %collective-permute-done.8 = bf16[128,1024]{1,0:T(8,128)(2,1)} collective-permute-done((bf16[128,1024]{1,0:T(8,128)(2,1)S(1)}, bf16[128,1024]{1,0:T(8,128)(2,1)}, u32[]{:S(2)}, u32[]{:S(2)}) %collective-permute-start.8) | collective-permute-done | bytes 262176 | tf_op jit(solution)/shard_map/ppermute | solution.py:30
  990.2 77.8 %conditional.18 = (f32[1024,8192]{0,1:T(8,128)}, f32[52,1024]{1,0:T(8,128)}, bf16[128,48,1024]{2,1,0:T(8,128)(2,1)}, bf16[128,192]{0,1:T(8,128)(2,1)S(1)}) conditional(s32[]{:T(128)} %clamp.2, (f32[1024,8192]{1,0:T(8,128)}, bf16[2,128,192]{1,0,2:T(2,128)(2,1)S(1)}, bf16[128,48,1024]{2,0,1:T(8,128)(2,1)S(1)}, ...), branch_computations={%region_93.96_spmd, %region_96.103_spmd, %region_103.104_spmd, %re... | conditional | flops 2618607616 | bytes 354323264 | solution.py:531
  995.1 33.5 %copy.446 = f32[1024,8192]{0,1:T(8,128)} copy(f32[1024,8192]{1,0:T(8,128)} %get-tuple-element.1246) | data formatting | bytes 67108864 | tf_op jit(solution)/shard_map
  1081.5 227.0 %collective-permute-done.9 = bf16[128,48,1024]{2,0,1:T(8,128)(2,1)S(1)} collective-permute-done((bf16[128,48,1024]{2,0,1:T(8,128)(2,1)S(1)}, bf16[128,48,1024]{2,0,1:T(8,128)(2,1)S(1)}, u32[]{:S(2)}, u32[]{:S(2)}) %collective-permute-start.9) | collective-permute-done | bytes 12582944 | tf_op jit(solution)/shard_map/ppermute | solution.py:30
  1308.4 26.7 %conditional.19 = (f32[1024,8192]{0,1:T(8,128)}, f32[52,1024]{1,0:T(8,128)}, bf16[128,192]{0,1:T(8,128)(2,1)S(1)}) conditional(s32[]{:T(128)} %clamp.2, (f32[1024,8192]{0,1:T(8,128)}, bf16[2,128,192]{1,0,2:T(2,128)(2,1)S(1)}, bf16[128,48,1024]{2,0,1:T(8,128)(2,1)S(1)}, f32[48,48]{0,1:T(8,128)S(1)}, ...), branch_computations={%region_105.108_spmd, %region_108.109_spmd, %region_109.110_spmd, ... | conditional | flops 255221760 | bytes 97536568 | solution.py:531
  1335.2 31.1 %copy.458 = f32[1024,8192]{1,0:T(8,128)} copy(f32[1024,8192]{0,1:T(8,128)} %get-tuple-element.703) | data formatting | bytes 67108864 | tf_op jit(solution)/shard_map/cond | solution.py:531
  1366.4 118.5 %reduce-scatter.11.cloned.1.call-done = f32[52,128]{1,0:T(8,128)} async-done(((f32[52,1024]{1,0:T(8,128)}), f32[52,128]{1,0:T(8,128)}) %reduce-scatter.11.cloned.1.call-update) | async-done | bytes 26640 | tf_op jit(solution)/shard_map/reduce_scatter | solution.py:541
  1488.9 542.4 %reduce-scatter.9.cloned.1.call-done = f32[128,8192]{1,0:T(8,128)} async-done(((f32[1024,8192]{1,0:T(8,128)}), f32[128,8192]{1,0:T(8,128)}) %reduce-scatter.9.cloned.1.call-update) | async-done | bytes 4194320 | tf_op jit(solution)/shard_map/reduce_scatter | solution.py:540
  2045.5 21.5 all-reduce.9.cloned.1.call-done
  2084.9 75.0 %all-reduce.11.cloned.1.call-done = (bf16[128,1024]{1,0:T(8,128)(2,1)}, bf16[128,1024]{1,0:T(8,128)(2,1)}, bf16[128,1024]{1,0:T(8,128)(2,1)}, bf16[128,1024]{1,0...) async-done(((bf16[128,1024]{1,0:T(8,128)(2,1)}, bf16[128,1024]{1,0:T(8,128)(2,1)}, ...) | async-done | bytes 4194320 | tf_op jit(solution)/shard_map/psum | solution.py:576
  2171.5 13.3 reduce-scatter.5.cloned.1.call-done
  2184.8 22.6 %reduce-scatter.7.cloned.1.call-done = bf16[256,48]{0,1:T(8,128)(2,1)} async-done(((bf16[256,192]{0,1:T(8,128)(2,1)}), bf16[256,48]{0,1:T(8,128)(2,1)}) %reduce-scatter.7.cloned.1.call-update) | async-done | bytes 24592 | tf_op jit(solution)/shard_map/reduce_scatter | solution.py:606
  (247 shorter events, 267.3 us)
Async XLA Ops:
  7.2 258.9 %all-gather.3.cloned.1.call-start = ((), (), s32[]{:S(2)}) async-start(), calls=%async_computation.8 | async-start | bytes 18874368 | tf_op jit(solution)/shard_map/all_gather | solution.py:313
  35.5 1449.4 %reduce-scatter.11.cloned.1.call-start = ((), (), s32[]{:S(2)}) async-start(), calls=%async_computation.7 | async-start | bytes 258048 | tf_op jit(solution)/shard_map/reduce_scatter | solution.py:541
  36.4 281.1 %copy-start.31 = (bf16[2,128,192]{1,0,2:T(2,128)(2,1)}, bf16[2,128,192]{1,0,2:T(2,128)(2,1)S(1)}, u32[]{:S(2)}) copy-start(bf16[2,128,192]{1,0,2:T(2,128)(2,1)S(1)} %reshape.1072) | copy-start | bytes 294916
  297.0 20.5 collective-permute-start
  311.6 184.1 %copy-start.41 = (bf16[1024,16]{0,1:T(8,128)(2,1)}, bf16[1024,16]{0,1:T(8,128)(2,1)S(1)}, u32[]{:S(2)}) copy-start(bf16[1024,16]{0,1:T(8,128)(2,1)S(1)} %fusion.453) | copy-start | bytes 98308
  355.6 140.0 %collective-permute-start.1 = (bf16[128,48,1024]{2,1,0:T(8,128)(2,1)}, bf16[128,48,1024]{2,1,0:T(8,128)(2,1)}, u32[]{:S(2)}, u32[]{:S(2)}) collective-permute-start(bf16[128,48,1024]{2,1,0:T(8,128)(2,1)} %get-tuple-element.682), channel_id=1, source_target_pairs={{0,8},{8,16},{16,24},{1,9},{9,17},{17,25},{2,10},{10,18},{18,26},{... | collective-permute-start | bytes 37748744 | tf_op jit(solution)/shard_map/ppermute | solution.py:30
  473.0 22.6 %collective-permute-start.2 = (bf16[128,1024]{1,0:T(8,128)(2,1)}, bf16[128,1024]{1,0:T(8,128)(2,1)S(1)}, u32[]{:S(2)}, u32[]{:S(2)}) collective-permute-start(bf16[128,1024]{1,0:T(8,128)(2,1)} %get-tuple-element.683), channel_id=1, source_target_pairs={{0,8},{8,16},{16,24},{1,9},{9,17},{17,25},{2,10},{10,18},{18,26},{... | collective-permute-start | bytes 786440 | tf_op jit(solution)/shard_map/ppermute | solution.py:30
  503.6 165.0 %slice-start.4 = ((s8[6291456]{0:T(1024)(128)(4,1)}), s8[4194304]{0:T(1024)(128)(4,1)S(1)}, s32[]{:S(2)}) async-start(s8[6291456]{0:T(1024)(128)(4,1)} %bitcast.403), calls=%async_computation.15 | async-start | bytes 8388608
  503.6 165.0 %slice-start.5 = ((s8[6291456]{0:T(1024)(128)(4,1)}), s8[2097152]{0:T(1024)(128)(4,1)S(1)}, s32[]{:S(2)}) async-start(s8[6291456]{0:T(1024)(128)(4,1)} %bitcast.403), calls=%async_computation.16 | async-start | bytes 4194304
  503.7 164.9 %collective-permute-start.3 = (bf16[128,1024]{1,0:T(8,128)(2,1)S(1)}, bf16[128,1024]{1,0:T(8,128)(2,1)S(1)}, u32[]{:S(2)}, u32[]{:S(2)}) collective-permute-start(bf16[128,1024]{1,0:T(8,128)(2,1)S(1)} %get-tuple-element.684), channel_id=1, source_target_pairs={{0,8},{8,16},{16,24},{1,9},{9,17},{17,25},{2,10},{10,18},{18,26},{... | collective-permute-start | bytes 786440 | tf_op jit(solution)/shard_map/ppermute | solution.py:30
  670.0 23.4 %collective-permute-start.4 = (bf16[128,1024]{1,0:T(8,128)(2,1)}, bf16[128,1024]{1,0:T(8,128)(2,1)S(1)}, u32[]{:S(2)}, u32[]{:S(2)}) collective-permute-start(bf16[128,1024]{1,0:T(8,128)(2,1)} %get-tuple-element.685), channel_id=1, source_target_pairs={{0,8},{8,16},{16,24},{1,9},{9,17},{17,25},{2,10},{10,18},{18,26},{... | collective-permute-start | bytes 786440 | tf_op jit(solution)/shard_map/ppermute | solution.py:30
  692.2 7.8 collective-permute-start.5
  705.6 8.3 collective-permute-start.6
  732.4 257.8 %copy-start.14 = (bf16[1024,48,4]{0,1,2:T(8,128)(2,1)S(1)}, bf16[1024,48,4]{0,1,2:T(8,128)(2,1)}, u32[]{:S(2)}) copy-start(bf16[1024,48,4]{0,1,2:T(8,128)(2,1)} %copy-done.13) | copy-start | bytes 1179652
  732.4 257.8 %copy-start.32 = (bf16[2,128,192]{1,0,2:T(2,128)(2,1)S(1)}, bf16[2,128,192]{1,0,2:T(2,128)(2,1)}, u32[]{:S(2)}) copy-start(bf16[2,128,192]{1,0,2:T(2,128)(2,1)} %copy-done.31) | copy-start | bytes 294916
  744.6 245.6 %collective-permute-start.7 = (bf16[128,48,1024]{2,0,1:T(8,128)(2,1)S(1)}, bf16[128,48,1024]{2,0,1:T(8,128)(2,1)S(1)}, u32[]{:S(2)}, u32[]{:S(2)}) collective-permute-start(bf16[128,48,1024]{2,0,1:T(8,128)(2,1)S(1)} %copy.445), channel_id=1, source_target_pairs={{8,0},{16,8},{24,16},{9,1},{17,9},{25,17},{10,2},{18,10},{26,18},{... | collective-permute-start | bytes 37748744 | tf_op jit(solution)/shard_map/ppermute | solution.py:30
  745.9 244.3 %collective-permute-start.8 = (bf16[128,1024]{1,0:T(8,128)(2,1)S(1)}, bf16[128,1024]{1,0:T(8,128)(2,1)}, u32[]{:S(2)}, u32[]{:S(2)}) collective-permute-start(bf16[128,1024]{1,0:T(8,128)(2,1)S(1)} %copy-done.61), channel_id=1, source_target_pairs={{8,0},{16,8},{24,16},{9,1},{17,9},{25,17},{10,2},{18,10},{26,18},{... | collective-permute-start | bytes 786440 | tf_op jit(solution)/shard_map/ppermute | solution.py:30
  1068.0 240.4 %copy-start.15 = (bf16[1024,48,4]{0,1,2:T(8,128)(2,1)S(1)}, bf16[1024,48,4]{0,1,2:T(8,128)(2,1)}, u32[]{:S(2)}) copy-start(bf16[1024,48,4]{0,1,2:T(8,128)(2,1)} %copy-done.13) | copy-start | bytes 1179652
  1080.2 228.3 %collective-permute-start.9 = (bf16[128,48,1024]{2,0,1:T(8,128)(2,1)S(1)}, bf16[128,48,1024]{2,0,1:T(8,128)(2,1)S(1)}, u32[]{:S(2)}, u32[]{:S(2)}) collective-permute-start(bf16[128,48,1024]{2,0,1:T(8,128)(2,1)S(1)} %copy.454), channel_id=1, source_target_pairs={{8,0},{16,8},{24,16},{9,1},{17,9},{25,17},{10,2},{18,10},{26,18},{... | collective-permute-start | bytes 37748744 | tf_op jit(solution)/shard_map/ppermute | solution.py:30
  1335.2 696.1 %reduce-scatter.9.cloned.1.call-start = ((), (), s32[]{:S(2)}) async-start(), calls=%async_computation.6 | async-start | bytes 37748736 | tf_op jit(solution)/shard_map/reduce_scatter | solution.py:540
  1366.3 700.6 %all-reduce.9.cloned.1.call-start = ((), (), s32[]{:S(2)}) async-start(), calls=%async_computation.9 | async-start | bytes 169984 | tf_op jit(solution)/shard_map/psum | solution.py:573
  2032.9 127.0 %all-reduce.11.cloned.1.call-start = ((), (), s32[]{:S(2)}) async-start(), calls=%async_computation.10 | async-start | bytes 8388608 | tf_op jit(solution)/shard_map/psum | solution.py:576
  2041.9 142.9 %reduce-scatter.5.cloned.1.call-start = ((), (), s32[]{:S(2)}) async-start(), calls=%async_computation.4 | async-start | bytes 655360 | tf_op jit(solution)/shard_map/reduce_scatter | solution.py:600
  2044.7 162.7 %reduce-scatter.7.cloned.1.call-start = ((), (), s32[]{:S(2)}) async-start(), calls=%async_computation.5 | async-start | bytes 122880 | tf_op jit(solution)/shard_map/reduce_scatter | solution.py:606
  (49 other events, 1024.4 us)
Sparse Core Ops, SparseCore 0:
  35.6 230.4 all-gather.2
  1335.3 149.5 reduce-scatter.10
  1489.1 542.1 reduce-scatter.8
  2036.7 30.2 all-reduce.8
  2071.4 88.4 all-reduce.10
  2163.0 21.7 reduce-scatter.4
  2187.8 19.5 reduce-scatter.6
where the time goes:
time: 2230 us; the launch traced here: 2210 us
  waiting for transfers between devices  1510 us (68%)
  starting transfers between devices  287 us (13%)
  local copies, waits for them, and re-layouts  200 us (9%)
  other arithmetic  83.5 us (4%)
  matrix products  56.2 us (3%)
  loops' own time  45.7 us (2%)
    reduce_scatter x1, waiting for transfers between devices, on_device(): lax.psum_scatter(flat_grads, 'dp', scatter_dimension=0, tiled=True)  542 us
    ppermute x10, waiting for transfers between devices, shifted(): return lax.ppermute(x, axis, pairs)  489 us
    ppermute x10, starting transfers between devices, shifted(): return lax.ppermute(x, axis, pairs)  286 us
    all_gather x1, waiting for transfers between devices, on_device(): weights = lax.all_gather(packed, 'dp', axis=0, tiled=True)  229 us
    reduce_scatter x1, waiting for transfers between devices, on_device(): lax.psum_scatter(small_grads, 'dp', scatter_dimension=1, tiled=True)  118 us
    psum x1, waiting for transfers between devices, on_device(): lax.psum(gradient_terms[3].astype(jnp.bfloat16), 'section')  75 us
    cond x4, local copies, waits for them, and re-layouts, on_device(): outputs = lax.switch(section_id, branches)  72 us
    another operation x8, local copies, waits for them, and re-layouts  50.5 us
  transfers between devices with their start and end apart: 17, of which 12 were waited for; matrix products, arithmetic and copies ran while one was open for 5% of the time, Pallas kernels for 0%

commit v1 on v0

v1 whole, which is shorter than its diff:
```python
from functools import partial

import jax
import jax.numpy as jnp
from jax import lax
from jax.sharding import PartitionSpec as P

D = 1024
HEADS = 16
HEAD = 64
FF = 4096
VARS = 48
PIX = 4
LEN = 128


highest = lax.Precision.HIGHEST
blocked = -1000000000.0
epsilon = 1e-05


def project(row_block, matrix):
    return jnp.dot(row_block, matrix, preferred_element_type=jnp.float32)


def project_back(row_block, matrix):
    return jnp.einsum("ta,ba->tb", row_block, matrix, preferred_element_type=jnp.float32)


def outer_sum(left_rows, right_rows):
    return jnp.einsum("ta,tb->ab", left_rows, right_rows, preferred_element_type=jnp.float32)


def layer_norm(row_block, norm_gain, shift_vec):
    averaged = jnp.mean(row_block, axis=-1, keepdims=True)
    centred = row_block - averaged
    variance = jnp.mean(centred * centred, axis=-1, keepdims=True)
    return centred * lax.rsqrt(variance + epsilon) * norm_gain + shift_vec


def on_device(
    patches,
    var_ids,
    segment_ids,
    embed_weight,
    var_embed,
    agg_query,
    agg_wq,
    agg_bq,
    agg_wk,
    agg_wv,
    agg_bv,
    agg_wo,
    agg_bo,
    attn_norm_gain,
    attn_norm_bias,
    attn_wqkv,
    attn_bq,
    attn_bv,
    attn_wo,
    attn_bo,
    mlp_norm_gain,
    mlp_norm_bias,
    mlp_up,
    mlp_bup,
    mlp_down,
    mlp_bdown,
    cotangent,
):
    s = lax.axis_index("section")
    r = lax.axis_index("dp")
    ns = lax.axis_size("section")
    nd = lax.axis_size("dp")
    rows = agg_wv.shape[0]
    tokens = patches.shape[0]
    seqs = tokens // LEN
    hl = HEADS // ns
    wl = D // ns
    fl = FF // ns
    cp = VARS * PIX

    def mine(array, axis, index, size):
        return lax.dynamic_slice_in_dim(array, index * size, size, axis)

    qkv_cols = mine(attn_wqkv.reshape(rows, 3, D), 2, s, wl).reshape(rows, 3 * wl)
    first = jnp.concatenate([mine(agg_wo, 1, s, wl), mine(attn_wo, 1, s, wl), qkv_cols], axis=1)
    second = jnp.concatenate([mine(mlp_up, 1, s, fl), mine(mlp_down, 1, s, fl)], axis=1)
    first = lax.all_gather(first, "dp", axis=0, tiled=True)
    second = lax.all_gather(second, "dp", axis=0, tiled=True)
    g_all = lax.all_gather(cotangent, "section", axis=1, tiled=True)
    out_ws = lax.all_to_all(first[:, : 2 * wl].reshape(ns, wl, 2 * wl), "section", 0, 0, tiled=True)
    agg_wo_rows = out_ws[:, :, :wl].transpose(1, 0, 2).reshape(wl, D)
    attn_wo_rows = out_ws[:, :, wl:].transpose(1, 0, 2).reshape(wl, D)
    qkv_w = first[:, 2 * wl :]
    up_w, down_w = second[:, :fl], second[:, fl:]

    var_row = var_ids[:, None] == jnp.arange(VARS, dtype=jnp.int32)[None, :]
    place = jnp.kron(var_row.astype(jnp.bfloat16), jnp.eye(PIX, dtype=jnp.bfloat16))
    spread = jnp.kron(jnp.eye(VARS, dtype=jnp.bfloat16), jnp.ones((1, PIX), jnp.bfloat16))
    pixels = project(patches, place).astype(jnp.bfloat16)

    basis = jnp.concatenate(
        [embed_weight.astype(jnp.float32), mine(var_embed, 1, r, rows).T], axis=1
    )
    wq_part = jnp.dot(
        mine(agg_query, 0, r, rows).astype(jnp.bfloat16)[None],
        agg_wq,
        preferred_element_type=jnp.float32,
    )
    wk_s, wv_s = mine(agg_wk, 1, s, wl), mine(agg_wv, 1, s, wl)
    kv = jnp.concatenate([wk_s, wv_s], axis=1).astype(jnp.float32)
    bkv = jnp.einsum("dc,dn->cn", basis, kv, precision=highest)
    bkv, query_proj = lax.psum((bkv, wq_part), "dp")
    query_proj = query_proj[0] + agg_bq
    query_s = mine(query_proj, 0, s, wl)
    score_scale = HEAD ** (-0.5)
    score_basis = (bkv[:, :wl] * query_s).reshape(-1, hl, HEAD).sum(-1) * score_scale
    value_basis = bkv[:, wl:].astype(jnp.bfloat16)
    key_query = (wk_s.astype(jnp.float32) * query_s).reshape(rows, hl, HEAD).sum(-1) * score_scale

    head_basis = score_basis[:cp, None, :] * spread.T.astype(jnp.float32)[:, :, None]
    head_basis = jnp.concatenate([head_basis, score_basis[cp:, None, :] * jnp.eye(VARS)[:, :, None]], 0)
    head_basis = head_basis.transpose(0, 2, 1).reshape(-1, hl * VARS)
    base = head_basis[cp:].sum(0)
    scores = jnp.dot(pixels.astype(jnp.float32), head_basis[:cp], precision=highest) + base
    probs = jax.nn.softmax(scores.reshape(tokens, hl, VARS), axis=-1)
    probs_low = probs.astype(jnp.bfloat16)
    wrep = jnp.einsum("thc,cq->thq", probs_low, spread, preferred_element_type=jnp.float32)
    mixed = jnp.concatenate(
        [(wrep * pixels[:, None, :].astype(jnp.float32)).astype(jnp.bfloat16), probs_low], axis=-1
    )
    value_heads = value_basis.reshape(-1, hl, HEAD)
    context = jnp.einsum("thq,qhj->thj", mixed, value_heads, preferred_element_type=jnp.float32)
    context = (context.reshape(tokens, wl) + mine(agg_bv, 0, s, wl)).astype(jnp.bfloat16)

    def section_sum(part):
        return lax.psum(part, "section")

    aggregated = section_sum(project(context, agg_wo_rows))
    aggregated = (aggregated + agg_bo).astype(jnp.bfloat16)
    context_all = lax.all_gather(context, "section", axis=1, tiled=True)

    agg_float = aggregated.astype(jnp.float32)
    normed_float, norm_pull = jax.vjp(layer_norm, agg_float, attn_norm_gain, attn_norm_bias)
    normed = normed_float.astype(jnp.bfloat16)
    projected = project(normed, qkv_w)
    shaped = (seqs, LEN, hl, HEAD)
    queries = (projected[:, :wl] + mine(attn_bq, 0, s, wl)).astype(jnp.bfloat16).reshape(shaped)
    keys = projected[:, wl : 2 * wl].astype(jnp.bfloat16).reshape(shaped)
    values = (projected[:, 2 * wl :] + mine(attn_bv, 0, s, wl)).astype(jnp.bfloat16).reshape(shaped)
    f32 = dict(preferred_element_type=jnp.float32)
    att = jnp.einsum("bthj,buhj->bhtu", queries, keys, **f32) * score_scale
    same = segment_ids[:, :, None] == segment_ids[:, None, :]
    att = jnp.where(same[:, None], att, blocked)
    att = jax.nn.softmax(att, axis=-1)
    att_low = att.astype(jnp.bfloat16)
    attended = jnp.einsum("bhtu,buhj->bthj", att_low, values, **f32).reshape(tokens, wl)
    attended = attended.astype(jnp.bfloat16)
    mid = section_sum(project(attended, attn_wo_rows))
    mid = (agg_float + mid + attn_bo).astype(jnp.bfloat16)
    attended_all = lax.all_gather(attended, "section", axis=1, tiled=True)

    mid_float = mid.astype(jnp.float32)
    mnormed_float, mnorm_pull = jax.vjp(layer_norm, mid_float, mlp_norm_gain, mlp_norm_bias)
    mnormed = mnormed_float.astype(jnp.bfloat16)
    hidden = project(mnormed, up_w) + mine(mlp_bup, 0, s, fl)
    act_float, gelu_pull = jax.vjp(partial(jax.nn.gelu, approximate=False), hidden)
    act = act_float.astype(jnp.bfloat16)
    out_part = project_back(act, down_w)
    out_cols = lax.psum_scatter(out_part, "section", scatter_dimension=1, tiled=True)
    activations = mine(mid_float, 1, s, wl) + out_cols + mine(mlp_bdown, 0, s, wl)
    activations = activations.astype(jnp.bfloat16)

    g_float = g_all.astype(jnp.float32)
    grad_down = outer_sum(g_all, act)
    grad_bdown = jnp.sum(g_float, axis=0)
    d_hidden = gelu_pull(project(g_all, down_w))[0].astype(jnp.bfloat16)
    grad_bup = jnp.sum(d_hidden.astype(jnp.float32), axis=0)
    grad_up = outer_sum(mnormed, d_hidden)
    grad_mlp = lax.psum_scatter(
        jnp.concatenate([grad_up, grad_down], axis=1), "dp", scatter_dimension=0, tiled=True
    )
    d_mnormed = section_sum(project_back(d_hidden, up_w))
    d_mid, grad_mgain, grad_mbias = mnorm_pull(d_mnormed)
    d_mid = (g_float + d_mid).astype(jnp.bfloat16)

    grad_attn_wo = outer_sum(attended_all, mine(d_mid, 1, s, wl))
    grad_attn_bo = jnp.sum(d_mid.astype(jnp.float32), axis=0)
    d_att = project_back(d_mid, attn_wo_rows).astype(jnp.bfloat16).reshape(shaped)
    d_values = jnp.einsum("bhtu,bthj->buhj", att_low, d_att, **f32).astype(jnp.bfloat16)
    d_probs = jnp.einsum("bthj,buhj->bhtu", d_att, values, **f32)
    d_scores = att * (d_probs - jnp.sum(att * d_probs, axis=-1, keepdims=True))
    d_scores = d_scores.astype(jnp.bfloat16)
    d_queries = jnp.einsum("bhtu,buhj->bthj", d_scores, keys, **f32) * score_scale
    d_keys = jnp.einsum("bhtu,bthj->buhj", d_scores, queries, **f32) * score_scale
    d_queries = d_queries.astype(jnp.bfloat16).reshape(tokens, wl)
    d_keys = d_keys.astype(jnp.bfloat16).reshape(tokens, wl)
    d_values = d_values.reshape(tokens, wl)
    grad_bq = jnp.sum(d_queries.astype(jnp.float32), axis=0)
    grad_bv = jnp.sum(d_values.astype(jnp.float32), axis=0)
    d_qkv = jnp.concatenate([d_queries, d_keys, d_values], axis=1)
    grad_qkv = outer_sum(normed, d_qkv)
    d_normed = section_sum(project_back(d_qkv, qkv_w))
    d_agg, grad_again, grad_abias = norm_pull(d_normed)
    d_agg = (d_mid.astype(jnp.float32) + d_agg).astype(jnp.bfloat16)

    grad_agg_wo = outer_sum(context_all, mine(d_agg, 1, s, wl))
    grad_agg_bo = jnp.sum(d_agg.astype(jnp.float32), axis=0)
    d_context = project_back(d_agg, agg_wo_rows).astype(jnp.bfloat16)
    grad_agg_bv = jnp.sum(d_context.astype(jnp.float32), axis=0)
    d_ctx_heads = d_context.reshape(tokens, hl, HEAD)
    cross = jnp.einsum("thj,thq->hjq", d_ctx_heads, mixed, **f32).reshape(wl, -1)
    pulled = jnp.einsum("thj,qhj->thq", d_ctx_heads, value_heads, **f32)
    d_weights = jnp.einsum(
        "thq,cq->thc",
        pulled[:, :, :cp] * pixels[:, None, :].astype(jnp.float32),
        spread.astype(jnp.float32),
        precision=highest,
    ) + pulled[:, :, cp:]
    d_sc = probs * (d_weights - jnp.sum(probs * d_weights, axis=-1, keepdims=True))
    d_sc = d_sc.astype(jnp.bfloat16)
    srep = jnp.einsum("thc,cq->thq", d_sc, spread, **f32)
    key_terms = jnp.concatenate(
        [
            jnp.sum(srep * pixels[:, None, :].astype(jnp.float32), axis=0),
            jnp.sum(d_sc.astype(jnp.float32), axis=0),
        ],
        axis=-1,
    )
    grad_pix = jnp.sum(wrep * pulled[:, :, :cp] + srep * score_basis[:cp].T[None], axis=1)
    grad_pix = section_sum(grad_pix).astype(jnp.bfloat16)
    patches_grad = mine(project_back(grad_pix, place).astype(jnp.bfloat16), 1, s, cp // ns)

    grad_attn = lax.psum_scatter(
        jnp.concatenate([grad_agg_wo, grad_attn_wo, grad_qkv], axis=1),
        "dp",
        scatter_dimension=0,
        tiled=True,
    )
    full_small = jnp.stack([grad_bdown, grad_mgain, grad_mbias, grad_attn_bo, grad_again, grad_abias, grad_agg_bo])
    part_small = jnp.concatenate([grad_bup, grad_bq, grad_bv, grad_agg_bv])
    cross, key_terms, full_small, part_small = lax.psum((cross, key_terms, full_small, part_small), "dp")

    grad_wv = jnp.dot(basis, cross.T, precision=highest)
    grad_basis = jnp.dot(wv_s.astype(jnp.float32), cross, precision=highest) + jnp.dot(
        key_query, key_terms, precision=highest
    )
    d_key_query = jnp.einsum("dq,hq->dh", basis, key_terms, precision=highest)
    grad_wk = (d_key_query[:, :, None] * query_s.reshape(hl, HEAD)[None]).reshape(rows, wl) * score_scale
    d_query = jnp.einsum("qhj,hq->hj", bkv[:, :wl].reshape(-1, hl, HEAD), key_terms, precision=highest)
    d_query = d_query.reshape(wl) * score_scale
    grad_basis = section_sum(grad_basis)
    d_query = lax.all_gather(d_query, "section", axis=0, tiled=True)
    part_small = lax.all_gather(part_small, "section", axis=0)
    grad_wq = mine(agg_query, 0, r, rows).astype(jnp.bfloat16).astype(jnp.float32)[:, None] * d_query
    grad_query = jnp.dot(agg_wq.astype(jnp.float32), d_query, precision=highest)
    joined = jnp.concatenate([grad_attn, grad_wv, grad_wk, grad_mlp], axis=1).astype(jnp.bfloat16)
    joined = lax.all_gather(joined, "section", axis=0)

    def columns(start, width):
        part = joined[:, :, start : start + width].astype(jnp.float32)
        return part.transpose(1, 0, 2).reshape(rows, ns * width)

    grad_qkv = joined[:, :, 2 * wl : 5 * wl].astype(jnp.float32).reshape(ns, rows, 3, wl)
    grad_qkv = grad_qkv.transpose(1, 2, 0, 3).reshape(rows, 3 * D)
    small = mine(full_small, 1, r, rows)
    bup = mine(part_small[:, :fl].reshape(-1), 0, r, FF // nd)
    bq = mine(part_small[:, fl : fl + wl].reshape(-1), 0, r, rows)
    bv = mine(part_small[:, fl + wl : fl + 2 * wl].reshape(-1), 0, r, rows)
    abv = mine(part_small[:, fl + 2 * wl :].reshape(-1), 0, r, rows)
    return (
        activations,
        patches_grad,
        grad_basis[:, :cp],
        grad_basis[:, cp:].T,
        grad_query,
        grad_wq,
        mine(d_query, 0, r, rows),
        columns(6 * wl, wl),
        columns(5 * wl, wl),
        abv,
        columns(0, wl),
        small[6],
        small[4],
        small[5],
        grad_qkv,
        bq,
        bv,
        columns(wl, wl),
        small[3],
        small[1],
        small[2],
        columns(7 * wl, fl),
        bup,
        columns(7 * wl + fl, fl),
        small[0],
    )


def solution(mesh):
    in_specs = (
        P("dp", None),
        P(),
        P("dp", None),
        P("dp", None),
        P(),
        P(),
        P("dp", None),
        P(),
        P("dp", None),
        P("dp", None),
        P(),
        P("dp", None),
        P(),
        P(),
        P(),
        P("dp", None),
        P(),
        P(),
        P("dp", None),
        P(),
        P(),
        P(),
        P("dp", None),
        P(),
        P("dp", None),
        P(),
        P("dp", "section"),
    )
    out_specs = (
        P("dp", "section"),
        P("dp", "section"),
        P("dp", None),
        P(None, "dp"),
        P("dp"),
        P("dp", None),
        P("dp"),
        P("dp", None),
        P("dp", None),
        P("dp"),
        P("dp", None),
        P("dp"),
        P("dp"),
        P("dp"),
        P("dp", None),
        P("dp"),
        P("dp"),
        P("dp", None),
        P("dp"),
        P("dp"),
        P("dp"),
        P("dp", None),
        P("dp"),
        P("dp", None),
        P("dp"),
    )
    return jax.shard_map(
        on_device, mesh=mesh, in_specs=in_specs, out_specs=out_specs, check_vma=False
    )
```

time: 2230 us -> 894 us (0.40)
  waiting for transfers between devices: 1510 us -> 616 us
  starting transfers between devices: 287 us -> 4.41 us
  local copies, waits for them, and re-layouts: 200 us -> 54.8 us
  blocking collectives: 15 us -> 111 us
  loops' own time: 45.7 us -> 0 us
  other arithmetic: 83.5 us -> 42.9 us
    ppermute x10 -> x0, waiting for transfers between devices: 489 us -> none  [shifted(): return lax.ppermute(x, axis, pairs)]
    reduce_scatter x4 -> x3, waiting for transfers between devices: 697 us -> 274 us  [the longest x1 152 us: on_device(): lax.psum_scatter(jnp.concatenate([grad_up, grad_down], axis=1), 'dp', sca...]
    ppermute x10 -> x0, starting transfers between devices: 286 us -> none  [shifted(): return lax.ppermute(x, axis, pairs)]
    cond x8 -> x0, local copies, waits for them, and re-layouts: 79.3 us -> none  [the longest x4 72 us: on_device(): outputs = lax.switch(section_id, branches)]
    psum x0 -> x3, blocking collectives: none -> 74.8 us  [the longest x1 37.7 us: on_device(): lax.psum((cross, key_terms, full_small, part_small), 'dp')]
    psum x2 -> x7, waiting for transfers between devices: 96.6 us -> 168 us  [the longest x5 106 us: section_sum(): return lax.psum(part, 'section')]
    all_gather x1 -> x3, waiting for transfers between devices: 229 us -> 163 us  [the longest x1 73.7 us: on_device(): second = lax.all_gather(second, 'dp', axis=0, tiled=True)]
    another operation x8 -> x1, local copies, waits for them, and re-layouts: 50.5 us -> 0.06 us  [on_device(): jnp.stack([grad_bdown, grad_mgain, grad_mbias, grad_attn_bo, grad_again,...]
  transfers between devices with their start and end apart: 17 -> 14, of which waited for: 12 -> 13; matrix products, arithmetic and copies ran while one was open for 5% -> 7% of each run, Pallas kernels for 0% -> 0%
where the time goes in v1:
time: 894 us; the launch traced here: 892 us
  waiting for transfers between devices  616 us (69%)
  blocking collectives  111 us (12%)
  local copies, waits for them, and re-layouts  54.8 us (6%)
  matrix products  48 us (5%)
  other arithmetic  42.9 us (5%)
  between operations  15.3 us (2%)
    reduce_scatter x1, waiting for transfers between devices, on_device(): lax.psum_scatter(jnp.concatenate([grad_up, grad_down], axis=1), 'dp', sca...  152 us
    psum x5, waiting for transfers between devices, section_sum(): return lax.psum(part, 'section')  106 us
    reduce_scatter x1, waiting for transfers between devices, on_device(): lax.psum_scatter(jnp.concatenate([grad_agg_wo, grad_attn_wo, grad_qkv], a...  99.1 us
    all_gather x1, waiting for transfers between devices, on_device(): second = lax.all_gather(second, 'dp', axis=0, tiled=True)  73.7 us
    all_gather x1, waiting for transfers between devices, on_device(): first = lax.all_gather(first, 'dp', axis=0, tiled=True)  55.6 us
    psum x1, waiting for transfers between devices, on_device(): bkv, query_proj = lax.psum((bkv, wq_part), 'dp')  44.1 us
    psum x1, blocking collectives, on_device(): lax.psum((cross, key_terms, full_small, part_small), 'dp')  37.7 us
    all_gather x1, waiting for transfers between devices, on_device(): joined = lax.all_gather(joined, 'section', axis=0)  33.5 us
  transfers between devices with their start and end apart: 14, of which 13 were waited for; matrix products, arithmetic and copies ran while one was open for 7% of the time, Pallas kernels for 0%

profile of v1, /device:TPU:0, one launch (start us, length us, event | category | flops | bytes accessed | tf_op | source)
XLA Modules:
  0.0 892.3 jit_solution(15343131513595622247)
XLA Ops:
  16.5 23.2 %psum.85 = f32[1024]{0:T(1024)S(1)} all-reduce(f32[1024]{0:T(1024)S(1)} %bitcast.294), channel_id=1, replica_groups=mesh['section'=4,'dp'=8] {'dp'}, use_global_device_ids=true, to_apply=%region_1.2 | all-reduce | flops 1024 | bytes 8192 | tf_op jit(solution)/shard_map/psum | solution.py:113
  43.0 44.1 %all-reduce.10.cloned.1.call-done = f32[240,512]{1,0:T(8,128)} async-done(((f32[240,512]{1,0:T(8,128)}), f32[240,512]{1,0:T(8,128)}) %all-reduce.10.cloned.1.call-update) | async-done | bytes 491536 | tf_op jit(solution)/shard_map/psum | solution.py:113
  90.3 55.6 %all-gather.6.cloned.1.call-done = bf16[1024,1280]{0,1:T(8,128)(2,1)} async-done(((bf16[128,1280]{0,1:T(8,128)(2,1)}), bf16[1024,1280]{0,1:T(8,128)(2,1)}) %all-gather.6.cloned.1.call-update) | async-done | bytes 2621456 | tf_op jit(solution)/shard_map/all_gather | solution.py:88
  155.2 11.1 %all-to-all-done = bf16[4,256,512]{1,2,0:T(8,128)(2,1)S(1)} async-done(((bf16[4,256,512]{1,2,0:T(8,128)(2,1)}), bf16[4,256,512]{1,2,0:T(8,128)(2,1)S(1)}, u32[]{:S(2)}, u32[]{:S(2)}) %all-to-all-start) | async-done | bytes 1048608 | tf_op jit(solution)/shard_map/all_to_all | solution.py:91
  171.1 30.1 %all-reduce.12.cloned.1.call-done = f32[256,1024]{1,0:T(8,128)} async-done(((f32[256,1024]{1,0:T(8,128)}), f32[256,1024]{1,0:T(8,128)}) %all-reduce.12.cloned.1.call-update) | async-done | bytes 1048592 | tf_op jit(solution)/shard_map/psum | solution.py:137
  215.7 6.8 all_gather.30
  222.5 28.1 %all-reduce.14.cloned.1.call-done = f32[256,1024]{1,0:T(8,128)} async-done(((f32[256,1024]{1,0:T(8,128)}), f32[256,1024]{1,0:T(8,128)}) %all-reduce.14.cloned.1.call-update) | async-done | bytes 1048592 | tf_op jit(solution)/shard_map/psum | solution.py:137
  253.5 73.7 %all-gather.8.cloned.1.call-done = bf16[1024,2048]{1,0:T(8,128)(2,1)} async-done(((bf16[128,2048]{1,0:T(8,128)(2,1)}), bf16[1024,2048]{1,0:T(8,128)(2,1)}) %all-gather.8.cloned.1.call-update) | async-done | bytes 4194320 | tf_op jit(solution)/shard_map/all_gather | solution.py:89
  327.2 5.5 multiply_convert_fusion
  337.7 9.8 %all_gather.32 = bf16[256,1024]{0,1:T(8,128)(2,1)} all-gather(bf16[256,256]{0,1:T(8,128)(2,1)S(1)} %fusion.59), channel_id=1, replica_groups=mesh['section'=4,'dp'=8] {'section'}, dimensions={1}, use_global_device_ids=true | all-gather | bytes 655360 | tf_op jit(solution)/shard_map/all_gather | solution.py:141
  347.5 9.1 %all_gather.33 = bf16[256,1024]{0,1:T(8,128)(2,1)} all-gather(bf16[256,256]{0,1:T(8,128)(2,1)S(1)} %bitcast.277), channel_id=1, replica_groups=mesh['section'=4,'dp'=8] {'section'}, dimensions={1}, use_global_device_ids=true | all-gather | bytes 655360 | tf_op jit(solution)/shard_map/all_gather | solution.py:161
  356.5 17.3 %all-reduce.16.cloned.1.call-done = f32[256,1024]{1,0:T(8,128)} async-done(((f32[256,1024]{1,0:T(8,128)}), f32[256,1024]{1,0:T(8,128)}) %all-reduce.16.cloned.1.call-update) | async-done | bytes 1048592 | tf_op jit(solution)/shard_map/psum | solution.py:137
  401.1 30.6 %all-reduce.18.cloned.1.call-done = f32[256,1024]{1,0:T(8,128)} async-done(((f32[256,1024]{1,0:T(8,128)}), f32[256,1024]{1,0:T(8,128)}) %all-reduce.18.cloned.1.call-update) | async-done | bytes 1048592 | tf_op jit(solution)/shard_map/psum | solution.py:137
  441.3 5.4 pad_maximum_fusion.1
  449.7 4.1 pad_maximum_fusion
  456.6 37.7 %all-reduce = (f32[4,240]{1,0:T(4,128)S(1)}, f32[1,1792]{1,0:T(1,128)S(1)}, f32[7,1024]{1,0:T(8,128)S(1)}) all-reduce(f32[4,240]{1,0:T(4,128)S(1)} %pad_maximum_fusion.13, f32[1,1792]{1,0:T(1,128)S(1)} %all_gather.35, f32[7,1024]{1,0:T(8,128)S(1)} %stack.19), channel_id=1, replica_groups=mesh['section'=4,'dp'=8] {'dp'}, use_global_device_ids=true, to_apply=%region_29.30 | all-reduce | flops 9920 | bytes 79360 | tf_op jit(solution)/shard_map/psum | solution.py:242
  494.3 18.0 %all-reduce.20.cloned.1.call-done = f32[256,240]{1,0:T(8,128)} async-done(((f32[256,240]{1,0:T(8,128)}), f32[256,240]{1,0:T(8,128)}) %all-reduce.20.cloned.1.call-update) | async-done | bytes 245776 | tf_op jit(solution)/shard_map/psum | solution.py:242
  519.1 99.1 %reduce-scatter.6.cloned.1.call-done = f32[128,1280]{0,1:T(8,128)} async-done(((f32[1024,1280]{0,1:T(8,128)}), f32[128,1280]{0,1:T(8,128)}) %reduce-scatter.6.cloned.1.call-update) | async-done | bytes 655376 | tf_op jit(solution)/shard_map/reduce_scatter | solution.py:234
  619.3 151.5 %reduce-scatter.8.cloned.1.call-done = f32[128,2048]{0,1:T(8,128)} async-done(((f32[1024,2048]{0,1:T(8,128)}), f32[128,2048]{0,1:T(8,128)}) %reduce-scatter.8.cloned.1.call-update) | async-done | bytes 1048592 | tf_op jit(solution)/shard_map/reduce_scatter | solution.py:180
  775.6 5.1 all-gather
  781.3 5.2 all-gather.1
  788.9 14.0 %all-reduce.23 = bf16[256,192]{0,1:T(8,128)(2,1)S(1)} all-reduce(f32[256,192]{0,1:T(8,128)S(1)} %get-tuple-element.134), channel_id=1, replica_groups=mesh['section'=4,'dp'=8] {'section'}, use_global_device_ids=true, to_apply=%region_24.25 | all-reduce | flops 49152 | bytes 294912 | tf_op jit(solution)/shard_map/psum | solution.py:137
  808.8 23.2 %reduce-scatter.4.cloned.1.call-done = f32[256,256]{1,0:T(8,128)} async-done(((f32[256,1024]{1,0:T(8,128)}), f32[256,256]{1,0:T(8,128)}) %reduce-scatter.4.cloned.1.call-update) | async-done | bytes 262160 | tf_op jit(solution)/shard_map/reduce_scatter | solution.py:170
  833.7 33.5 %all-gather.10.cloned.1.call-done = bf16[4,128,3840]{2,1,0:T(8,128)(2,1)} async-done(((bf16[1,128,3840]{2,1,0:T(8,128)(2,1)}), bf16[4,128,3840]{2,1,0:T(8,128)(2,1)}) %all-gather.10.cloned.1.call-update) | async-done | bytes 3932176 | tf_op jit(solution)/shard_map/all_gather | solution.py:258
  (386 shorter events, 135.3 us)
Async XLA Ops:
  7.2 79.9 %all-reduce.10.cloned.1.call-start = ((), (), s32[]{:S(2)}) async-start(), calls=%async_computation.4 | async-start | bytes 983040 | tf_op jit(solution)/shard_map/psum | solution.py:113
  11.2 134.7 %all-gather.6.cloned.1.call-start = ((), (), s32[]{:S(2)}) async-start(), calls=%async_computation.5 | async-start | bytes 2949120 | tf_op jit(solution)/shard_map/all_gather | solution.py:88
  39.8 47.3 %copy-start.56 = (f32[256]{0:T(256)}, f32[256]{0:T(256)S(1)}, u32[]{:S(2)}) copy-start(f32[256]{0:T(256)S(1)} %dynamic_slice.80) | copy-start | bytes 3076
  42.7 103.2 %copy-start.14 = (bf16[192,192]{1,0:T(8,128)(2,1)}, bf16[192,192]{1,0:T(8,128)(2,1)S(1)}, u32[]{:S(2)}) copy-start(bf16[192,192]{1,0:T(8,128)(2,1)S(1)} %mul.400) | copy-start | bytes 221188
  90.3 62.8 %copy-start.36 = (f32[256,4]{0,1:T(4,128)}, f32[256,4]{0,1:T(4,128)S(1)}, u32[]{:S(2)}) copy-start(f32[256,4]{0,1:T(4,128)S(1)} %reduce_max.18) | copy-start | bytes 12292
  148.2 18.1 %all-to-all-start = ((bf16[4,256,512]{1,2,0:T(8,128)(2,1)}), bf16[4,256,512]{1,2,0:T(8,128)(2,1)S(1)}, u32[]{:S(2)}, u32[]{:S(2)}) async-start(bf16[4,256,512]{1,2,0:T(8,128)(2,1)} %bitcast.242), calls=%async_computation | async-start | bytes 2097152 | tf_op jit(solution)/shard_map/all_to_all | solution.py:91
  151.8 49.4 %all-reduce.12.cloned.1.call-start = ((), (), s32[]{:S(2)}) async-start(), calls=%async_computation.6 | async-start | bytes 2097152 | tf_op jit(solution)/shard_map/psum | solution.py:137
  167.7 82.9 %all-reduce.14.cloned.1.call-start = ((), (), s32[]{:S(2)}) async-start(), calls=%async_computation.7 | async-start | bytes 2097152 | tf_op jit(solution)/shard_map/psum | solution.py:137
  213.6 113.6 %all-gather.8.cloned.1.call-start = ((), (), s32[]{:S(2)}) async-start(), calls=%async_computation.8 | async-start | bytes 4718592 | tf_op jit(solution)/shard_map/all_gather | solution.py:89
  215.6 111.6 %copy-start.34 = (f32[1024]{0:T(1024)S(1)}, f32[1024]{0:T(1024)}, u32[]{:S(2)}) copy-start(f32[1024]{0:T(1024)} %param.47) | copy-start | bytes 12292
  215.6 111.6 %copy-start.46 = (f32[1024]{0:T(1024)S(1)}, f32[1024]{0:T(1024)}, u32[]{:S(2)}) copy-start(f32[1024]{0:T(1024)} %param.48) | copy-start | bytes 12292
  215.6 111.6 %dynamic-slice-start = ((f32[4096]{0:T(1024)}, s32[]{:T(128)}), f32[1024]{0:T(1024)S(1)}, s32[]{:S(2)}) async-start(f32[4096]{0:T(1024)} %param.50, s32[]{:T(128)} %select_n.17), calls=%async_computation.18 | async-start | bytes 8704 | tf_op jit(solution)/shard_map/dynamic_slice | solution.py:83
  215.6 158.3 %all-reduce.16.cloned.1.call-start = ((), (), s32[]{:S(2)}) async-start(), calls=%async_computation.10 | async-start | bytes 2097152 | tf_op jit(solution)/shard_map/psum | solution.py:137
  253.2 79.5 %copy-start.48 = (f32[256]{0:T(256)}, f32[256]{0:T(256)S(1)}, u32[]{:S(2)}) copy-start(f32[256]{0:T(256)S(1)} %broadcast_multiply_fusion.7) | copy-start | bytes 3076
  253.5 79.2 %copy-start.68 = (f32[256]{0:T(256)}, f32[256]{0:T(256)S(1)}, u32[]{:S(2)}) copy-start(f32[256]{0:T(256)S(1)} %multiply_reduce_fusion.2) | copy-start | bytes 3076
  253.5 79.2 %copy-start.52 = (f32[256]{0:T(256)}, f32[256]{0:T(256)S(1)}, u32[]{:S(2)}) copy-start(f32[256]{0:T(256)S(1)} %fusion.91) | copy-start | bytes 3076
  336.9 94.9 %all-reduce.18.cloned.1.call-start = ((), (), s32[]{:S(2)}) async-start(), calls=%async_computation.11 | async-start | bytes 2097152 | tf_op jit(solution)/shard_map/psum | solution.py:137
  395.1 117.2 %all-reduce.20.cloned.1.call-start = ((), (), s32[]{:S(2)}) async-start(), calls=%async_computation.12 | async-start | bytes 524288 | tf_op jit(solution)/shard_map/psum | solution.py:242
  441.2 177.0 %reduce-scatter.6.cloned.1.call-start = ((), (), s32[]{:S(2)}) async-start(), calls=%async_computation.14 | async-start | bytes 5898240 | tf_op jit(solution)/shard_map/reduce_scatter | solution.py:234
  446.7 324.1 %reduce-scatter.8.cloned.1.call-start = ((), (), s32[]{:S(2)}) async-start(), calls=%async_computation.15 | async-start | bytes 9437184 | tf_op jit(solution)/shard_map/reduce_scatter | solution.py:180
  454.0 352.0 %all-reduce.22.cloned.1.call-start = ((), (), s32[]{:S(2)}) async-start(), calls=%async_computation.13 | async-start | bytes 245760 | tf_op jit(solution)/shard_map/psum | solution.py:137
  455.1 57.2 %copy-start.21 = (bf16[128,256]{1,0:T(8,128)(2,1)S(1)}, bf16[128,256]{1,0:T(8,128)(2,1)}, u32[]{:S(2)}) copy-start(bf16[128,256]{1,0:T(8,128)(2,1)} %copy-done.20) | copy-start | bytes 196612
  514.7 317.3 %reduce-scatter.4.cloned.1.call-start = ((), (), s32[]{:S(2)}) async-start(), calls=%async_computation.9 | async-start | bytes 1310720 | tf_op jit(solution)/shard_map/reduce_scatter | solution.py:170
  518.1 349.1 %all-gather.10.cloned.1.call-start = ((), (), s32[]{:S(2)}) async-start(), calls=%async_computation.16 | async-start | bytes 4915200 | tf_op jit(solution)/shard_map/all_gather | solution.py:258
  (75 other events, 459.2 us)
Sparse Core Ops, SparseCore 0:
  12.0 75.0 all-reduce.9
  89.9 55.9 all-gather.5
  167.9 33.2 all-reduce.11
  213.7 36.8 all-reduce.13
  253.4 73.7 all-gather.7
  337.0 36.8 all-reduce.15
  395.2 36.4 all-reduce.17
  441.3 70.9 all-reduce.19
  515.9 102.2 reduce-scatter.5
  621.7 149.1 reduce-scatter.7
  773.8 29.6 all-reduce.21
  806.5 25.4 reduce-scatter.3
  834.2 33.0 all-gather.9

commit v2 on v1

v2 whole, which is shorter than its diff:
```python
from functools import partial
from types import SimpleNamespace

import jax
import jax.numpy as jnp
from jax import lax
from jax.experimental import pallas as pl
from jax.experimental.pallas import tpu as pltpu
from jax.sharding import PartitionSpec as P

D = 1024
HEADS = 16
HEAD = 64
FF = 4096
VARS = 48
PIX = 4
LEN = 128

highest = lax.Precision.HIGHEST
blocked = -1000000000.0
epsilon = 1e-05
MESH = pl.DeviceIdType.MESH
BF = jnp.bfloat16
F32 = jnp.float32
CHUNK = 256
CP = VARS * PIX
LANES = 128


def nn(a, b):
    return jnp.dot(a, b, preferred_element_type=F32)


def nt(a, b):
    return lax.dot_general(a, b, (((1,), (1,)), ((), ())), preferred_element_type=F32)


def tn(a, b):
    return lax.dot_general(a, b, (((0,), (0,)), ((), ())), preferred_element_type=F32)


def split(x):
    high = x.astype(BF)
    return high, (x - high.astype(F32)).astype(BF)


def iota(shape, dim):
    return lax.broadcasted_iota(jnp.int32, shape, dim)


def colsum(x):
    return jnp.sum(x.astype(F32), axis=0, keepdims=True)


def each(low, high, body):
    if high - low <= 8:
        for k in range(low, high):
            body(k)
    else:

        def step(k, carry):
            body(k)
            return carry

        lax.fori_loop(low, high, step, 0)


class Transfer:
    def __init__(self, make, low, high):
        self.make, self.low, self.high = make, low, high

    def start(self):
        each(self.low, self.high, lambda k: self.make(k).start())
        return self

    def wait_recv(self):
        each(self.low, self.high, lambda k: self.make(k).wait_recv())

    def wait_send(self):
        each(self.low, self.high, lambda k: self.make(k).wait_send())


def kernel(ns, nd, refs_in, refs_out, sc):
    s = lax.axis_index("section")
    r = lax.axis_index("dp")
    nx = 2
    nz = nd // nx
    z, x = lax.div(r, nx), lax.rem(r, nx)
    i, o = refs_in, refs_out
    rows = D // nd
    tokens = i.patches.shape[0]
    shard = tokens // ns
    wl, fl, hl = D // ns, FF // ns, HEADS // ns
    zq = nz // ns
    own_cols = pl.ds(pl.multiple_of(s * wl, LANES), wl)
    own_ff = pl.ds(pl.multiple_of(s * fl, LANES), fl)
    own_rows = pl.ds(pl.multiple_of(s * shard, 16), shard)
    scale = HEAD ** (-0.5)
    send, recv = sc.send, sc.recv
    used = {"n": 0}
    pending = []

    def sems(count):
        base = used["n"]
        used["n"] += count
        return base

    def remote(src, dst, sem, device):
        return pltpu.make_async_remote_copy(
            src_ref=src,
            dst_ref=dst,
            send_sem=send.at[sem],
            recv_sem=recv.at[sem],
            device_id=device,
            device_id_type=MESH,
        )

    def over_section(src, dst):
        base = sems(ns)

        def make(k):
            t = lax.rem(s + k, ns)
            return remote(src(t), dst, base + k, (t, r))

        transfer = Transfer(make, 1, ns).start()
        pending.append(transfer)
        return transfer

    def over_dp(src, dst):
        base = sems(nd)

        def make(k):
            t = lax.rem(r + k, nd)
            return remote(src(t), dst, base + k, (s, t))

        transfer = Transfer(make, 1, nd).start()
        pending.append(transfer)
        return transfer

    def over_z(src, dst):
        base = sems(nz)

        def make(k):
            t = lax.rem(z + k, nz)
            return remote(src(t), dst, base + k, (s, t * nx + x))

        transfer = Transfer(make, 1, nz).start()
        pending.append(transfer)
        return transfer

    def over_x(src, dst):
        base = sems(1)
        transfer = Transfer(lambda k: remote(src, dst, base, (s, z * nx + 1 - x)), 0, 1).start()
        pending.append(transfer)
        return transfer

    local_used = {"n": 0}

    def local(src, dst):
        sem = local_used["n"]
        local_used["n"] += 1
        copy = pltpu.make_async_copy(src, dst, sc.local.at[sem])
        copy.start()
        return copy

    small_loads = [
        local(i.agg_wq.at[:, own_cols], sc.wq),
        local(i.agg_wk.at[:, own_cols], sc.wk),
        local(i.agg_wv.at[:, own_cols], sc.wv),
    ]
    qkv_loads = [
        local(
            i.attn_wqkv.at[:, pl.ds(pl.multiple_of(j * D + s * wl, LANES), wl)],
            sc.qkv_w.at[z, x, :, pl.ds(j * wl, wl)],
        )
        for j in range(3)
    ]
    up_load = local(i.mlp_up.at[:, own_ff], sc.up_w.at[z, x])
    down_load = local(i.mlp_down.at[:, own_ff], sc.down_w.at[z, x])
    cot_load = local(i.cotangent, sc.g_full.at[:, own_cols])

    barrier = pltpu.get_barrier_semaphore()
    for k in range(1, ns):
        pl.semaphore_signal(barrier, inc=1, device_id=(lax.rem(s + k, ns), r), device_id_type=MESH)
    each(
        1,
        nd,
        lambda k: pl.semaphore_signal(
            barrier, inc=1, device_id=(s, lax.rem(r + k, nd)), device_id_type=MESH
        ),
    )

    chan = (iota((CP, VARS), 0) >> 2 == iota((CP, VARS), 1)).astype(F32).astype(BF)
    ids = jnp.broadcast_to(i.var_ids[...].astype(F32), (CHUNK, VARS)).astype(BF)
    ids = nt(chan, ids)
    lane = iota((CP, CHUNK), 1)
    row = iota((CP, CHUNK), 0)
    hit = ((lane >> 2).astype(F32) == ids) & ((lane & 3) == (row & 3)) & (lane < CP)
    place = hit.astype(F32).astype(BF)
    sc.place[...] = place
    lane = iota((tokens, CHUNK), 1)
    ones = ((lane >= CP) & (lane < CP + VARS)).astype(F32)
    sc.pix[...] = (nn(i.patches[...], place) + ones).astype(BF)
    row = iota((CHUNK, LANES), 0)
    lane = iota((CHUNK, LANES), 1)
    owner = jnp.where(row < CP, row >> 2, row - CP)
    sc.fold[...] = ((owner == lane) & (lane < VARS)).astype(F32).astype(BF)
    chosen = (iota((rows, D), 1) == iota((rows, D), 0) + r * rows).astype(F32).astype(BF)
    lane = iota((CP, CHUNK), 1)
    row = iota((CP, CHUNK), 0)
    widen = (lane == row).astype(F32).astype(BF)
    lane = iota((VARS, CHUNK), 1)
    row = iota((VARS, CHUNK), 0)
    widen_var = (lane == row + CP).astype(F32).astype(BF)
    var_rows = nt(chosen, i.var_embed[...].astype(BF)).astype(BF)
    sc.basis[...] = (nn(i.embed_weight[...], widen) + nn(var_rows, widen_var)).astype(BF)
    query = jnp.broadcast_to(i.agg_query[...].astype(BF).astype(F32), (16, D))
    query = jnp.where(iota((16, D), 0) == 0, query, 0.0).astype(BF)
    query_rows = nt(query, chosen).astype(BF)
    sc.vecs[...] = jnp.zeros_like(sc.vecs)
    sc.bup[...] = jnp.zeros_like(sc.bup)

    for copy in small_loads:
        copy.wait()
    sc.q_src[...] = nn(query_rows, sc.wq[...])[0:8]
    value_part = tn(sc.basis[...], sc.wv[...])
    blk = CHUNK // nd
    for t in range(nd):
        sc.bv_src[t] = value_part[t * blk : (t + 1) * blk]
    cot_load.wait()

    pl.semaphore_wait(barrier, ns - 1 + nd - 1)

    def push(src, dst):
        transfer = over_dp(lambda t: src, dst.at[r])
        dst[r] = src[...]
        return transfer

    def summed(dst, count):
        total = dst[0]
        for k in range(1, count):
            total = total + dst[k]
        return total

    q_push = push(sc.q_src, sc.q_recv)
    bv_rs = over_dp(lambda t: sc.bv_src.at[t], sc.bv_recv.at[r])
    sc.bv_recv[r] = sc.bv_src[r]
    g_gather = over_section(lambda t: sc.g_full.at[:, own_cols], sc.g_full.at[:, own_cols])

    def rows_out(whole, dst):
        base = sems(zq)
        base_send = sems(nz)
        local_base = local_used["n"]
        local_used["n"] += zq

        def make(j, k):
            t = lax.rem(z + k, nz)
            return pltpu.make_async_remote_copy(
                src_ref=whole,
                dst_ref=dst.at[j, x],
                send_sem=send.at[base_send + k],
                recv_sem=recv.at[base + j],
                device_id=(s, t * nx + x),
                device_id_type=MESH,
            )

        def go(j):
            @pl.when(z == s * zq + j)
            def _():
                pltpu.make_async_copy(whole, dst.at[j, x], sc.local.at[local_base + j]).start()
                each(1, nz, lambda k: make(j, k).start())

        def arrive(j):
            @pl.when(z == s * zq + j)
            def _():
                pltpu.make_async_copy(whole, dst.at[j, x], sc.local.at[local_base + j]).wait()

            @pl.when(z != s * zq + j)
            def _():
                make(j, 1).wait_recv()

        def finish(j):
            @pl.when(z == s * zq + j)
            def _():
                each(1, nz, lambda k: make(j, k).wait_send())

        def start():
            each(0, zq, go)

        def forward():
            each(0, zq, arrive)
            return over_x(dst.at[:, x], dst.at[:, x])

        return start, forward, lambda: each(0, zq, finish)

    awo_start, awo_forward, awo_finish = rows_out(i.agg_wo, sc.awo)
    two_start, two_forward, two_finish = rows_out(i.attn_wo, sc.two)
    awo_start()
    for copy in qkv_loads:
        copy.wait()
    qkv_z = over_z(lambda t: sc.qkv_w.at[z, x], sc.qkv_w.at[z, x])
    two_start()

    q_push.wait_recv()
    query_proj = summed(sc.q_recv, nd)[0:1] + i.agg_bq[:, own_cols]
    sc.query_proj[...] = query_proj
    head_rows = (iota((16, wl), 1) >> 6 == iota((16, wl), 0)).astype(F32)
    high, low = split(head_rows * (query_proj * scale))
    key_query = (nt(high, sc.wk[...]) + nt(low, sc.wk[...])).astype(BF)
    sc.key_query[...] = key_query
    sc.s_src[...] = nn(key_query, sc.basis[...])[0:8]
    s_push = push(sc.s_src, sc.s_recv)
    bv_rs.wait_recv()
    sc.bv_own[...] = summed(sc.bv_recv, nd)
    bv_ag = push(sc.bv_own, sc.bv_all)
    up_load.wait()
    up_z = over_z(lambda t: sc.up_w.at[z, x], sc.up_w.at[z, x])

    s_push.wait_recv()
    score_rows = summed(sc.s_recv, nd)
    sc.score_rows[...] = score_rows
    fold = sc.fold[...]
    lane_ok = iota((tokens, LANES), 1) < VARS
    for h in range(hl):
        pix = sc.pix[...].astype(F32)
        high, low = split(pix * score_rows[h : h + 1])
        scores = nn(high, fold) + nn(low, fold)
        scores = jnp.where(lane_ok, scores, -1e30)
        scores = jnp.exp(scores - jnp.max(scores, axis=-1, keepdims=True))
        probs = scores / jnp.sum(scores, axis=-1, keepdims=True)
        sc.probs[h] = probs
        wrep = nt(probs.astype(BF), fold)
        sc.wrep[h] = wrep.astype(BF)
        sc.mixed[h] = (wrep * pix).astype(BF)
    awo_x = awo_forward()
    bv_ag.wait_recv()
    for t in range(nd):
        sc.bv[t * blk : (t + 1) * blk] = sc.bv_all[t]
    value_basis = sc.bv[...].astype(BF)
    head_of = iota((1, wl), 1) >> 6
    context = jnp.broadcast_to(i.agg_bv[:, own_cols], (tokens, wl))
    for h in range(hl):
        context = context + jnp.where(head_of == h, nn(sc.mixed[h], value_basis), 0.0)
    sc.context[...] = context.astype(BF)
    awo_x.wait_recv()

    def weight(ref):
        return ref[...].reshape(ref.shape[0] * ref.shape[1] * ref.shape[2], ref.shape[3])

    def scatter(part, landed, value):
        part[...] = value.astype(BF)
        transfer = over_section(lambda t: part.at[pl.ds(pl.multiple_of(t * shard, 16), shard)], landed.at[s])
        landed[s] = part[own_rows, :]
        return transfer

    def gather(full, value):
        full[own_rows, :] = value.astype(BF)
        return over_section(lambda t: full.at[own_rows], full.at[own_rows])

    def landed_sum(landed):
        total = landed[0].astype(F32)
        for k in range(1, ns):
            total = total + landed[k].astype(F32)
        return total

    def norm(value, gain, bias, kept, rstd_kept):
        centred = value - jnp.mean(value, axis=-1, keepdims=True)
        rstd = lax.rsqrt(jnp.mean(centred * centred, axis=-1, keepdims=True) + epsilon)
        hat = centred * rstd
        kept[...] = hat
        rstd_kept[...] = jnp.broadcast_to(rstd, rstd_kept.shape)
        return hat * gain[...] + bias[...]

    def norm_back(grad, gain, kept, rstd_kept, gain_row, bias_row):
        hat = kept[...]
        sc.vecs[gain_row : gain_row + 1, :] = colsum(grad * hat)
        sc.vecs[bias_row : bias_row + 1, :] = colsum(grad)
        inner = grad * gain[...]
        mean = jnp.mean(inner, axis=-1, keepdims=True)
        dot = jnp.mean(inner * hat, axis=-1, keepdims=True)
        return rstd_kept[:, 0:1] * (inner - mean - hat * dot)

    def transposed(full, dst):
        for j in range(D // CHUNK):
            turned = full[:, j * CHUNK : (j + 1) * CHUNK].astype(F32).T.astype(BF)
            n = dst.shape[0] // (D // CHUNK)
            dst[j * n : (j + 1) * n] = turned.reshape((n,) + dst.shape[1:])

    def head_block(value, dst):
        at = pl.ds(s * zq, zq)
        dst[at] = value.astype(F32).T.astype(BF).reshape((zq,) + dst.shape[1:])
        return over_section(lambda t: dst.at[at], dst.at[at])

    rs1 = scatter(sc.rs1_part, sc.rs1_recv, nn(sc.context[...], weight(sc.awo)))
    context_gather = head_block(sc.context[...], sc.contextT)
    g_gather.wait_recv()
    qkv_z.wait_recv()
    qkv_x = over_x(sc.qkv_w.at[:, x], sc.qkv_w.at[:, x])
    down_load.wait()
    down_z = over_z(lambda t: sc.down_w.at[z, x], sc.down_w.at[z, x])
    rs1.wait_recv()
    agg = (landed_sum(sc.rs1_recv) + i.agg_bo[...]).astype(BF).astype(F32)
    sc.agg[...] = agg
    ag1 = gather(sc.normed, norm(agg, i.attn_norm_gain, i.attn_norm_bias, sc.hat1, sc.rstd1))
    two_x = two_forward()
    transposed(sc.g_full, sc.gT)
    qkv_x.wait_recv()
    ag1.wait_recv()

    normed = sc.normed[...]
    qkv_w = weight(sc.qkv_w)
    for j in range(3):
        part = nn(normed, qkv_w[:, j * wl : (j + 1) * wl])
        if j == 0:
            part = part + i.attn_bq[:, own_cols]
        if j == 2:
            part = part + i.attn_bv[:, own_cols]
        sc.qkv[:, j * wl : (j + 1) * wl] = part.astype(BF)
    lo = (iota((1, LANES), 1) < HEAD).astype(F32)
    first, second = lo.astype(BF), (1.0 - lo).astype(BF)

    def pair(a):
        return jnp.concatenate([a * first, a * second], axis=0)

    def pick(a):
        return jnp.where(iota((LEN, LANES), 1) < HEAD, a[0:LEN], a[LEN:])

    tiles = [(b, p) for b in range(tokens // LEN) for p in range(wl // LANES)]

    def tile(ref, b, p, j=0):
        return ref[b * LEN : (b + 1) * LEN, j * wl + p * LANES : j * wl + (p + 1) * LANES]

    for n, (b, p) in enumerate(tiles):
        q, k, v = [tile(sc.qkv, b, p, j) for j in range(3)]
        ids = jnp.broadcast_to(i.segment_ids[b : b + 1, :].astype(F32), (LEN, LEN))
        same = ids == ids.T
        scores = nt(pair(q), k) * scale
        scores = jnp.where(jnp.concatenate([same, same], axis=0), scores, blocked)
        scores = jnp.exp(scores - jnp.max(scores, axis=-1, keepdims=True))
        probs = scores / jnp.sum(scores, axis=-1, keepdims=True)
        sc.att[n] = probs
        sc.attended[b * LEN : (b + 1) * LEN, p * LANES : (p + 1) * LANES] = pick(
            nn(probs.astype(BF), v)
        ).astype(BF)
    two_x.wait_recv()
    rs2 = scatter(sc.rs2_part, sc.rs2_recv, nn(sc.attended[...], weight(sc.two)))
    attended_gather = head_block(sc.attended[...], sc.attendedT)
    up_z.wait_recv()
    up_x = over_x(sc.up_w.at[:, x], sc.up_w.at[:, x])
    transposed(sc.normed, sc.normedT)
    rs2.wait_recv()
    mid = (sc.agg[...] + landed_sum(sc.rs2_recv) + i.attn_bo[...]).astype(BF).astype(F32)
    sc.mid[...] = mid
    ag2 = gather(sc.mnormed, norm(mid, i.mlp_norm_gain, i.mlp_norm_bias, sc.hat2, sc.rstd2))
    ag2.wait_recv()
    up_x.wait_recv()

    def columns(ref, j):
        return ref[:, :, :, j * CHUNK : (j + 1) * CHUNK].reshape(D, CHUNK)

    mnormed = sc.mnormed[...]
    for j in range(fl // CHUNK):
        at = slice(j * CHUNK, (j + 1) * CHUNK)
        bias = i.mlp_bup[:, pl.ds(pl.multiple_of(s * fl + j * CHUNK, LANES), CHUNK)]
        hidden = nn(mnormed, columns(sc.up_w, j)) + bias
        phi = 0.5 + 0.5 * lax.erf(hidden * 0.7071067811865476)
        density = jnp.exp(hidden * hidden * -0.5) * 0.3989422804014327
        sc.act[:, at] = (hidden * phi).astype(BF)
        sc.slope[:, at] = phi + hidden * density
    down_z.wait_recv()
    down_x = over_x(sc.down_w.at[:, x], sc.down_w.at[:, x])

    names = (
        [(o.mlp_down, s * fl + j * CHUNK) for j in range(fl // CHUNK)]
        + [(o.mlp_up, s * fl + j * CHUNK) for j in range(fl // CHUNK)]
        + [(o.attn_wo, s * wl)]
        + [(o.attn_wqkv, j * D + s * wl) for j in range(3)]
        + [(o.agg_wo, s * wl)]
    )
    to_x, to_z = {}, {}
    out_copies, out_sends = [], []

    def produce(c, left, right):
        def half(side):
            block = left[:, pl.ds(side, 1)].reshape(nz * rows, tokens)
            return nn(block, right).reshape(nz, rows, CHUNK)

        sc.x_send[c] = half(1 - x).astype(BF)
        to_x[c] = over_x(sc.x_send.at[c], sc.x_recv.at[c])
        sc.keep[c] = half(x)

    def middle(c):
        to_x[c].wait_recv()
        sc.z_send[c] = (sc.keep[c] + sc.x_recv[c].astype(F32)).astype(BF)
        to_z[c] = over_z(lambda t: sc.z_send.at[c, t], sc.z_recv.at[c, z])
        sc.z_recv[c, z] = sc.z_send[c, z]

    def publish(c, array, start):
        dst = array.at[:, pl.ds(pl.multiple_of(start, LANES), CHUNK)]
        out_sends.append(over_section(lambda t: sc.final.at[c], dst))
        out_copies.append(local(sc.final.at[c], dst))

    def finish(c):
        to_z[c].wait_recv()
        total = sc.z_recv[c, 0].astype(F32)
        for k in range(1, nz):
            total = total + sc.z_recv[c, k].astype(F32)
        sc.final[c] = total.astype(BF)
        publish(c, *names[c])

    for j in range(fl // CHUNK):
        produce(j, sc.gT, sc.act[:, j * CHUNK : (j + 1) * CHUNK])
    transposed(sc.mnormed, sc.mnormedT)
    down_x.wait_recv()
    g_full = sc.g_full[...]
    for j in range(fl // CHUNK):
        at = slice(j * CHUNK, (j + 1) * CHUNK)
        d_hidden = nn(g_full, columns(sc.down_w, j)) * sc.slope[:, at]
        sc.d_hidden[:, at] = d_hidden.astype(BF)
    up_w = weight(sc.up_w)
    rs3 = scatter(sc.rs3_part, sc.rs3_recv, nt(sc.d_hidden[...], up_w))
    nmlp = fl // CHUNK
    for j in range(nmlp):
        at = slice(j * CHUNK, (j + 1) * CHUNK)
        produce(nmlp + j, sc.mnormedT, sc.d_hidden[:, at])
    sc.bup[:, own_ff] = colsum(sc.d_hidden[...])
    rs3.wait_recv()
    g_shard = sc.g_full[own_rows, :].astype(F32)
    sc.vecs[0:1, :] = colsum(g_shard)
    d_mid = norm_back(landed_sum(sc.rs3_recv), i.mlp_norm_gain, sc.hat2, sc.rstd2, 1, 2)
    d_mid = (g_shard + d_mid).astype(BF)
    sc.vecs[3:4, :] = colsum(d_mid)
    ag3 = gather(sc.d_mid, d_mid)
    d_mid = d_mid.astype(F32)
    sc.out_part[...] = nt(sc.act[...], weight(sc.down_w))
    sc.out_part[own_rows, :] = sc.out_part[own_rows, :] + sc.mid[...] + i.mlp_bdown[...]
    sc.out_low[...] = sc.out_part[...].astype(BF)
    out_rs = over_section(
        lambda t: sc.out_low.at[:, pl.ds(pl.multiple_of(t * wl, LANES), wl)], sc.out_recv.at[s]
    )
    sc.out_recv[s] = sc.out_low[:, own_cols]
    for c in range(2):
        middle(c)
    ag3.wait_recv()

    d_att = nt(sc.d_mid[...], weight(sc.two)).astype(BF)
    sc.d_att[...] = d_att
    for n, (b, p) in enumerate(tiles):
        q, k, v = [tile(sc.qkv, b, p, j) for j in range(3)]
        q, d_out = pair(q), pair(tile(sc.d_att, b, p))
        probs = sc.att[n]
        d_probs = nt(d_out, v)
        d_scores = probs * (d_probs - jnp.sum(probs * d_probs, axis=-1, keepdims=True))
        d_scores = d_scores.astype(BF)
        parts = (pick(nn(d_scores, k)) * scale, tn(d_scores, q) * scale, tn(probs.astype(BF), d_out))
        for j in range(3):
            lanes = slice(j * wl + p * LANES, j * wl + (p + 1) * LANES)
            sc.d_qkv[b * LEN : (b + 1) * LEN, lanes] = parts[j].astype(BF)
    rs4 = scatter(sc.rs4_part, sc.rs4_recv, nt(sc.d_qkv[...], weight(sc.qkv_w)))
    attended_gather.wait_recv()
    produce(2 * nmlp, sc.attendedT, sc.d_mid[:, own_cols])
    for j in range(3):
        produce(2 * nmlp + 1 + j, sc.normedT, sc.d_qkv[:, j * wl : (j + 1) * wl])
    sc.vecs[7:8, own_cols] = colsum(sc.d_qkv[:, 0:wl])
    sc.vecs[8:9, own_cols] = colsum(sc.d_qkv[:, 2 * wl : 3 * wl])
    for c in range(2, 4):
        middle(c)
    rs4.wait_recv()
    d_agg = norm_back(landed_sum(sc.rs4_recv), i.attn_norm_gain, sc.hat1, sc.rstd1, 4, 5)
    d_agg = (sc.d_mid[own_rows, :].astype(F32) + d_agg).astype(BF)
    sc.vecs[6:7, :] = colsum(d_agg)
    ag4 = gather(sc.d_agg, d_agg)
    for c in range(4, 6):
        middle(c)
    finish(0)
    finish(1)
    ag4.wait_recv()

    context_gather.wait_recv()
    produce(2 * nmlp + 4, sc.contextT, sc.d_agg[:, own_cols])
    d_context = nt(sc.d_agg[...], weight(sc.awo)).astype(BF)
    sc.vecs[9:10, own_cols] = colsum(d_context)
    value_basis = sc.bv[...].astype(BF)
    cross = jnp.zeros((wl, CHUNK), F32)
    grad_pix = jnp.zeros((tokens, CHUNK), F32)
    sc.key_src[...] = jnp.zeros_like(sc.key_src)
    for h in range(hl):
        masked = d_context * (head_of == h).astype(F32).astype(BF)
        pulled = nt(masked, value_basis)
        cross = cross + tn(masked, sc.mixed[h])
        pix = sc.pix[...].astype(F32)
        high, low = split(pulled * pix)
        d_weights = nn(high, fold) + nn(low, fold)
        probs = sc.probs[h]
        d_scores = probs * (d_weights - jnp.sum(probs * d_weights, axis=-1, keepdims=True))
        srep = nt(d_scores.astype(BF), fold)
        sc.key_src[h : h + 1, :] = colsum(srep * pix)
        grad_pix = grad_pix + sc.wrep[h].astype(F32) * pulled
        grad_pix = grad_pix + srep * sc.score_rows[h : h + 1, :]
    key_push = push(sc.key_src, sc.key_recv)
    for t in range(nd):
        sc.m_src[t] = cross[t * blk : (t + 1) * blk]
    m_rs = over_dp(lambda t: sc.m_src.at[t], sc.m_recv.at[r])
    sc.m_recv[r] = sc.m_src[r]
    grad_pix = grad_pix.astype(BF)
    pw = CP // ns
    for t in range(ns):
        sc.pix_src[t, :, 0:pw] = nt(grad_pix, sc.place[t * pw : (t + 1) * pw, :]).astype(BF)
    pix_rs = over_section(lambda t: sc.pix_src.at[t], sc.pix_recv.at[s])
    sc.pix_recv[s] = sc.pix_src[s]
    for t in range(nd):
        sc.small_src[t, 0:10] = sc.vecs[0:10, t * rows : (t + 1) * rows]
        for j in range(FF // D):
            start = (t * (FF // D) + j) * rows
            sc.small_src[t, 10 + j : 11 + j] = sc.bup[:, start : start + rows]
    small_rs = over_dp(lambda t: sc.small_src.at[t], sc.small_recv.at[r])
    sc.small_recv[r] = sc.small_src[r]

    middle(6)
    m_rs.wait_recv()
    sc.m_own[...] = summed(sc.m_recv, nd)
    m_ag = push(sc.m_own, sc.m_all)
    middle(7)
    key_push.wait_recv()
    key_terms = summed(sc.key_recv, nd)
    wide = jnp.concatenate([jnp.broadcast_to(key_terms[h : h + 1], (HEAD, CHUNK)) for h in range(hl)], axis=0)
    d_key = nt(sc.basis[...], wide.astype(BF))
    d_query = jnp.sum(sc.wk[...].astype(F32) * d_key, axis=0, keepdims=True) * scale
    sc.dq_src[...] = jnp.broadcast_to(d_query, sc.dq_src.shape)
    dq_push = push(sc.dq_src, sc.dq_recv)
    count = len(names)
    sc.final[count] = (d_key * (sc.query_proj[...] * scale)).astype(BF)
    publish(count, o.agg_wk, s * wl)
    finish(2)
    small_rs.wait_recv()
    sc.sec_small[s] = summed(sc.small_recv, nd)
    small_ag = over_section(lambda t: sc.sec_small.at[s], sc.sec_small.at[s])
    middle(8)
    finish(3)
    m_ag.wait_recv()
    for t in range(nd):
        sc.cross[t * blk : (t + 1) * blk] = sc.m_all[t]
    cross = sc.cross[...].astype(BF)
    sc.final[count + 1] = nt(sc.basis[...], cross).astype(BF)
    publish(count + 1, o.agg_wv, s * wl)
    key_low = jnp.concatenate([key_terms, jnp.zeros_like(key_terms)], axis=0).astype(BF)
    grad_basis = nn(sc.wv[...], cross) + tn(sc.key_query[...], key_low)
    sc.basis_recv[s] = grad_basis.astype(BF)
    basis_sum = over_section(lambda t: sc.basis_recv.at[s], sc.basis_recv.at[s])
    dq_push.wait_recv()
    o.d_query[s] = summed(sc.dq_recv, nd)
    dq_gather = over_section(lambda t: o.d_query.at[s], o.d_query.at[s])
    middle(9)
    finish(4)
    middle(10)
    finish(5)
    middle(11)
    finish(6)
    middle(12)
    finish(7)
    small_ag.wait_recv()
    o.small[...] = summed(sc.sec_small, ns)
    pix_rs.wait_recv()
    total = sc.pix_recv[0].astype(F32)
    for k in range(1, ns):
        total = total + sc.pix_recv[k].astype(F32)
    o.patches[...] = total.astype(BF)
    out_rs.wait_recv()
    total = sc.out_recv[0].astype(F32)
    for k in range(1, ns):
        total = total + sc.out_recv[k].astype(F32)
    o.activations[...] = total.astype(BF)
    basis_sum.wait_recv()
    total = sc.basis_recv[0].astype(F32)
    for k in range(1, ns):
        total = total + sc.basis_recv[k].astype(F32)
    o.basis[...] = total
    for c in range(8, 13):
        finish(c)
    dq_gather.wait_recv()
    for transfer in out_sends:
        transfer.wait_recv()
    for copy in out_copies:
        copy.wait()
    awo_finish()
    two_finish()
    for transfer in pending:
        transfer.wait_send()
    assert used["n"] <= send.shape[0], used["n"]
    assert local_used["n"] <= sc.local.shape[0]


def scratch(ns, nd, tokens):
    nz, rows = nd // 2, D // nd
    wl, fl, hl = D // ns, FF // ns, HEADS // ns
    shard, zq, blk = tokens // ns, nz // ns, CHUNK // nd
    chunks = 2 * (fl // CHUNK) + 5
    v = pltpu.VMEM
    shapes = dict(
        wq=v((rows, wl), BF),
        wk=v((rows, wl), BF),
        wv=v((rows, wl), BF),
        qkv_w=v((nz, 2, rows, 3 * wl), BF),
        up_w=v((nz, 2, rows, fl), BF),
        down_w=v((nz, 2, rows, fl), BF),
        awo=v((zq, 2, rows, D), BF),
        two=v((zq, 2, rows, D), BF),
        g_full=v((tokens, D), BF),
        place=v((CP, CHUNK), BF),
        pix=v((tokens, CHUNK), BF),
        fold=v((CHUNK, LANES), BF),
        basis=v((rows, CHUNK), BF),
        vecs=v((16, D), F32),
        bup=v((1, FF), F32),
        query_proj=v((1, wl), F32),
        key_query=v((16, rows), BF),
        score_rows=v((8, CHUNK), F32),
        bv_own=v((blk, CHUNK), F32),
        m_own=v((blk, CHUNK), F32),
        bv=v((CHUNK, CHUNK), F32),
        cross=v((CHUNK, CHUNK), F32),
        probs=v((hl, tokens, LANES), F32),
        wrep=v((hl, tokens, CHUNK), BF),
        mixed=v((hl, tokens, CHUNK), BF),
        context=v((tokens, wl), BF),
        agg=v((shard, D), F32),
        mid=v((shard, D), F32),
        hat1=v((shard, D), F32),
        hat2=v((shard, D), F32),
        rstd1=v((shard, LANES), F32),
        rstd2=v((shard, LANES), F32),
        normed=v((tokens, D), BF),
        mnormed=v((tokens, D), BF),
        qkv=v((tokens, 3 * wl), BF),
        d_qkv=v((tokens, 3 * wl), BF),
        att=v((tokens // LEN * (wl // LANES), 2 * LEN, LEN), F32),
        attended=v((tokens, wl), BF),
        d_att=v((tokens, wl), BF),
        act=v((tokens, fl), BF),
        slope=v((tokens, fl), F32),
        d_hidden=v((tokens, fl), BF),
        d_mid=v((tokens, D), BF),
        d_agg=v((tokens, D), BF),
        out_part=v((tokens, D), F32),
        out_low=v((tokens, D), BF),
        out_recv=v((ns, tokens, wl), BF),
        pix_src=v((ns, tokens, LANES), BF),
        pix_recv=v((ns, tokens, LANES), BF),
        small_src=v((nd, 16, rows), F32),
        small_recv=v((nd, 16, rows), F32),
        sec_small=v((ns, 16, rows), F32),
        basis_recv=v((ns, rows, CHUNK), BF),
        x_send=v((chunks, nz, rows, CHUNK), BF),
        x_recv=v((chunks, nz, rows, CHUNK), BF),
        keep=v((chunks, nz, rows, CHUNK), F32),
        z_send=v((chunks, nz, rows, CHUNK), BF),
        z_recv=v((chunks, nz, rows, CHUNK), BF),
        final=v((chunks + 2, rows, CHUNK), BF),
    )
    whole = v((nz, 2, rows, tokens), BF)
    shapes.update(gT=whole, contextT=whole, attendedT=whole, normedT=whole, mnormedT=whole)
    part = v((tokens, D), BF)
    shapes.update(rs1_part=part, rs2_part=part, rs3_part=part, rs4_part=part)
    part = v((ns, shard, D), BF)
    shapes.update(rs1_recv=part, rs2_recv=part, rs3_recv=part, rs4_recv=part)
    part = v((8, CHUNK), F32)
    shapes.update(q_src=part, s_src=part, key_src=part, dq_src=part)
    part = v((nd, 8, CHUNK), F32)
    shapes.update(q_recv=part, s_recv=part, key_recv=part, dq_recv=part)
    part = v((nd, blk, CHUNK), F32)
    shapes.update(bv_src=part, bv_recv=part, bv_all=part, m_src=part, m_recv=part, m_all=part)
    count = 9 * nd + 24 * ns + chunks * (1 + nz) + 6 * nz + 16 + 2 * zq + chunks * ns
    dma = pltpu.SemaphoreType.DMA
    shapes.update(send=dma((count,)), recv=dma((count,)), local=dma((32 + 2 * zq,)))
    return shapes


def fused(ns, nd, near, far):
    tokens = near["patches"].shape[0]
    rows = D // nd
    shapes = scratch(ns, nd, tokens)
    arrays = {**near, **far}
    hbm = pl.BlockSpec(memory_space=pl.ANY)
    vmem = pl.BlockSpec(memory_space=pltpu.VMEM)
    outs = dict(
        activations=((tokens, D // ns), BF, vmem),
        patches=((tokens, LANES), BF, vmem),
        basis=((rows, CHUNK), F32, vmem),
        d_query=((ns, 8, D // ns), F32, vmem),
        small=((16, rows), F32, vmem),
        mlp_up=((rows, FF), BF, hbm),
        mlp_down=((rows, FF), BF, hbm),
        attn_wqkv=((rows, 3 * D), BF, hbm),
        attn_wo=((rows, D), BF, hbm),
        agg_wo=((rows, D), BF, hbm),
        agg_wv=((rows, D), BF, hbm),
        agg_wk=((rows, D), BF, hbm),
    )

    def body(*refs):
        n_in, n_out = len(arrays), len(outs)
        kernel(
            ns,
            nd,
            SimpleNamespace(**dict(zip(arrays, refs[:n_in]))),
            SimpleNamespace(**dict(zip(outs, refs[n_in : n_in + n_out]))),
            SimpleNamespace(**dict(zip(shapes, refs[n_in + n_out :]))),
        )

    result = pl.pallas_call(
        body,
        out_shape=[jax.ShapeDtypeStruct(shape, kind) for shape, kind, _ in outs.values()],
        in_specs=[vmem] * len(near) + [hbm] * len(far),
        out_specs=[spec for _, _, spec in outs.values()],
        scratch_shapes=list(shapes.values()),
        compiler_params=pltpu.CompilerParams(
            collective_id=0, has_side_effects=True, vmem_limit_bytes=60 * 1024 * 1024
        ),
        name="block",
    )(*arrays.values())
    return SimpleNamespace(**dict(zip(outs, result)))


def on_device(
    ns,
    nd,
    patches,
    var_ids,
    segment_ids,
    embed_weight,
    var_embed,
    agg_query,
    agg_wq,
    agg_bq,
    agg_wk,
    agg_wv,
    agg_bv,
    agg_wo,
    agg_bo,
    attn_norm_gain,
    attn_norm_bias,
    attn_wqkv,
    attn_bq,
    attn_bv,
    attn_wo,
    attn_bo,
    mlp_norm_gain,
    mlp_norm_bias,
    mlp_up,
    mlp_bup,
    mlp_down,
    mlp_bdown,
    cotangent,
):
    near = dict(
        patches=patches,
        var_ids=var_ids,
        segment_ids=segment_ids,
        embed_weight=embed_weight,
        var_embed=var_embed,
        agg_query=agg_query,
        agg_bq=agg_bq,
        agg_bv=agg_bv,
        agg_bo=agg_bo,
        attn_norm_gain=attn_norm_gain,
        attn_norm_bias=attn_norm_bias,
        attn_bq=attn_bq,
        attn_bv=attn_bv,
        attn_bo=attn_bo,
        mlp_norm_gain=mlp_norm_gain,
        mlp_norm_bias=mlp_norm_bias,
        mlp_bup=mlp_bup,
        mlp_bdown=mlp_bdown,
    )
    far = dict(
        agg_wq=agg_wq,
        agg_wk=agg_wk,
        agg_wv=agg_wv,
        agg_wo=agg_wo,
        attn_wqkv=attn_wqkv,
        attn_wo=attn_wo,
        mlp_up=mlp_up,
        mlp_down=mlp_down,
        cotangent=cotangent,
    )
    near = {name: a.reshape(1, -1) if a.ndim == 1 else a for name, a in near.items()}
    got = fused(ns, nd, near, far)
    r = lax.axis_index("dp")
    rows = D // nd

    def mine(array, size):
        return lax.dynamic_slice_in_dim(array, r * size, size, 0)

    d_query = got.d_query[:, 0, :].reshape(D)
    query = mine(agg_query, rows).astype(BF).astype(F32)
    small = got.small
    return (
        got.activations,
        got.patches[:, : CP // ns],
        got.basis[:, :CP],
        got.basis[:, CP : CP + VARS].T,
        jnp.sum(agg_wq.astype(F32) * d_query, axis=1),
        query[:, None] * d_query,
        mine(d_query, rows),
        got.agg_wk.astype(F32),
        got.agg_wv.astype(F32),
        small[9],
        got.agg_wo.astype(F32),
        small[6],
        small[4],
        small[5],
        got.attn_wqkv.astype(F32),
        small[7],
        small[8],
        got.attn_wo.astype(F32),
        small[3],
        small[1],
        small[2],
        got.mlp_up.astype(F32),
        small[10 : 10 + FF // D].reshape(-1),
        got.mlp_down.astype(F32),
        small[0],
    )


def solution(mesh):
    in_specs = (
        P("dp", None),
        P(),
        P("dp", None),
        P("dp", None),
        P(),
        P(),
        P("dp", None),
        P(),
        P("dp", None),
        P("dp", None),
        P(),
        P("dp", None),
        P(),
        P(),
        P(),
        P("dp", None),
        P(),
        P(),
        P("dp", None),
        P(),
        P(),
        P(),
        P("dp", None),
        P(),
        P("dp", None),
        P(),
        P("dp", "section"),
    )
    out_specs = (
        P("dp", "section"),
        P("dp", "section"),
        P("dp", None),
        P(None, "dp"),
        P("dp"),
        P("dp", None),
        P("dp"),
        P("dp", None),
        P("dp", None),
        P("dp"),
        P("dp", None),
        P("dp"),
        P("dp"),
        P("dp"),
        P("dp", None),
        P("dp"),
        P("dp"),
        P("dp", None),
        P("dp"),
        P("dp"),
        P("dp"),
        P("dp", None),
        P("dp"),
        P("dp", None),
        P("dp"),
    )
    sizes = (mesh.shape["section"], mesh.shape["dp"])
    return jax.shard_map(
        partial(on_device, *sizes), mesh=mesh, in_specs=in_specs, out_specs=out_specs, check_vma=False
    )
```

time: 894 us -> 320 us (0.36)
  waiting for transfers between devices: 616 us -> 0 us
  Pallas kernels: 0 us -> 292 us
  blocking collectives: 111 us -> 0 us
  matrix products: 48 us -> 0 us
  local copies, waits for them, and re-layouts: 54.8 us -> 11.9 us
  other arithmetic: 42.9 us -> 11.1 us
  between operations: 15.3 us -> 0.7 us
    pallas_call x0 -> x1, Pallas kernels: none -> 292 us  [fused(): pl.pallas_call(body, out_shape=[jax.ShapeDtypeStruct(shape, kind) for sha...]
    reduce_scatter x3 -> x0, waiting for transfers between devices: 274 us -> none  [the longest x1 152 us: on_device(): lax.psum_scatter(jnp.concatenate([grad_up, grad_down], axis=1), 'dp', sca...]
    psum x7 -> x0, waiting for transfers between devices: 168 us -> none  [the longest x5 106 us: section_sum(): return lax.psum(part, 'section')]
    all_gather x3 -> x0, waiting for transfers between devices: 163 us -> none  [the longest x1 73.7 us: on_device(): second = lax.all_gather(second, 'dp', axis=0, tiled=True)]
    psum x3 -> x0, blocking collectives: 74.8 us -> none  [the longest x1 37.7 us: on_device(): lax.psum((cross, key_terms, full_small, part_small), 'dp')]
    dot_general x37 -> x0, matrix products: 46.1 us -> none  [the longest x6 12.1 us: project(): return jnp.dot(row_block, matrix, preferred_element_type=jnp.float32)]
    all_gather x5 -> x0, blocking collectives: 35.9 us -> none  [the longest x1 9.75 us: on_device(): context_all = lax.all_gather(context, 'section', axis=1, tiled=True)]
    reduce_sum x15 -> x0, other arithmetic: 14.7 us -> none  [the longest x4 9.26 us: layer_norm(): return centred * lax.rsqrt(variance + epsilon) * norm_gain + shift_vec]
  transfers between devices with their start and end apart: 14 -> 0, of which waited for: 13 -> 0; matrix products, arithmetic and copies ran while one was open for 7% -> 0% of each run, Pallas kernels for 0% -> 0%
where the time goes in v2:
time: 320 us; the launch traced here: 316 us
  Pallas kernels  292 us (91%)
  local copies, waits for them, and re-layouts  11.9 us (4%)
  other arithmetic  11.1 us (3%)
    pallas_call x1, Pallas kernels, fused(): pl.pallas_call(body, out_shape=[jax.ShapeDtypeStruct(shape, kind) for sha...  292 us
    unnamed x24, local copies, waits for them, and re-layouts  6.91 us

profile of v2, /device:TPU:0, one launch (start us, length us, event | category | flops | bytes accessed | tf_op | source)
XLA Modules:
  0.0 316.0 jit_solution(8300350938159775657)
XLA Ops:
  0.7 1.7 copy.52.refs_0_
  2.3 1.5 copy.53.refs_3_
  3.9 292.2 %block.1 = (bf16[256,256]{1,0:T(8,128)(2,1)}, bf16[256,128]{1,0:T(8,128)(2,1)}, f32[128,256]{1,0:T(8,128)}, f32[4,8,256]{2,1,0:T(8,128)}, f32[16,128]{1,0:T(8,12...) custom-call(bf16[256,192]{1,0:T(8,128)(2,1)} %copy.52.refs_0_, ...), custom_call_target="tpu_custom_call" | custom-call | tf_op jit(solution)/shard_map/block/pallas_call | solution.py:810
  296.1 1.5 slice_bitcast_fusion.2
  297.6 0.8 slice.48
  298.4 0.8 convert_convert_fusion
  299.1 1.4 broadcast_multiply_fusion
  300.5 0.6 dynamic_slice.7
  301.1 1.6 copy.55
  302.8 0.9 slice_bitcast_fusion
  303.7 0.7 copy.56
  304.4 1.3 slice_bitcast_fusion.1
  305.6 2.8 convert_element_type.38
  308.4 1.5 convert_element_type.39
  309.9 1.3 convert_element_type.36
  311.2 0.0 copy-done.6
  311.2 0.8 convert_element_type.33
  312.1 0.0 copy-done.5
  312.1 0.8 convert_element_type.34
  312.9 0.0 copy-done.4
  312.9 0.8 convert_element_type.35
  313.8 0.8 convert_element_type.37
  314.6 0.7 copy.54
  315.3 0.7 copy.58
  (15 shorter events, 0.0 us)
Async XLA Ops:
  3.9 295.3 %copy-start.1 = (bf16[128,1024]{1,0:T(8,128)(2,1)S(1)}, bf16[128,1024]{1,0:T(8,128)(2,1)}, u32[]{:S(2)}) copy-start(bf16[128,1024]{1,0:T(8,128)(2,1)} %refs_18_.1) | copy-start | bytes 786436
  299.1 9.3 %copy-start = (bf16[128,4096]{1,0:T(8,128)(2,1)S(1)}, bf16[128,4096]{1,0:T(8,128)(2,1)}, u32[]{:S(2)}) copy-start(bf16[128,4096]{1,0:T(8,128)(2,1)} %get-tuple-element.48) | copy-start | bytes 3145732
  308.4 1.5 copy-start.2
  308.4 2.8 copy-start.6
  309.9 2.2 copy-start.5
  309.9 3.0 copy-start.4
  309.9 3.8 %copy-start.3 = (bf16[128,1024]{1,0:T(8,128)(2,1)S(1)}, bf16[128,1024]{1,0:T(8,128)(2,1)}, u32[]{:S(2)}) copy-start(bf16[128,1024]{1,0:T(8,128)(2,1)} %get-tuple-element.46) | copy-start | bytes 786436
  311.2 3.4 %copy-start.8 = (bf16[256,128]{1,0:T(8,128)(2,1)S(1)}, bf16[256,128]{1,0:T(8,128)(2,1)}, u32[]{:S(2)}) copy-start(bf16[256,128]{1,0:T(8,128)(2,1)} %get-tuple-element.38) | copy-start | bytes 196612
  311.2 4.1 %copy-start.7 = (bf16[256,256]{1,0:T(8,128)(2,1)S(1)}, bf16[256,256]{1,0:T(8,128)(2,1)}, u32[]{:S(2)}) copy-start(bf16[256,256]{1,0:T(8,128)(2,1)} %get-tuple-element.111) | copy-start | bytes 393220

commit v3 on v2

--- a/solution.py
+++ b/solution.py
@@ -88,7 +88,7 @@
     z, x = lax.div(r, nx), lax.rem(r, nx)
     i, o = refs_in, refs_out
     rows = D // nd
-    tokens = i.patches.shape[0]
+    tokens = i.patches.shape[1]
     shard = tokens // ns
     wl, fl, hl = D // ns, FF // ns, HEADS // ns
     zq = nz // ns
@@ -168,15 +168,33 @@
         local(i.agg_wk.at[:, own_cols], sc.wk),
         local(i.agg_wv.at[:, own_cols], sc.wv),
     ]
-    qkv_loads = [
-        local(
-            i.attn_wqkv.at[:, pl.ds(pl.multiple_of(j * D + s * wl, LANES), wl)],
-            sc.qkv_w.at[z, x, :, pl.ds(j * wl, wl)],
-        )
-        for j in range(3)
+    sources = [(i.agg_wo, sc.awo_c, 0, s * wl)]
+    sources += [(i.attn_wqkv, sc.qkv_w, j * wl, j * D + s * wl) for j in range(3)]
+    sources += [(i.attn_wo, sc.two_c, 0, s * wl)]
+    sources += [(i.mlp_up, sc.up_w, j * CHUNK, s * fl + j * CHUNK) for j in range(fl // CHUNK)]
+    sources += [(i.mlp_down, sc.down_w, j * CHUNK, s * fl + j * CHUNK) for j in range(fl // CHUNK)]
+    pieces = [(dst, pl.ds(at, CHUNK)) for _, dst, at, _ in sources]
+    piece_loads = [
+        local(src.at[:, pl.ds(pl.multiple_of(col, LANES), CHUNK)], dst.at[z, x, :, pl.ds(at, CHUNK)])
+        for src, dst, at, col in sources
     ]
-    up_load = local(i.mlp_up.at[:, own_ff], sc.up_w.at[z, x])
-    down_load = local(i.mlp_down.at[:, own_ff], sc.down_w.at[z, x])
+    n_pieces = len(pieces)
+    from_z, from_x = {}, {}
+
+    def issue_z(count):
+        for c in range(len(from_z), min(len(from_z) + count, n_pieces)):
+            dst, cols = pieces[c]
+            block = dst.at[z, x, :, cols]
+            from_z[c] = over_z(lambda t, block=block: block, block)
+
+    def forward(count):
+        for c in range(len(from_x), min(len(from_x) + count, n_pieces)):
+            from_z[c].wait_recv()
+            dst, cols = pieces[c]
+            half = dst.at[:, x, :, cols]
+            from_x[c] = over_x(half, half)
+            issue_z(1)
+
     cot_load = local(i.cotangent, sc.g_full.at[:, own_cols])
 
     barrier = pltpu.get_barrier_semaphore()
@@ -200,7 +218,7 @@
     sc.place[...] = place
     lane = iota((tokens, CHUNK), 1)
     ones = ((lane >= CP) & (lane < CP + VARS)).astype(F32)
-    sc.pix[...] = (nn(i.patches[...], place) + ones).astype(BF)
+    sc.pix[...] = (tn(i.patches[...], place) + ones).astype(BF)
     row = iota((CHUNK, LANES), 0)
     lane = iota((CHUNK, LANES), 1)
     owner = jnp.where(row < CP, row >> 2, row - CP)
@@ -213,10 +231,11 @@
     row = iota((VARS, CHUNK), 0)
     widen_var = (lane == row + CP).astype(F32).astype(BF)
     var_rows = nt(chosen, i.var_embed[...].astype(BF)).astype(BF)
-    sc.basis[...] = (nn(i.embed_weight[...], widen) + nn(var_rows, widen_var)).astype(BF)
+    sc.basis[...] = (tn(i.embed_weight[...], widen) + nn(var_rows, widen_var)).astype(BF)
     query = jnp.broadcast_to(i.agg_query[...].astype(BF).astype(F32), (16, D))
     query = jnp.where(iota((16, D), 0) == 0, query, 0.0).astype(BF)
     query_rows = nt(query, chosen).astype(BF)
+    o.query_rows[...] = query_rows
     sc.vecs[...] = jnp.zeros_like(sc.vecs)
     sc.bup[...] = jnp.zeros_like(sc.bup)
 
@@ -228,8 +247,70 @@
     for t in range(nd):
         sc.bv_src[t] = value_part[t * blk : (t + 1) * blk]
     cot_load.wait()
+    for copy in piece_loads:
+        copy.wait()
 
     pl.semaphore_wait(barrier, ns - 1 + nd - 1)
+
+    def weight(ref):
+        return ref[...].reshape(ref.shape[0] * ref.shape[1] * ref.shape[2], ref.shape[3])
+
+    def scatter(part, landed, value):
+        part[...] = value.astype(BF)
+        transfer = over_section(lambda t: part.at[pl.ds(pl.multiple_of(t * shard, 16), shard)], landed.at[s])
+        landed[s] = part[own_rows, :]
+        return transfer
+
+    def gather(full, value):
+        full[own_rows, :] = value.astype(BF)
+        return over_section(lambda t: full.at[own_rows], full.at[own_rows])
+
+    def landed_sum(landed):
+        total = landed[0].astype(F32)
+        for k in range(1, ns):
+            total = total + landed[k].astype(F32)
+        return total
+
+    def normal(value):
+        centred = value - jnp.mean(value, axis=-1, keepdims=True)
+        rstd = lax.rsqrt(jnp.mean(centred * centred, axis=-1, keepdims=True) + epsilon)
+        return centred * rstd, rstd
+
+    def whole_norm(full, gain, bias, dst):
+        for t in range(ns):
+            at = slice(t * shard, (t + 1) * shard)
+            hat, _ = normal(full[at, :].astype(F32))
+            dst[at, :] = (hat * gain[...] + bias[...]).astype(BF)
+
+    def kept_norm(full, kept, rstd_kept):
+        hat, rstd = normal(full[own_rows, :].astype(F32))
+        kept[...] = hat
+        rstd_kept[...] = jnp.broadcast_to(rstd, rstd_kept.shape)
+
+    def norm_back(grad, gain, kept, rstd_kept, gain_row, bias_row):
+        hat = kept[...]
+        sc.vecs[gain_row : gain_row + 1, :] = colsum(grad * hat)
+        sc.vecs[bias_row : bias_row + 1, :] = colsum(grad)
+        inner = grad * gain[...]
+        mean = jnp.mean(inner, axis=-1, keepdims=True)
+        dot = jnp.mean(inner * hat, axis=-1, keepdims=True)
+        return rstd_kept[:, 0:1] * (inner - mean - hat * dot)
+
+    def transposed(full, dst):
+        for j in range(D // CHUNK):
+            turned = full[:, j * CHUNK : (j + 1) * CHUNK].astype(F32).T.astype(BF)
+            n = dst.shape[0] // (D // CHUNK)
+            dst[j * n : (j + 1) * n] = turned.reshape((n,) + dst.shape[1:])
+
+    def by_rows(cols, dst):
+        at = pl.ds(s * zq, zq)
+        dst[:, :, :, own_cols] = cols[at]
+        return over_section(
+            lambda t: cols.at[pl.ds(t * zq, zq)], dst.at[:, :, :, own_cols]
+        )
+
+    def columns(ref, j):
+        return ref[:, :, :, j * CHUNK : (j + 1) * CHUNK].reshape(D, CHUNK)
 
     def push(src, dst):
         transfer = over_dp(lambda t: src, dst.at[r])
@@ -246,60 +327,6 @@
     bv_rs = over_dp(lambda t: sc.bv_src.at[t], sc.bv_recv.at[r])
     sc.bv_recv[r] = sc.bv_src[r]
     g_gather = over_section(lambda t: sc.g_full.at[:, own_cols], sc.g_full.at[:, own_cols])
-
-    def rows_out(whole, dst):
-        base = sems(zq)
-        base_send = sems(nz)
-        local_base = local_used["n"]
-        local_used["n"] += zq
-
-        def make(j, k):
-            t = lax.rem(z + k, nz)
-            return pltpu.make_async_remote_copy(
-                src_ref=whole,
-                dst_ref=dst.at[j, x],
-                send_sem=send.at[base_send + k],
-                recv_sem=recv.at[base + j],
-                device_id=(s, t * nx + x),
-                device_id_type=MESH,
-            )
-
-        def go(j):
-            @pl.when(z == s * zq + j)
-            def _():
-                pltpu.make_async_copy(whole, dst.at[j, x], sc.local.at[local_base + j]).start()
-                each(1, nz, lambda k: make(j, k).start())
-
-        def arrive(j):
-            @pl.when(z == s * zq + j)
-            def _():
-                pltpu.make_async_copy(whole, dst.at[j, x], sc.local.at[local_base + j]).wait()
-
-            @pl.when(z != s * zq + j)
-            def _():
-                make(j, 1).wait_recv()
-
-        def finish(j):
-            @pl.when(z == s * zq + j)
-            def _():
-                each(1, nz, lambda k: make(j, k).wait_send())
-
-        def start():
-            each(0, zq, go)
-
-        def forward():
-            each(0, zq, arrive)
-            return over_x(dst.at[:, x], dst.at[:, x])
-
-        return start, forward, lambda: each(0, zq, finish)
-
-    awo_start, awo_forward, awo_finish = rows_out(i.agg_wo, sc.awo)
-    two_start, two_forward, two_finish = rows_out(i.attn_wo, sc.two)
-    awo_start()
-    for copy in qkv_loads:
-        copy.wait()
-    qkv_z = over_z(lambda t: sc.qkv_w.at[z, x], sc.qkv_w.at[z, x])
-    two_start()
 
     q_push.wait_recv()
     query_proj = summed(sc.q_recv, nd)[0:1] + i.agg_bq[:, own_cols]
@@ -313,8 +340,7 @@
     bv_rs.wait_recv()
     sc.bv_own[...] = summed(sc.bv_recv, nd)
     bv_ag = push(sc.bv_own, sc.bv_all)
-    up_load.wait()
-    up_z = over_z(lambda t: sc.up_w.at[z, x], sc.up_w.at[z, x])
+    issue_z(2)
 
     s_push.wait_recv()
     score_rows = summed(sc.s_recv, nd)
@@ -332,7 +358,6 @@
         wrep = nt(probs.astype(BF), fold)
         sc.wrep[h] = wrep.astype(BF)
         sc.mixed[h] = (wrep * pix).astype(BF)
-    awo_x = awo_forward()
     bv_ag.wait_recv()
     for t in range(nd):
         sc.bv[t * blk : (t + 1) * blk] = sc.bv_all[t]
@@ -341,76 +366,29 @@
     context = jnp.broadcast_to(i.agg_bv[:, own_cols], (tokens, wl))
     for h in range(hl):
         context = context + jnp.where(head_of == h, nn(sc.mixed[h], value_basis), 0.0)
-    sc.context[...] = context.astype(BF)
-    awo_x.wait_recv()
-
-    def weight(ref):
-        return ref[...].reshape(ref.shape[0] * ref.shape[1] * ref.shape[2], ref.shape[3])
-
-    def scatter(part, landed, value):
-        part[...] = value.astype(BF)
-        transfer = over_section(lambda t: part.at[pl.ds(pl.multiple_of(t * shard, 16), shard)], landed.at[s])
-        landed[s] = part[own_rows, :]
-        return transfer
-
-    def gather(full, value):
-        full[own_rows, :] = value.astype(BF)
-        return over_section(lambda t: full.at[own_rows], full.at[own_rows])
-
-    def landed_sum(landed):
-        total = landed[0].astype(F32)
-        for k in range(1, ns):
-            total = total + landed[k].astype(F32)
-        return total
-
-    def norm(value, gain, bias, kept, rstd_kept):
-        centred = value - jnp.mean(value, axis=-1, keepdims=True)
-        rstd = lax.rsqrt(jnp.mean(centred * centred, axis=-1, keepdims=True) + epsilon)
-        hat = centred * rstd
-        kept[...] = hat
-        rstd_kept[...] = jnp.broadcast_to(rstd, rstd_kept.shape)
-        return hat * gain[...] + bias[...]
-
-    def norm_back(grad, gain, kept, rstd_kept, gain_row, bias_row):
-        hat = kept[...]
-        sc.vecs[gain_row : gain_row + 1, :] = colsum(grad * hat)
-        sc.vecs[bias_row : bias_row + 1, :] = colsum(grad)
-        inner = grad * gain[...]
-        mean = jnp.mean(inner, axis=-1, keepdims=True)
-        dot = jnp.mean(inner * hat, axis=-1, keepdims=True)
-        return rstd_kept[:, 0:1] * (inner - mean - hat * dot)
-
-    def transposed(full, dst):
-        for j in range(D // CHUNK):
-            turned = full[:, j * CHUNK : (j + 1) * CHUNK].astype(F32).T.astype(BF)
-            n = dst.shape[0] // (D // CHUNK)
-            dst[j * n : (j + 1) * n] = turned.reshape((n,) + dst.shape[1:])
-
-    def head_block(value, dst):
-        at = pl.ds(s * zq, zq)
-        dst[at] = value.astype(F32).T.astype(BF).reshape((zq,) + dst.shape[1:])
-        return over_section(lambda t: dst.at[at], dst.at[at])
-
-    rs1 = scatter(sc.rs1_part, sc.rs1_recv, nn(sc.context[...], weight(sc.awo)))
-    context_gather = head_block(sc.context[...], sc.contextT)
+    sc.context_full[:, own_cols] = context.astype(BF)
+    context_gather = over_section(lambda t: sc.context_full.at[:, own_cols], sc.context_full.at[:, own_cols])
+    issue_z(1)
+    forward(1)
     g_gather.wait_recv()
-    qkv_z.wait_recv()
-    qkv_x = over_x(sc.qkv_w.at[:, x], sc.qkv_w.at[:, x])
-    down_load.wait()
-    down_z = over_z(lambda t: sc.down_w.at[z, x], sc.down_w.at[z, x])
-    rs1.wait_recv()
-    agg = (landed_sum(sc.rs1_recv) + i.agg_bo[...]).astype(BF).astype(F32)
-    sc.agg[...] = agg
-    ag1 = gather(sc.normed, norm(agg, i.attn_norm_gain, i.attn_norm_bias, sc.hat1, sc.rstd1))
-    two_x = two_forward()
     transposed(sc.g_full, sc.gT)
-    qkv_x.wait_recv()
-    ag1.wait_recv()
-
+    context_gather.wait_recv()
+    forward(1)
+    from_x[0].wait_recv()
+    part = nn(sc.context_full[...], weight(sc.awo_c)) + i.agg_bo[:, own_cols]
+    sc.agg_full[:, own_cols] = part.astype(BF)
+    agg_gather = over_section(lambda t: sc.agg_full.at[:, own_cols], sc.agg_full.at[:, own_cols])
+    transposed(sc.context_full, sc.contextT)
+    forward(1)
+    agg_gather.wait_recv()
+    whole_norm(sc.agg_full, i.attn_norm_gain, i.attn_norm_bias, sc.normed)
+    kept_norm(sc.agg_full, sc.hat1, sc.rstd1)
+    transposed(sc.normed, sc.normedT)
+    forward(1)
     normed = sc.normed[...]
-    qkv_w = weight(sc.qkv_w)
     for j in range(3):
-        part = nn(normed, qkv_w[:, j * wl : (j + 1) * wl])
+        from_x[1 + j].wait_recv()
+        part = nn(normed, columns(sc.qkv_w, j))
         if j == 0:
             part = part + i.attn_bq[:, own_cols]
         if j == 2:
@@ -442,34 +420,41 @@
         sc.attended[b * LEN : (b + 1) * LEN, p * LANES : (p + 1) * LANES] = pick(
             nn(probs.astype(BF), v)
         ).astype(BF)
-    two_x.wait_recv()
-    rs2 = scatter(sc.rs2_part, sc.rs2_recv, nn(sc.attended[...], weight(sc.two)))
-    attended_gather = head_block(sc.attended[...], sc.attendedT)
-    up_z.wait_recv()
-    up_x = over_x(sc.up_w.at[:, x], sc.up_w.at[:, x])
-    transposed(sc.normed, sc.normedT)
-    rs2.wait_recv()
-    mid = (sc.agg[...] + landed_sum(sc.rs2_recv) + i.attn_bo[...]).astype(BF).astype(F32)
-    sc.mid[...] = mid
-    ag2 = gather(sc.mnormed, norm(mid, i.mlp_norm_gain, i.mlp_norm_bias, sc.hat2, sc.rstd2))
-    ag2.wait_recv()
-    up_x.wait_recv()
-
-    def columns(ref, j):
-        return ref[:, :, :, j * CHUNK : (j + 1) * CHUNK].reshape(D, CHUNK)
-
+    sc.attended_full[:, own_cols] = sc.attended[...]
+    attended_gather = over_section(
+        lambda t: sc.attended_full.at[:, own_cols], sc.attended_full.at[:, own_cols]
+    )
+    forward(1)
+    attended_gather.wait_recv()
+    forward(1)
+    from_x[4].wait_recv()
+    part = nn(sc.attended_full[...], weight(sc.two_c)) + i.attn_bo[:, own_cols]
+    sc.mid_full[:, own_cols] = (part + sc.agg_full[:, own_cols].astype(F32)).astype(BF)
+    mid_gather = over_section(lambda t: sc.mid_full.at[:, own_cols], sc.mid_full.at[:, own_cols])
+    transposed(sc.attended_full, sc.attendedT)
+    forward(1)
+    mid_gather.wait_recv()
+    awo_rows = by_rows(sc.awo_c, sc.awo)
+    two_rows = by_rows(sc.two_c, sc.two)
+    whole_norm(sc.mid_full, i.mlp_norm_gain, i.mlp_norm_bias, sc.mnormed)
+    kept_norm(sc.mid_full, sc.hat2, sc.rstd2)
+    transposed(sc.mnormed, sc.mnormedT)
+    forward(2)
     mnormed = sc.mnormed[...]
     for j in range(fl // CHUNK):
         at = slice(j * CHUNK, (j + 1) * CHUNK)
         bias = i.mlp_bup[:, pl.ds(pl.multiple_of(s * fl + j * CHUNK, LANES), CHUNK)]
+        from_x[5 + j].wait_recv()
         hidden = nn(mnormed, columns(sc.up_w, j)) + bias
         phi = 0.5 + 0.5 * lax.erf(hidden * 0.7071067811865476)
         density = jnp.exp(hidden * hidden * -0.5) * 0.3989422804014327
         sc.act[:, at] = (hidden * phi).astype(BF)
         sc.slope[:, at] = phi + hidden * density
-    down_z.wait_recv()
-    down_x = over_x(sc.down_w.at[:, x], sc.down_w.at[:, x])
-
+        if j == 0:
+            forward(1)
+        if j == 2:
+            forward(1)
+    forward(2)
     names = (
         [(o.mlp_down, s * fl + j * CHUNK) for j in range(fl // CHUNK)]
         + [(o.mlp_up, s * fl + j * CHUNK) for j in range(fl // CHUNK)]
@@ -477,7 +462,7 @@
         + [(o.attn_wqkv, j * D + s * wl) for j in range(3)]
         + [(o.agg_wo, s * wl)]
     )
-    to_x, to_z = {}, {}
+    to_x, to_z, made, done = {}, {}, [], []
     out_copies, out_sends = [], []
 
     def produce(c, left, right):
@@ -486,11 +471,16 @@
             return nn(block, right).reshape(nz, rows, CHUNK)
 
         sc.x_send[c] = half(1 - x).astype(BF)
-        to_x[c] = over_x(sc.x_send.at[c], sc.x_recv.at[c])
+        made.append(c)
         sc.keep[c] = half(x)
+
+    def issue_x(count):
+        for c in made[len(to_x) : len(to_x) + count]:
+            to_x[c] = over_x(sc.x_send.at[c], sc.x_recv.at[c])
 
     def middle(c):
         to_x[c].wait_recv()
+        issue_x(1)
         sc.z_send[c] = (sc.keep[c] + sc.x_recv[c].astype(F32)).astype(BF)
         to_z[c] = over_z(lambda t: sc.z_send.at[c, t], sc.z_recv.at[c, z])
         sc.z_recv[c, z] = sc.z_send[c, z]
@@ -508,18 +498,27 @@
         sc.final[c] = total.astype(BF)
         publish(c, *names[c])
 
+    def pump(count):
+        for _ in range(count):
+            c = len(to_z)
+            if c < len(names):
+                middle(c)
+            if len(done) < len(names) and (c == len(names) or len(done) < c - 1):
+                finish(len(done))
+                done.append(c)
+
     for j in range(fl // CHUNK):
         produce(j, sc.gT, sc.act[:, j * CHUNK : (j + 1) * CHUNK])
-    transposed(sc.mnormed, sc.mnormedT)
-    down_x.wait_recv()
+    issue_x(3)
     g_full = sc.g_full[...]
+    nmlp = fl // CHUNK
     for j in range(fl // CHUNK):
         at = slice(j * CHUNK, (j + 1) * CHUNK)
+        from_x[5 + nmlp + j].wait_recv()
         d_hidden = nn(g_full, columns(sc.down_w, j)) * sc.slope[:, at]
         sc.d_hidden[:, at] = d_hidden.astype(BF)
     up_w = weight(sc.up_w)
     rs3 = scatter(sc.rs3_part, sc.rs3_recv, nt(sc.d_hidden[...], up_w))
-    nmlp = fl // CHUNK
     for j in range(nmlp):
         at = slice(j * CHUNK, (j + 1) * CHUNK)
         produce(nmlp + j, sc.mnormedT, sc.d_hidden[:, at])
@@ -533,16 +532,16 @@
     ag3 = gather(sc.d_mid, d_mid)
     d_mid = d_mid.astype(F32)
     sc.out_part[...] = nt(sc.act[...], weight(sc.down_w))
-    sc.out_part[own_rows, :] = sc.out_part[own_rows, :] + sc.mid[...] + i.mlp_bdown[...]
+    sc.out_part[own_rows, :] = sc.out_part[own_rows, :] + sc.mid_full[own_rows, :].astype(F32) + i.mlp_bdown[...]
     sc.out_low[...] = sc.out_part[...].astype(BF)
     out_rs = over_section(
         lambda t: sc.out_low.at[:, pl.ds(pl.multiple_of(t * wl, LANES), wl)], sc.out_recv.at[s]
     )
     sc.out_recv[s] = sc.out_low[:, own_cols]
-    for c in range(2):
-        middle(c)
+    pump(1)
     ag3.wait_recv()
 
+    two_rows.wait_recv()
     d_att = nt(sc.d_mid[...], weight(sc.two)).astype(BF)
     sc.d_att[...] = d_att
     for n, (b, p) in enumerate(tiles):
@@ -557,37 +556,32 @@
             lanes = slice(j * wl + p * LANES, j * wl + (p + 1) * LANES)
             sc.d_qkv[b * LEN : (b + 1) * LEN, lanes] = parts[j].astype(BF)
     rs4 = scatter(sc.rs4_part, sc.rs4_recv, nt(sc.d_qkv[...], weight(sc.qkv_w)))
-    attended_gather.wait_recv()
     produce(2 * nmlp, sc.attendedT, sc.d_mid[:, own_cols])
     for j in range(3):
         produce(2 * nmlp + 1 + j, sc.normedT, sc.d_qkv[:, j * wl : (j + 1) * wl])
     sc.vecs[7:8, own_cols] = colsum(sc.d_qkv[:, 0:wl])
     sc.vecs[8:9, own_cols] = colsum(sc.d_qkv[:, 2 * wl : 3 * wl])
-    for c in range(2, 4):
-        middle(c)
+    pump(1)
     rs4.wait_recv()
     d_agg = norm_back(landed_sum(sc.rs4_recv), i.attn_norm_gain, sc.hat1, sc.rstd1, 4, 5)
     d_agg = (sc.d_mid[own_rows, :].astype(F32) + d_agg).astype(BF)
     sc.vecs[6:7, :] = colsum(d_agg)
     ag4 = gather(sc.d_agg, d_agg)
-    for c in range(4, 6):
-        middle(c)
-    finish(0)
-    finish(1)
+    pump(1)
     ag4.wait_recv()
 
-    context_gather.wait_recv()
+    awo_rows.wait_recv()
     produce(2 * nmlp + 4, sc.contextT, sc.d_agg[:, own_cols])
     d_context = nt(sc.d_agg[...], weight(sc.awo)).astype(BF)
     sc.vecs[9:10, own_cols] = colsum(d_context)
     value_basis = sc.bv[...].astype(BF)
-    cross = jnp.zeros((wl, CHUNK), F32)
+    cross = jnp.zeros((CHUNK, wl), F32)
     grad_pix = jnp.zeros((tokens, CHUNK), F32)
     sc.key_src[...] = jnp.zeros_like(sc.key_src)
     for h in range(hl):
         masked = d_context * (head_of == h).astype(F32).astype(BF)
         pulled = nt(masked, value_basis)
-        cross = cross + tn(masked, sc.mixed[h])
+        cross = cross + tn(sc.mixed[h], masked)
         pix = sc.pix[...].astype(F32)
         high, low = split(pulled * pix)
         d_weights = nn(high, fold) + nn(low, fold)
@@ -605,7 +599,7 @@
     grad_pix = grad_pix.astype(BF)
     pw = CP // ns
     for t in range(ns):
-        sc.pix_src[t, :, 0:pw] = nt(grad_pix, sc.place[t * pw : (t + 1) * pw, :]).astype(BF)
+        sc.pix_src[t] = nt(sc.place[t * pw : (t + 1) * pw, :], grad_pix).astype(BF)
     pix_rs = over_section(lambda t: sc.pix_src.at[t], sc.pix_recv.at[s])
     sc.pix_recv[s] = sc.pix_src[s]
     for t in range(nd):
@@ -616,11 +610,10 @@
     small_rs = over_dp(lambda t: sc.small_src.at[t], sc.small_recv.at[r])
     sc.small_recv[r] = sc.small_src[r]
 
-    middle(6)
+    pump(2)
     m_rs.wait_recv()
     sc.m_own[...] = summed(sc.m_recv, nd)
     m_ag = push(sc.m_own, sc.m_all)
-    middle(7)
     key_push.wait_recv()
     key_terms = summed(sc.key_recv, nd)
     wide = jnp.concatenate([jnp.broadcast_to(key_terms[h : h + 1], (HEAD, CHUNK)) for h in range(hl)], axis=0)
@@ -631,59 +624,46 @@
     count = len(names)
     sc.final[count] = (d_key * (sc.query_proj[...] * scale)).astype(BF)
     publish(count, o.agg_wk, s * wl)
-    finish(2)
+    pump(2)
     small_rs.wait_recv()
     sc.sec_small[s] = summed(sc.small_recv, nd)
     small_ag = over_section(lambda t: sc.sec_small.at[s], sc.sec_small.at[s])
-    middle(8)
-    finish(3)
+    pump(1)
     m_ag.wait_recv()
     for t in range(nd):
         sc.cross[t * blk : (t + 1) * blk] = sc.m_all[t]
     cross = sc.cross[...].astype(BF)
-    sc.final[count + 1] = nt(sc.basis[...], cross).astype(BF)
+    sc.final[count + 1] = nn(sc.basis[...], cross).astype(BF)
     publish(count + 1, o.agg_wv, s * wl)
     key_low = jnp.concatenate([key_terms, jnp.zeros_like(key_terms)], axis=0).astype(BF)
-    grad_basis = nn(sc.wv[...], cross) + tn(sc.key_query[...], key_low)
+    grad_basis = nt(cross, sc.wv[...]) + tn(key_low, sc.key_query[...])
     sc.basis_recv[s] = grad_basis.astype(BF)
     basis_sum = over_section(lambda t: sc.basis_recv.at[s], sc.basis_recv.at[s])
+    pump(1)
     dq_push.wait_recv()
     o.d_query[s] = summed(sc.dq_recv, nd)
     dq_gather = over_section(lambda t: o.d_query.at[s], o.d_query.at[s])
-    middle(9)
-    finish(4)
-    middle(10)
-    finish(5)
-    middle(11)
-    finish(6)
-    middle(12)
-    finish(7)
+
+    def section_total(ref):
+        total = ref[0].astype(F32)
+        for k in range(1, ns):
+            total = total + ref[k].astype(F32)
+        return total
+
+    out_rs.wait_recv()
+    o.activations[...] = section_total(sc.out_recv).astype(BF)
+    pix_rs.wait_recv()
+    o.patches[...] = section_total(sc.pix_recv).astype(BF)
     small_ag.wait_recv()
     o.small[...] = summed(sc.sec_small, ns)
-    pix_rs.wait_recv()
-    total = sc.pix_recv[0].astype(F32)
-    for k in range(1, ns):
-        total = total + sc.pix_recv[k].astype(F32)
-    o.patches[...] = total.astype(BF)
-    out_rs.wait_recv()
-    total = sc.out_recv[0].astype(F32)
-    for k in range(1, ns):
-        total = total + sc.out_recv[k].astype(F32)
-    o.activations[...] = total.astype(BF)
+    pump(20)
     basis_sum.wait_recv()
-    total = sc.basis_recv[0].astype(F32)
-    for k in range(1, ns):
-        total = total + sc.basis_recv[k].astype(F32)
-    o.basis[...] = total
-    for c in range(8, 13):
-        finish(c)
+    o.basis[...] = section_total(sc.basis_recv)
     dq_gather.wait_recv()
     for transfer in out_sends:
         transfer.wait_recv()
     for copy in out_copies:
         copy.wait()
-    awo_finish()
-    two_finish()
     for transfer in pending:
         transfer.wait_send()
     assert used["n"] <= send.shape[0], used["n"]
@@ -703,6 +683,8 @@
         qkv_w=v((nz, 2, rows, 3 * wl), BF),
         up_w=v((nz, 2, rows, fl), BF),
         down_w=v((nz, 2, rows, fl), BF),
+        awo_c=v((nz, 2, rows, wl), BF),
+        two_c=v((nz, 2, rows, wl), BF),
         awo=v((zq, 2, rows, D), BF),
         two=v((zq, 2, rows, D), BF),
         g_full=v((tokens, D), BF),
@@ -722,9 +704,10 @@
         probs=v((hl, tokens, LANES), F32),
         wrep=v((hl, tokens, CHUNK), BF),
         mixed=v((hl, tokens, CHUNK), BF),
-        context=v((tokens, wl), BF),
-        agg=v((shard, D), F32),
-        mid=v((shard, D), F32),
+        context_full=v((tokens, D), BF),
+        attended_full=v((tokens, D), BF),
+        agg_full=v((tokens, D), BF),
+        mid_full=v((tokens, D), BF),
         hat1=v((shard, D), F32),
         hat2=v((shard, D), F32),
         rstd1=v((shard, LANES), F32),
@@ -744,12 +727,12 @@
         out_part=v((tokens, D), F32),
         out_low=v((tokens, D), BF),
         out_recv=v((ns, tokens, wl), BF),
-        pix_src=v((ns, tokens, LANES), BF),
-        pix_recv=v((ns, tokens, LANES), BF),
+        pix_src=v((ns, CP // ns, tokens), BF),
+        pix_recv=v((ns, CP // ns, tokens), BF),
         small_src=v((nd, 16, rows), F32),
         small_recv=v((nd, 16, rows), F32),
         sec_small=v((ns, 16, rows), F32),
-        basis_recv=v((ns, rows, CHUNK), BF),
+        basis_recv=v((ns, CHUNK, rows), BF),
         x_send=v((chunks, nz, rows, CHUNK), BF),
         x_recv=v((chunks, nz, rows, CHUNK), BF),
         keep=v((chunks, nz, rows, CHUNK), F32),
@@ -760,23 +743,23 @@
     whole = v((nz, 2, rows, tokens), BF)
     shapes.update(gT=whole, contextT=whole, attendedT=whole, normedT=whole, mnormedT=whole)
     part = v((tokens, D), BF)
-    shapes.update(rs1_part=part, rs2_part=part, rs3_part=part, rs4_part=part)
+    shapes.update(rs3_part=part, rs4_part=part)
     part = v((ns, shard, D), BF)
-    shapes.update(rs1_recv=part, rs2_recv=part, rs3_recv=part, rs4_recv=part)
+    shapes.update(rs3_recv=part, rs4_recv=part)
     part = v((8, CHUNK), F32)
     shapes.update(q_src=part, s_src=part, key_src=part, dq_src=part)
     part = v((nd, 8, CHUNK), F32)
     shapes.update(q_recv=part, s_recv=part, key_recv=part, dq_recv=part)
     part = v((nd, blk, CHUNK), F32)
     shapes.update(bv_src=part, bv_recv=part, bv_all=part, m_src=part, m_recv=part, m_all=part)
-    count = 9 * nd + 24 * ns + chunks * (1 + nz) + 6 * nz + 16 + 2 * zq + chunks * ns
+    count = 9 * nd + 24 * ns + 2 * chunks * (1 + nz) + chunks * ns
     dma = pltpu.SemaphoreType.DMA
-    shapes.update(send=dma((count,)), recv=dma((count,)), local=dma((32 + 2 * zq,)))
+    shapes.update(send=dma((count,)), recv=dma((count,)), local=dma((8 + 2 * chunks + 4,)))
     return shapes
 
 
 def fused(ns, nd, near, far):
-    tokens = near["patches"].shape[0]
+    tokens = near["patches"].shape[1]
     rows = D // nd
     shapes = scratch(ns, nd, tokens)
     arrays = {**near, **far}
@@ -784,8 +767,9 @@
     vmem = pl.BlockSpec(memory_space=pltpu.VMEM)
     outs = dict(
         activations=((tokens, D // ns), BF, vmem),
-        patches=((tokens, LANES), BF, vmem),
-        basis=((rows, CHUNK), F32, vmem),
+        patches=((CP // ns, tokens), BF, vmem),
+        basis=((CHUNK, rows), F32, vmem),
+        query_rows=((16, rows), BF, vmem),
         d_query=((ns, 8, D // ns), F32, vmem),
         small=((16, rows), F32, vmem),
         mlp_up=((rows, FF), BF, hbm),
@@ -819,6 +803,93 @@
         name="block",
     )(*arrays.values())
     return SimpleNamespace(**dict(zip(outs, result)))
+
+
+def widen(nd, got, agg_wq):
+    rows = D // nd
+    step = min(rows, 32)
+    big = dict(
+        mlp_up=got.mlp_up,
+        mlp_down=got.mlp_down,
+        attn_wqkv=got.attn_wqkv,
+        attn_wo=got.attn_wo,
+        agg_wo=got.agg_wo,
+        agg_wv=got.agg_wv,
+        agg_wk=got.agg_wk,
+    )
+    rest = dict(
+        activations=got.activations,
+        patches=got.patches,
+        basis=got.basis,
+        query_rows=got.query_rows,
+        d_query=got.d_query,
+        small=got.small,
+        agg_wq=agg_wq,
+    )
+    line = (1, rows)
+    outs = dict(
+        activations=(got.activations.shape, BF),
+        patches=(got.patches.shape, BF),
+        embed=((CP, rows), F32),
+        var=((VARS, rows), F32),
+        query=(line, F32),
+        wq=((rows, D), F32),
+        bq=(line, F32),
+        bup=((1, rows * (FF // D)), F32),
+    )
+    lines = tuple(range(10))
+
+    def body(*refs):
+        n = len(big)
+        for src, dst in zip(refs[:n], refs[n + len(rest) : 2 * n + len(rest)]):
+            dst[...] = src[...].astype(F32)
+        i = SimpleNamespace(**dict(zip(rest, refs[n : n + len(rest)])))
+        left = refs[2 * n + len(rest) :]
+        o = SimpleNamespace(**dict(zip(outs, left)))
+        left = left[len(outs) :]
+        r = lax.axis_index("dp")
+
+        @pl.when(pl.program_id(0) == 0)
+        def _():
+            o.activations[...] = i.activations[...]
+            o.patches[...] = i.patches[...]
+            o.embed[...] = i.basis[0:CP]
+            o.var[...] = i.basis[CP : CP + VARS]
+            d_query = jnp.concatenate([i.d_query[k] for k in range(i.d_query.shape[0])], axis=1)
+            d_query = jnp.concatenate([d_query, d_query], axis=0)
+            d_query = jnp.where(iota(d_query.shape, 0) == 0, d_query, 0.0)
+            high, low = split(d_query)
+            low, rest_low = split(d_query - high.astype(F32))
+            chosen = (iota((rows, D), 1) == iota((rows, D), 0) + r * rows).astype(F32).astype(BF)
+            o.bq[...] = (nt(high, chosen) + nt(low, chosen) + nt(rest_low, chosen))[0:1]
+            weight = i.agg_wq[...]
+            o.query[...] = (nt(high, weight) + nt(low, weight) + nt(rest_low, weight))[0:1]
+            first = i.query_rows[...]
+            o.wq[...] = tn(first, high) + tn(first, low) + tn(first, rest_low)
+            o.bup[...] = jnp.concatenate([i.small[10 + k : 11 + k] for k in range(FF // D)], axis=1)
+            for k in lines:
+                left[k][...] = i.small[k : k + 1]
+
+    def by_step(a):
+        return pl.BlockSpec((step, a.shape[1]), lambda g: (g, 0))
+
+    def fixed(shape):
+        return pl.BlockSpec(shape, lambda g: (0,) * len(shape))
+
+    shaped = [jax.ShapeDtypeStruct(a.shape, F32) for a in big.values()]
+    shaped += [jax.ShapeDtypeStruct(*a) for a in outs.values()]
+    shaped += [jax.ShapeDtypeStruct(line, F32) for _ in lines]
+    result = pl.pallas_call(
+        body,
+        grid=(rows // step,),
+        out_shape=shaped,
+        in_specs=[by_step(a) for a in big.values()] + [fixed(a.shape) for a in rest.values()],
+        out_specs=[by_step(a) for a in big.values()] + [fixed(a.shape) for a in shaped[len(big) :]],
+        compiler_params=pltpu.CompilerParams(vmem_limit_bytes=48 * 1024 * 1024),
+        name="widen",
+    )(*big.values(), *rest.values())
+    names = list(big) + list(outs)
+    return SimpleNamespace(**dict(zip(names, result))), [a.reshape(-1) for a in result[len(names) :]]
 
 
 def on_device(
@@ -884,41 +955,34 @@
         cotangent=cotangent,
     )
     near = {name: a.reshape(1, -1) if a.ndim == 1 else a for name, a in near.items()}
+    near["patches"], near["embed_weight"] = patches.T, embed_weight.T
     got = fused(ns, nd, near, far)
-    r = lax.axis_index("dp")
-    rows = D // nd
-
-    def mine(array, size):
-        return lax.dynamic_slice_in_dim(array, r * size, size, 0)
-
-    d_query = got.d_query[:, 0, :].reshape(D)
-    query = mine(agg_query, rows).astype(BF).astype(F32)
-    small = got.small
+    out, small = widen(nd, got, agg_wq)
     return (
-        got.activations,
-        got.patches[:, : CP // ns],
-        got.basis[:, :CP],
-        got.basis[:, CP : CP + VARS].T,
-        jnp.sum(agg_wq.astype(F32) * d_query, axis=1),
-        query[:, None] * d_query,
-        mine(d_query, rows),
-        got.agg_wk.astype(F32),
-        got.agg_wv.astype(F32),
+        out.activations,
+        out.patches.T,
+        out.embed.T,
+        out.var,
+        out.query.reshape(-1),
+        out.wq,
+        out.bq.reshape(-1),
+        out.agg_wk,
+        out.agg_wv,
         small[9],
-        got.agg_wo.astype(F32),
+        out.agg_wo,
         small[6],
         small[4],
         small[5],
-        got.attn_wqkv.astype(F32),
+        out.attn_wqkv,
         small[7],
         small[8],
-        got.attn_wo.astype(F32),
+        out.attn_wo,
         small[3],
         small[1],
         small[2],
-        got.mlp_up.astype(F32),
-        small[10 : 10 + FF // D].reshape(-1),
-        got.mlp_down.astype(F32),
+        out.mlp_up,
+        out.bup.reshape(-1),
+        out.mlp_down,
         small[0],
     )
 

time: 320 us -> 251 us (0.78)
  Pallas kernels: 292 us -> 235 us
  other arithmetic: 11.1 us -> 0 us
    pallas_call x1, Pallas kernels: 292 us -> 231 us  [fused(): pl.pallas_call(body, out_shape=[jax.ShapeDtypeStruct(shape, kind) for sha...]
    convert_element_type x8 -> x0, other arithmetic: 9.71 us -> none  [the longest x1 2.76 us: on_device(): got.mlp_up.astype(F32)]
    unnamed x24 -> x28, local copies, waits for them, and re-layouts: 6.91 us -> 12.1 us
    pallas_call x0 -> x1, Pallas kernels: none -> 4.5 us  [widen(): pl.pallas_call(body, grid=(rows // step,), out_shape=shaped, in_specs=[by...]
where the time goes in v3:
time: 251 us; the launch traced here: 248 us
  Pallas kernels  235 us (94%)
  local copies, waits for them, and re-layouts  12.1 us (5%)
    pallas_call x1, Pallas kernels, fused(): pl.pallas_call(body, out_shape=[jax.ShapeDtypeStruct(shape, kind) for sha...  231 us
    unnamed x28, local copies, waits for them, and re-layouts  12.1 us

profile of v3, /device:TPU:0, one launch (start us, length us, event | category | flops | bytes accessed | tf_op | source)
XLA Modules:
  0.0 248.4 jit_solution(9884939000489405433)
XLA Ops:
  0.7 0.0 copy-start.2
  0.7 230.9 %block.1 = (bf16[256,256]{1,0:T(8,128)(2,1)}, bf16[48,256]{1,0:T(8,128)(2,1)}, f32[256,128]{1,0:T(8,128)}, bf16[16,128]{1,0:T(8,128)(2,1)}, f32[4,8,256]{2,1,0:T...) custom-call(bf16[192,256]{1,0:T(8,128)(2,1)} %bitcast.31, ...), custom_call_target="tpu_custom_call" | custom-call | tf_op jit(solution)/shard_map/block/pallas_call | solution.py:794
  231.6 0.0 copy-done.2
  231.6 0.0 copy-start
  231.6 1.2 copy-done
  232.8 0.0 copy-start.1
  232.8 1.2 copy-done.1
  234.1 1.1 copy-done.3
  235.2 0.0 copy-start.4
  235.2 0.9 copy-done.4
  236.2 0.0 copy-start.5
  236.2 0.9 copy-done.5
  237.1 0.0 copy-start.6
  237.1 0.9 copy-done.6
  238.1 0.0 copy-start.7
  238.1 0.9 copy-done.7
  239.0 0.0 copy-start.8
  239.0 0.9 copy-done.8
  239.9 0.9 copy-done.9
  240.8 0.8 copy-done.10
  241.6 0.7 copy-done.11
  242.3 0.7 copy-done.12
  243.0 0.7 copy-done.13
  243.7 4.5 %widen.1 = (f32[128,4096]{1,0:T(8,128)}, f32[128,4096]{1,0:T(8,128)}, f32[128,3072]{1,0:T(8,128)}, f32[128,1024]{1,0:T(8,128)}, f32[128,1024]{1,0:T(8,128)}, /*i...) custom-call(bf16[128,4096]{1,0:T(8,128)(2,1)S(1)} %copy-done, ...), custom_call_target="tpu_custom_call" | custom-call | tf_op jit(solution)/shard_map/widen/pallas_call | solution.py:882
  (6 shorter events, 0.0 us)
Async XLA Ops:
  0.7 230.9 %copy-start.2 = (bf16[128,1024]{1,0:T(8,128)(2,1)S(1)}, bf16[128,1024]{1,0:T(8,128)(2,1)}, u32[]{:S(2)}) copy-start(bf16[128,1024]{1,0:T(8,128)(2,1)} %refs_13_.1) | copy-start | bytes 786436
  231.6 1.2 copy-start
  232.8 1.2 copy-start.1
  234.1 1.1 copy-start.3
  235.2 0.9 copy-start.4
  236.2 0.9 copy-start.5
  237.1 0.9 copy-start.6
  238.1 0.9 copy-start.7
  239.0 0.9 copy-start.8
  239.9 0.9 copy-start.9
  240.8 0.8 copy-start.10
  241.6 0.7 copy-start.11
  242.3 0.7 copy-start.12
  243.0 0.7 copy-start.13

commit v4 on v3

--- a/solution.py
+++ b/solution.py
@@ -328,6 +328,7 @@
     sc.bv_recv[r] = sc.bv_src[r]
     g_gather = over_section(lambda t: sc.g_full.at[:, own_cols], sc.g_full.at[:, own_cols])
 
+    issue_z(2)
     q_push.wait_recv()
     query_proj = summed(sc.q_recv, nd)[0:1] + i.agg_bq[:, own_cols]
     sc.query_proj[...] = query_proj
@@ -340,7 +341,7 @@
     bv_rs.wait_recv()
     sc.bv_own[...] = summed(sc.bv_recv, nd)
     bv_ag = push(sc.bv_own, sc.bv_all)
-    issue_z(2)
+    issue_z(1)
 
     s_push.wait_recv()
     score_rows = summed(sc.s_recv, nd)
@@ -358,6 +359,8 @@
         wrep = nt(probs.astype(BF), fold)
         sc.wrep[h] = wrep.astype(BF)
         sc.mixed[h] = (wrep * pix).astype(BF)
+    issue_z(2)
+    forward(1)
     bv_ag.wait_recv()
     for t in range(nd):
         sc.bv[t * blk : (t + 1) * blk] = sc.bv_all[t]
@@ -368,12 +371,10 @@
         context = context + jnp.where(head_of == h, nn(sc.mixed[h], value_basis), 0.0)
     sc.context_full[:, own_cols] = context.astype(BF)
     context_gather = over_section(lambda t: sc.context_full.at[:, own_cols], sc.context_full.at[:, own_cols])
-    issue_z(1)
-    forward(1)
     g_gather.wait_recv()
     transposed(sc.g_full, sc.gT)
+    forward(1)
     context_gather.wait_recv()
-    forward(1)
     from_x[0].wait_recv()
     part = nn(sc.context_full[...], weight(sc.awo_c)) + i.agg_bo[:, own_cols]
     sc.agg_full[:, own_cols] = part.astype(BF)
@@ -394,6 +395,8 @@
         if j == 2:
             part = part + i.attn_bv[:, own_cols]
         sc.qkv[:, j * wl : (j + 1) * wl] = part.astype(BF)
+        if j == 1:
+            forward(1)
     lo = (iota((1, LANES), 1) < HEAD).astype(F32)
     first, second = lo.astype(BF), (1.0 - lo).astype(BF)
 
@@ -439,7 +442,7 @@
     whole_norm(sc.mid_full, i.mlp_norm_gain, i.mlp_norm_bias, sc.mnormed)
     kept_norm(sc.mid_full, sc.hat2, sc.rstd2)
     transposed(sc.mnormed, sc.mnormedT)
-    forward(2)
+    forward(1)
     mnormed = sc.mnormed[...]
     for j in range(fl // CHUNK):
         at = slice(j * CHUNK, (j + 1) * CHUNK)
@@ -480,7 +483,8 @@
 
     def middle(c):
         to_x[c].wait_recv()
-        issue_x(1)
+        if c >= 6:
+            issue_x(1)
         sc.z_send[c] = (sc.keep[c] + sc.x_recv[c].astype(F32)).astype(BF)
         to_z[c] = over_z(lambda t: sc.z_send.at[c, t], sc.z_recv.at[c, z])
         sc.z_recv[c, z] = sc.z_send[c, z]
@@ -509,7 +513,7 @@
 
     for j in range(fl // CHUNK):
         produce(j, sc.gT, sc.act[:, j * CHUNK : (j + 1) * CHUNK])
-    issue_x(3)
+    issue_x(4)
     g_full = sc.g_full[...]
     nmlp = fl // CHUNK
     for j in range(fl // CHUNK):
@@ -523,6 +527,7 @@
         at = slice(j * CHUNK, (j + 1) * CHUNK)
         produce(nmlp + j, sc.mnormedT, sc.d_hidden[:, at])
     sc.bup[:, own_ff] = colsum(sc.d_hidden[...])
+    issue_x(4)
     rs3.wait_recv()
     g_shard = sc.g_full[own_rows, :].astype(F32)
     sc.vecs[0:1, :] = colsum(g_shard)
@@ -538,9 +543,10 @@
         lambda t: sc.out_low.at[:, pl.ds(pl.multiple_of(t * wl, LANES), wl)], sc.out_recv.at[s]
     )
     sc.out_recv[s] = sc.out_low[:, own_cols]
+    pump(2)
+    ag3.wait_recv()
+
     pump(1)
-    ag3.wait_recv()
-
     two_rows.wait_recv()
     d_att = nt(sc.d_mid[...], weight(sc.two)).astype(BF)
     sc.d_att[...] = d_att
@@ -567,7 +573,7 @@
     d_agg = (sc.d_mid[own_rows, :].astype(F32) + d_agg).astype(BF)
     sc.vecs[6:7, :] = colsum(d_agg)
     ag4 = gather(sc.d_agg, d_agg)
-    pump(1)
+    pump(2)
     ag4.wait_recv()
 
     awo_rows.wait_recv()
@@ -610,6 +616,7 @@
     small_rs = over_dp(lambda t: sc.small_src.at[t], sc.small_recv.at[r])
     sc.small_recv[r] = sc.small_src[r]
 
+    issue_x(1)
     pump(2)
     m_rs.wait_recv()
     sc.m_own[...] = summed(sc.m_recv, nd)
@@ -885,7 +892,7 @@
         out_shape=shaped,
         in_specs=[by_step(a) for a in big.values()] + [fixed(a.shape) for a in rest.values()],
         out_specs=[by_step(a) for a in big.values()] + [fixed(a.shape) for a in shaped[len(big) :]],
-        compiler_params=pltpu.CompilerParams(vmem_limit_bytes=48 * 1024 * 1024),
+        compiler_params=pltpu.CompilerParams(vmem_limit_bytes=60 * 1024 * 1024),
         name="widen",
     )(*big.values(), *rest.values())
     names = list(big) + list(outs)

time: 251 us -> 238 us (0.948)
  the two profiles are of different devices: /device:TPU:0 before, /device:TPU:29 now
where the time goes in v4:
time: 238 us
  Pallas kernels  237 us (100%)
    pallas_call x1, Pallas kernels, fused(): pl.pallas_call(body, out_shape=[jax.ShapeDtypeStruct(shape, kind) for sha...  230 us
    pallas_call x1, Pallas kernels, widen(): pl.pallas_call(body, grid=(rows // step,), out_shape=shaped, in_specs=[by...  7.21 us

profile of v4, /device:TPU:29, one launch (start us, length us, event | category | flops | bytes accessed | tf_op | source)
XLA Modules:
  0.0 237.8 jit_solution(18082594363690658231)
XLA Ops:
  0.7 229.8 %block.1 = (bf16[256,256]{1,0:T(8,128)(2,1)}, bf16[48,256]{1,0:T(8,128)(2,1)}, f32[256,128]{1,0:T(8,128)}, bf16[16,128]{1,0:T(8,128)(2,1)}, f32[4,8,256]{2,1,0:T...) custom-call(bf16[192,256]{1,0:T(8,128)(2,1)} %bitcast.31, ...), custom_call_target="tpu_custom_call" | custom-call | tf_op jit(solution)/shard_map/block/pallas_call | solution.py:801
  230.5 7.2 %widen.1 = (f32[128,4096]{1,0:T(8,128)}, f32[128,4096]{1,0:T(8,128)}, f32[128,3072]{1,0:T(8,128)}, f32[128,1024]{1,0:T(8,128)}, f32[128,1024]{1,0:T(8,128)}, /*i...) custom-call(bf16[128,4096]{1,0:T(8,128)(2,1)} %get-tuple-element.63., ...), custom_call_target="tpu_custom_call" | custom-call | tf_op jit(solution)/shard_map/widen/pallas_call | solution.py:889

commit v5 on v4

--- a/solution.py
+++ b/solution.py
@@ -105,12 +105,12 @@
         used["n"] += count
         return base
 
-    def remote(src, dst, sem, device):
+    def remote(src, dst, sem, device, landing=None):
         return pltpu.make_async_remote_copy(
             src_ref=src,
             dst_ref=dst,
             send_sem=send.at[sem],
-            recv_sem=recv.at[sem],
+            recv_sem=recv.at[sem if landing is None else landing],
             device_id=device,
             device_id_type=MESH,
         )
@@ -147,6 +147,122 @@
         transfer = Transfer(make, 1, nz).start()
         pending.append(transfer)
         return transfer
+
+    line = nz == 4
+    partner = z + 1 - 2 * lax.rem(z, 2)
+    inner = (z == 1) | (z == 2)
+    outer = (z == 0) | (z == 3)
+    beyond = [lax.rem(2 * lax.div(z, 2) + 2 + j, 4) for j in range(2)]
+    gate = 2 - lax.div(z, 2)
+
+    def at_z(t):
+        return (s, t * nx + x)
+
+    def line_spread(block):
+        base = sems(8)
+
+        def own(k):
+            to = at_z(partner if k == 0 else gate)
+            return remote(block(z), block(z), base + 4 + k, to, base + z)
+
+        def passed(j):
+            b = beyond[j]
+            return remote(block(b), block(b), base + 6 + j, at_z(partner), base + b)
+
+        for k in range(2):
+            own(k).start()
+
+        def arrived(k):
+            t = [partner, *beyond][k]
+            remote(block(t), block(t), base + 4, at_z(partner), base + t).wait_recv()
+            if k > 0:
+
+                @pl.when(inner)
+                def _():
+                    passed(k - 1).start()
+
+            return t
+
+        def wait_send():
+            for k in range(2):
+                own(k).wait_send()
+
+            @pl.when(inner)
+            def _():
+                for j in range(2):
+                    passed(j).wait_send()
+
+        pending.append(SimpleNamespace(wait_send=wait_send))
+        return arrived
+
+    def spread(block):
+        if line:
+            return line_spread(block)
+        return over_z(lambda t: block(z), block(z)).wait_recv
+
+    def line_reduce(parts, landed, merged):
+        base = sems(5)
+
+        def near():
+            return remote(parts.at[partner], landed.at[0], base, at_z(partner))
+
+        def far(j):
+            return remote(parts.at[beyond[j]], landed.at[2 + j], base + 1 + j, at_z(partner))
+
+        def across(j):
+            return remote(merged.at[j], landed.at[1], base + 3 + j, at_z(beyond[j]), base + 3)
+
+        near().start()
+
+        @pl.when(outer)
+        def _():
+            for j in range(2):
+                far(j).start()
+
+        def merge():
+            @pl.when(inner)
+            def _():
+                for j in range(2):
+                    far(j).wait_recv()
+                    both = parts[beyond[j]].astype(F32) + landed[2 + j].astype(F32)
+                    merged[j] = both.astype(BF)
+                    across(j).start()
+
+        def total():
+            near().wait_recv()
+            across(0).wait_recv()
+            return parts[z].astype(F32) + landed[0].astype(F32) + landed[1].astype(F32)
+
+        def wait_send():
+            near().wait_send()
+
+            @pl.when(outer)
+            def _():
+                for j in range(2):
+                    far(j).wait_send()
+
+            @pl.when(inner)
+            def _():
+                for j in range(2):
+                    across(j).wait_send()
+
+        pending.append(SimpleNamespace(wait_send=wait_send))
+        return SimpleNamespace(merge=merge, total=total)
+
+    def reduce(parts, landed, merged):
+        if line:
+            return line_reduce(parts, landed, merged)
+        transfer = over_z(lambda t: parts.at[t], landed.at[z])
+        landed[z] = parts[z]
+
+        def total():
+            transfer.wait_recv()
+            value = landed[0].astype(F32)
+            for k in range(1, nz):
+                value = value + landed[k].astype(F32)
+            return value
+
+        return SimpleNamespace(merge=lambda: None, total=total)
 
     def over_x(src, dst):
         base = sems(1)
@@ -179,21 +295,39 @@
         for src, dst, at, col in sources
     ]
     n_pieces = len(pieces)
-    from_z, from_x = {}, {}
+    from_z, from_x, own_x = {}, {}, {}
 
     def issue_z(count):
         for c in range(len(from_z), min(len(from_z) + count, n_pieces)):
             dst, cols = pieces[c]
+            from_z[c] = spread(lambda t, dst=dst, cols=cols: dst.at[t, x, :, cols])
+
+    def issue_own(count):
+        for c in range(len(own_x), min(len(own_x) + count, n_pieces if line else 0)):
+            dst, cols = pieces[c]
             block = dst.at[z, x, :, cols]
-            from_z[c] = over_z(lambda t, block=block: block, block)
+            own_x[c] = over_x(block, block)
 
     def forward(count):
         for c in range(len(from_x), min(len(from_x) + count, n_pieces)):
-            from_z[c].wait_recv()
+            if c >= len(own_x):
+                issue_own(1)
             dst, cols = pieces[c]
-            half = dst.at[:, x, :, cols]
-            from_x[c] = over_x(half, half)
+            if line:
+                from_x[c] = []
+                for k in range(nz - 1):
+                    t = from_z[c](k)
+                    block = dst.at[t, x, :, cols]
+                    from_x[c].append(over_x(block, block))
+            else:
+                from_z[c]()
+                half = dst.at[:, x, :, cols]
+                from_x[c] = [over_x(half, half)]
             issue_z(1)
+
+    def landed_x(c):
+        for transfer in from_x[c] + ([own_x[c]] if line else []):
+            transfer.wait_recv()
 
     cot_load = local(i.cotangent, sc.g_full.at[:, own_cols])
 
@@ -245,7 +379,7 @@
     value_part = tn(sc.basis[...], sc.wv[...])
     blk = CHUNK // nd
     for t in range(nd):
-        sc.bv_src[t] = value_part[t * blk : (t + 1) * blk]
+        sc.bv_src[t] = value_part[t * blk : (t + 1) * blk].astype(sc.bv_src.dtype)
     cot_load.wait()
     for copy in piece_loads:
         copy.wait()
@@ -318,9 +452,9 @@
         return transfer
 
     def summed(dst, count):
-        total = dst[0]
+        total = dst[0].astype(F32)
         for k in range(1, count):
-            total = total + dst[k]
+            total = total + dst[k].astype(F32)
         return total
 
     q_push = push(sc.q_src, sc.q_recv)
@@ -328,7 +462,6 @@
     sc.bv_recv[r] = sc.bv_src[r]
     g_gather = over_section(lambda t: sc.g_full.at[:, own_cols], sc.g_full.at[:, own_cols])
 
-    issue_z(2)
     q_push.wait_recv()
     query_proj = summed(sc.q_recv, nd)[0:1] + i.agg_bq[:, own_cols]
     sc.query_proj[...] = query_proj
@@ -339,9 +472,10 @@
     sc.s_src[...] = nn(key_query, sc.basis[...])[0:8]
     s_push = push(sc.s_src, sc.s_recv)
     bv_rs.wait_recv()
-    sc.bv_own[...] = summed(sc.bv_recv, nd)
+    sc.bv_own[...] = summed(sc.bv_recv, nd).astype(sc.bv_own.dtype)
     bv_ag = push(sc.bv_own, sc.bv_all)
-    issue_z(1)
+    issue_z(3)
+    issue_own(6)
 
     s_push.wait_recv()
     score_rows = summed(sc.s_recv, nd)
@@ -363,7 +497,7 @@
     forward(1)
     bv_ag.wait_recv()
     for t in range(nd):
-        sc.bv[t * blk : (t + 1) * blk] = sc.bv_all[t]
+        sc.bv[t * blk : (t + 1) * blk] = sc.bv_all[t].astype(F32)
     value_basis = sc.bv[...].astype(BF)
     head_of = iota((1, wl), 1) >> 6
     context = jnp.broadcast_to(i.agg_bv[:, own_cols], (tokens, wl))
@@ -373,9 +507,11 @@
     context_gather = over_section(lambda t: sc.context_full.at[:, own_cols], sc.context_full.at[:, own_cols])
     g_gather.wait_recv()
     transposed(sc.g_full, sc.gT)
+    issue_own(2)
     forward(1)
+    issue_own(1)
     context_gather.wait_recv()
-    from_x[0].wait_recv()
+    landed_x(0)
     part = nn(sc.context_full[...], weight(sc.awo_c)) + i.agg_bo[:, own_cols]
     sc.agg_full[:, own_cols] = part.astype(BF)
     agg_gather = over_section(lambda t: sc.agg_full.at[:, own_cols], sc.agg_full.at[:, own_cols])
@@ -388,7 +524,7 @@
     forward(1)
     normed = sc.normed[...]
     for j in range(3):
-        from_x[1 + j].wait_recv()
+        landed_x(1 + j)
         part = nn(normed, columns(sc.qkv_w, j))
         if j == 0:
             part = part + i.attn_bq[:, own_cols]
@@ -430,7 +566,7 @@
     forward(1)
     attended_gather.wait_recv()
     forward(1)
-    from_x[4].wait_recv()
+    landed_x(4)
     part = nn(sc.attended_full[...], weight(sc.two_c)) + i.attn_bo[:, own_cols]
     sc.mid_full[:, own_cols] = (part + sc.agg_full[:, own_cols].astype(F32)).astype(BF)
     mid_gather = over_section(lambda t: sc.mid_full.at[:, own_cols], sc.mid_full.at[:, own_cols])
@@ -447,7 +583,7 @@
     for j in range(fl // CHUNK):
         at = slice(j * CHUNK, (j + 1) * CHUNK)
         bias = i.mlp_bup[:, pl.ds(pl.multiple_of(s * fl + j * CHUNK, LANES), CHUNK)]
-        from_x[5 + j].wait_recv()
+        landed_x(5 + j)
         hidden = nn(mnormed, columns(sc.up_w, j)) + bias
         phi = 0.5 + 0.5 * lax.erf(hidden * 0.7071067811865476)
         density = jnp.exp(hidden * hidden * -0.5) * 0.3989422804014327
@@ -478,16 +614,36 @@
         sc.keep[c] = half(x)
 
     def issue_x(count):
-        for c in made[len(to_x) : len(to_x) + count]:
+        fresh = [c for c in made if c >= early and c not in to_x]
+        for c in fresh[:count]:
             to_x[c] = over_x(sc.x_send.at[c], sc.x_recv.at[c])
+
+    early = 2
+    merged = [early - 1]
+
+    def produce_early(c, left, right):
+        for side in range(nx):
+            part = nn(left[:, side].reshape(nz * rows, tokens), right)
+            sc.e_send[c, :, side] = part.reshape(nz, rows, CHUNK).astype(BF)
+        made.append(c)
+        to_z[c] = reduce(sc.e_send.at[c], sc.e_recv.at[c], sc.e_merged.at[c])
+
+    def middle_early(c):
+        sc.e_sum[c] = to_z[c].total()
+        sc.e_out[c] = sc.e_sum[c, 1 - x].astype(BF)
+        to_x[c] = over_x(sc.e_out.at[c], sc.e_in.at[c])
+
+    def finish_early(c):
+        to_x[c].wait_recv()
+        sc.final[c] = (sc.e_sum[c, x] + sc.e_in[c].astype(F32)).astype(BF)
+        publish(c, *names[c])
 
     def middle(c):
         to_x[c].wait_recv()
         if c >= 6:
             issue_x(1)
         sc.z_send[c] = (sc.keep[c] + sc.x_recv[c].astype(F32)).astype(BF)
-        to_z[c] = over_z(lambda t: sc.z_send.at[c, t], sc.z_recv.at[c, z])
-        sc.z_recv[c, z] = sc.z_send[c, z]
+        to_z[c] = reduce(sc.z_send.at[c], sc.z_recv.at[c], sc.z_merged.at[c])
 
     def publish(c, array, start):
         dst = array.at[:, pl.ds(pl.multiple_of(start, LANES), CHUNK)]
@@ -495,32 +651,43 @@
         out_copies.append(local(sc.final.at[c], dst))
 
     def finish(c):
-        to_z[c].wait_recv()
-        total = sc.z_recv[c, 0].astype(F32)
-        for k in range(1, nz):
-            total = total + sc.z_recv[c, k].astype(F32)
-        sc.final[c] = total.astype(BF)
+        sc.final[c] = to_z[c].total().astype(BF)
         publish(c, *names[c])
+
+    order = list(range(early, 8)) + list(range(early)) + list(range(8, len(names)))
 
     def pump(count):
         for _ in range(count):
             c = len(to_z)
             if c < len(names):
                 middle(c)
-            if len(done) < len(names) and (c == len(names) or len(done) < c - 1):
-                finish(len(done))
-                done.append(c)
+            if early < c <= len(names) and merged[-1] < c - 1:
+                merged.append(c - 1)
+                to_z[c - 1].merge()
+            if c == len(names) and merged[-1] < c - 1:
+                merged.append(c - 1)
+                to_z[c - 1].merge()
+            n = order[len(done)] if len(done) < len(names) else len(names)
+            if n < early:
+                finish_early(n)
+                done.append(n)
+            elif n < len(names) and (c == len(names) or n < c - 2):
+                finish(n)
+                done.append(n)
 
     for j in range(fl // CHUNK):
-        produce(j, sc.gT, sc.act[:, j * CHUNK : (j + 1) * CHUNK])
-    issue_x(4)
+        make_part = produce_early if j < early else produce
+        make_part(j, sc.gT, sc.act[:, j * CHUNK : (j + 1) * CHUNK])
+    issue_x(2)
     g_full = sc.g_full[...]
     nmlp = fl // CHUNK
     for j in range(fl // CHUNK):
         at = slice(j * CHUNK, (j + 1) * CHUNK)
-        from_x[5 + nmlp + j].wait_recv()
+        landed_x(5 + nmlp + j)
         d_hidden = nn(g_full, columns(sc.down_w, j)) * sc.slope[:, at]
         sc.d_hidden[:, at] = d_hidden.astype(BF)
+    for c in range(early):
+        to_z[c].merge()
     up_w = weight(sc.up_w)
     rs3 = scatter(sc.rs3_part, sc.rs3_recv, nt(sc.d_hidden[...], up_w))
     for j in range(nmlp):
@@ -536,6 +703,8 @@
     sc.vecs[3:4, :] = colsum(d_mid)
     ag3 = gather(sc.d_mid, d_mid)
     d_mid = d_mid.astype(F32)
+    for c in range(early):
+        middle_early(c)
     sc.out_part[...] = nt(sc.act[...], weight(sc.down_w))
     sc.out_part[own_rows, :] = sc.out_part[own_rows, :] + sc.mid_full[own_rows, :].astype(F32) + i.mlp_bdown[...]
     sc.out_low[...] = sc.out_part[...].astype(BF)
@@ -599,7 +768,7 @@
         grad_pix = grad_pix + srep * sc.score_rows[h : h + 1, :]
     key_push = push(sc.key_src, sc.key_recv)
     for t in range(nd):
-        sc.m_src[t] = cross[t * blk : (t + 1) * blk]
+        sc.m_src[t] = cross[t * blk : (t + 1) * blk].astype(sc.m_src.dtype)
     m_rs = over_dp(lambda t: sc.m_src.at[t], sc.m_recv.at[r])
     sc.m_recv[r] = sc.m_src[r]
     grad_pix = grad_pix.astype(BF)
@@ -619,7 +788,7 @@
     issue_x(1)
     pump(2)
     m_rs.wait_recv()
-    sc.m_own[...] = summed(sc.m_recv, nd)
+    sc.m_own[...] = summed(sc.m_recv, nd).astype(sc.m_own.dtype)
     m_ag = push(sc.m_own, sc.m_all)
     key_push.wait_recv()
     key_terms = summed(sc.key_recv, nd)
@@ -638,7 +807,7 @@
     pump(1)
     m_ag.wait_recv()
     for t in range(nd):
-        sc.cross[t * blk : (t + 1) * blk] = sc.m_all[t]
+        sc.cross[t * blk : (t + 1) * blk] = sc.m_all[t].astype(F32)
     cross = sc.cross[...].astype(BF)
     sc.final[count + 1] = nn(sc.basis[...], cross).astype(BF)
     publish(count + 1, o.agg_wv, s * wl)
@@ -704,10 +873,15 @@
         query_proj=v((1, wl), F32),
         key_query=v((16, rows), BF),
         score_rows=v((8, CHUNK), F32),
-        bv_own=v((blk, CHUNK), F32),
-        m_own=v((blk, CHUNK), F32),
         bv=v((CHUNK, CHUNK), F32),
         cross=v((CHUNK, CHUNK), F32),
+        e_send=v((2, nz, 2, rows, CHUNK), BF),
+        e_recv=v((2, nz, 2, rows, CHUNK), BF),
+        e_merged=v((2, 2, 2, rows, CHUNK), BF),
+        z_merged=v((chunks, 2, rows, CHUNK), BF),
+        e_sum=v((2, 2, rows, CHUNK), F32),
+        e_out=v((2, rows, CHUNK), BF),
+        e_in=v((2, rows, CHUNK), BF),
         probs=v((hl, tokens, LANES), F32),
         wrep=v((hl, tokens, CHUNK), BF),
         mixed=v((hl, tokens, CHUNK), BF),
@@ -757,9 +931,13 @@
     shapes.update(q_src=part, s_src=part, key_src=part, dq_src=part)
     part = v((nd, 8, CHUNK), F32)
     shapes.update(q_recv=part, s_recv=part, key_recv=part, dq_recv=part)
-    part = v((nd, blk, CHUNK), F32)
+    kind = BF if blk % 16 == 0 else F32
+    part = v((nd, blk, CHUNK), kind)
     shapes.update(bv_src=part, bv_recv=part, bv_all=part, m_src=part, m_recv=part, m_all=part)
-    count = 9 * nd + 24 * ns + 2 * chunks * (1 + nz) + chunks * ns
+    part = v((blk, CHUNK), kind)
+    shapes.update(bv_own=part, m_own=part)
+    spread, reduced = (8, 5) if nz == 4 else (nz, nz)
+    count = 9 * nd + 32 * ns + chunks * (spread + reduced + 6)
     dma = pltpu.SemaphoreType.DMA
     shapes.update(send=dma((count,)), recv=dma((count,)), local=dma((8 + 2 * chunks + 4,)))
     return shapes

time: 238 us -> 203 us (0.85)
  the two profiles are of different devices: /device:TPU:29 before, /device:TPU:0 now
where the time goes in v5:
time: 203 us
  Pallas kernels  202 us (100%)
    pallas_call x1, Pallas kernels, fused(): pl.pallas_call(body, out_shape=[jax.ShapeDtypeStruct(shape, kind) for sha...  194 us
    pallas_call x1, Pallas kernels, widen(): pl.pallas_call(body, grid=(rows // step,), out_shape=shaped, in_specs=[by...  7.2 us

profile of v5, /device:TPU:0, one launch (start us, length us, event | category | flops | bytes accessed | tf_op | source)
XLA Modules:
  0.0 202.5 jit_solution(1090740028233011660)
XLA Ops:
  0.7 194.4 %block.1 = (bf16[256,256]{1,0:T(8,128)(2,1)}, bf16[48,256]{1,0:T(8,128)(2,1)}, f32[256,128]{1,0:T(8,128)}, bf16[16,128]{1,0:T(8,128)(2,1)}, f32[4,8,256]{2,1,0:T...) custom-call(bf16[192,256]{1,0:T(8,128)(2,1)} %bitcast.31, ...), custom_call_target="tpu_custom_call" | custom-call | tf_op jit(solution)/shard_map/block/pallas_call | solution.py:979
  195.1 7.2 %widen.1 = (f32[128,4096]{1,0:T(8,128)}, f32[128,4096]{1,0:T(8,128)}, f32[128,3072]{1,0:T(8,128)}, f32[128,1024]{1,0:T(8,128)}, f32[128,1024]{1,0:T(8,128)}, /*i...) custom-call(bf16[128,4096]{1,0:T(8,128)(2,1)} %get-tuple-element.63., ...), custom_call_target="tpu_custom_call" | custom-call | tf_op jit(solution)/shard_map/widen/pallas_call | solution.py:1067

commit v6 on v5

--- a/solution.py
+++ b/solution.py
@@ -66,18 +66,18 @@
 
 
 class Transfer:
-    def __init__(self, make, low, high):
-        self.make, self.low, self.high = make, low, high
+    def __init__(self, make, low, high, whole):
+        self.make, self.low, self.high, self.whole = make, low, high, whole
 
     def start(self):
         each(self.low, self.high, lambda k: self.make(k).start())
         return self
 
     def wait_recv(self):
-        each(self.low, self.high, lambda k: self.make(k).wait_recv())
+        self.whole().wait_recv()
 
     def wait_send(self):
-        each(self.low, self.high, lambda k: self.make(k).wait_send())
+        self.whole().wait_send()
 
 
 def kernel(ns, nd, refs_in, refs_out, sc):
@@ -97,56 +97,81 @@
     own_rows = pl.ds(pl.multiple_of(s * shard, 16), shard)
     scale = HEAD ** (-0.5)
     send, recv = sc.send, sc.recv
-    used = {"n": 0}
+    used = SimpleNamespace(send=0, recv=0, local=0)
     pending = []
 
-    def sems(count):
-        base = used["n"]
-        used["n"] += count
-        return base
-
-    def remote(src, dst, sem, device, landing=None):
+    def send_sem():
+        used.send += 1
+        return used.send - 1
+
+    def recv_sem(count=1):
+        used.recv += count
+        return used.recv - count
+
+    def remote(src, dst, out, landing, device):
         return pltpu.make_async_remote_copy(
             src_ref=src,
             dst_ref=dst,
-            send_sem=send.at[sem],
-            recv_sem=recv.at[sem if landing is None else landing],
+            send_sem=send.at[out],
+            recv_sem=recv.at[landing],
             device_id=device,
             device_id_type=MESH,
         )
 
-    def over_section(src, dst):
-        base = sems(ns)
+    beside = (s, z * nx + 1 - x)
+
+    def await_sent(ref, out):
+        remote(ref, ref, out, 0, beside).wait_send()
+
+    def await_landed(ref, landing):
+        remote(ref, ref, 0, landing, beside).wait_recv()
+
+    def all_sent(ref, out):
+        pending.append(lambda: await_sent(ref, out))
+
+    def over(peer, count, src, dst, whole, out=None, landing=None):
+        alone = out is None
+        out = send_sem() if alone else out
+        landing = recv_sem() if landing is None else landing
 
         def make(k):
-            t = lax.rem(s + k, ns)
-            return remote(src(t), dst, base + k, (t, r))
-
-        transfer = Transfer(make, 1, ns).start()
-        pending.append(transfer)
+            t, device = peer(k)
+            return remote(src(t), dst, out, landing, device)
+
+        transfer = Transfer(make, 1, count, lambda: remote(whole, whole, out, landing, beside)).start()
+        if alone:
+            pending.append(transfer.wait_send)
         return transfer
 
-    def over_dp(src, dst):
-        base = sems(nd)
-
-        def make(k):
-            t = lax.rem(r + k, nd)
-            return remote(src(t), dst, base + k, (s, t))
-
-        transfer = Transfer(make, 1, nd).start()
-        pending.append(transfer)
-        return transfer
-
-    def over_z(src, dst):
-        base = sems(nz)
-
-        def make(k):
-            t = lax.rem(z + k, nz)
-            return remote(src(t), dst, base + k, (s, t * nx + x))
-
-        transfer = Transfer(make, 1, nz).start()
-        pending.append(transfer)
-        return transfer
+    def section_peer(k):
+        t = lax.rem(s + k, ns)
+        return t, (t, r)
+
+    def dp_peer(k):
+        t = lax.rem(r + k, nd)
+        return t, (s, t)
+
+    def z_peer(k):
+        t = lax.rem(z + k, nz)
+        return t, (s, t * nx + x)
+
+    def over_section(src, dst, whole):
+        return over(section_peer, ns, src, dst, whole)
+
+    def over_dp(src, dst, whole):
+        return over(dp_peer, nd, src, dst, whole)
+
+    def over_x(src, dst, out, landing=None, whole=None):
+        whole = src if whole is None else whole
+        return over(lambda k: (0, beside), 2, lambda t: src, dst, whole, out, landing)
+
+    def local(src, dst, sem):
+        copy = pltpu.make_async_copy(src, dst, sc.local.at[sem])
+        copy.start()
+        return copy
+
+    def await_local(ref, sem):
+        pltpu.make_async_copy(ref, ref, sc.local.at[sem]).wait()
 
     line = nz == 4
     partner = z + 1 - 2 * lax.rem(z, 2)
@@ -158,101 +183,104 @@
     def at_z(t):
         return (s, t * nx + x)
 
-    def line_spread(block):
-        base = sems(8)
-
-        def own(k):
-            to = at_z(partner if k == 0 else gate)
-            return remote(block(z), block(z), base + 4 + k, to, base + z)
-
-        def passed(j):
-            b = beyond[j]
-            return remote(block(b), block(b), base + 6 + j, at_z(partner), base + b)
-
-        for k in range(2):
-            own(k).start()
+    blocks = sc.z_recv
+    n_pieces = blocks.shape[0]
+    crossing = 2 if line else 0
+
+    def spread_group(count):
+        own, passed = send_sem(), send_sem()
+        whole = blocks.at[0:count, 0 : min(2, nz)] if line else blocks.at[0:count, 0 : nz - 1]
+        all_sent(whole, own)
+        if line:
+
+            def sent():
+                @pl.when(inner)
+                def _():
+                    await_sent(whole, passed)
+
+            pending.append(sent)
+        return own, passed
+
+    first_spread = spread_group(n_pieces)
+    second_spread = spread_group(crossing) if crossing else None
+
+    def line_spread(block, group):
+        base = recv_sem(3)
+        out, out_passed = group
+        mine_beyond = base + 1 + lax.rem(z, 2)
+        remote(block(z), block(z), out, base, at_z(partner)).start()
+        remote(block(z), block(z), out, mine_beyond, at_z(gate)).start()
 
         def arrived(k):
             t = [partner, *beyond][k]
-            remote(block(t), block(t), base + 4, at_z(partner), base + t).wait_recv()
+            await_landed(block(t), base + k)
             if k > 0:
 
                 @pl.when(inner)
                 def _():
-                    passed(k - 1).start()
+                    remote(block(t), block(t), out_passed, base + k, at_z(partner)).start()
 
             return t
 
-        def wait_send():
-            for k in range(2):
-                own(k).wait_send()
+        return arrived
+
+    def spread(block, group=first_spread):
+        if line:
+            return line_spread(block, group)
+        whole = blocks.at[0, 0 : nz - 1]
+        return over(z_peer, nz, lambda t: block(z), block(z), whole, group[0]).wait_recv
+
+    def reduce_group(count, landed):
+        near, far, across = send_sem(), send_sem(), send_sem()
+        if not line:
+            all_sent(landed.at[0:count, 0 : nz - 1], near)
+            return near, far, across
+        all_sent(landed.at[0:count, 0], near)
+
+        def sent():
+            @pl.when(outer)
+            def _():
+                await_sent(landed.at[0:count, 0:2], far)
 
             @pl.when(inner)
             def _():
-                for j in range(2):
-                    passed(j).wait_send()
-
-        pending.append(SimpleNamespace(wait_send=wait_send))
-        return arrived
-
-    def spread(block):
-        if line:
-            return line_spread(block)
-        return over_z(lambda t: block(z), block(z)).wait_recv
-
-    def line_reduce(parts, landed, merged):
-        base = sems(5)
-
-        def near():
-            return remote(parts.at[partner], landed.at[0], base, at_z(partner))
-
-        def far(j):
-            return remote(parts.at[beyond[j]], landed.at[2 + j], base + 1 + j, at_z(partner))
-
-        def across(j):
-            return remote(merged.at[j], landed.at[1], base + 3 + j, at_z(beyond[j]), base + 3)
-
-        near().start()
+                await_sent(landed.at[0:count, 0:2], across)
+
+        pending.append(sent)
+        return near, far, across
+
+    def line_reduce(parts, landed, merged, group):
+        near, far, across = group
+        base = recv_sem(3)
+        remote(parts.at[partner], landed.at[0], near, base, at_z(partner)).start()
 
         @pl.when(outer)
         def _():
             for j in range(2):
-                far(j).start()
+                remote(parts.at[beyond[j]], landed.at[2 + j], far, base + 1, at_z(partner)).start()
 
         def merge():
             @pl.when(inner)
             def _():
+                await_landed(landed.at[2:4], base + 1)
                 for j in range(2):
-                    far(j).wait_recv()
                     both = parts[beyond[j]].astype(F32) + landed[2 + j].astype(F32)
                     merged[j] = both.astype(BF)
-                    across(j).start()
+                    remote(merged.at[j], landed.at[1], across, base + 2, at_z(beyond[j])).start()
 
         def total():
-            near().wait_recv()
-            across(0).wait_recv()
+            await_landed(landed.at[0], base)
+            await_landed(landed.at[1], base + 2)
             return parts[z].astype(F32) + landed[0].astype(F32) + landed[1].astype(F32)
 
-        def wait_send():
-            near().wait_send()
-
-            @pl.when(outer)
-            def _():
-                for j in range(2):
-                    far(j).wait_send()
-
-            @pl.when(inner)
-            def _():
-                for j in range(2):
-                    across(j).wait_send()
-
-        pending.append(SimpleNamespace(wait_send=wait_send))
         return SimpleNamespace(merge=merge, total=total)
 
-    def reduce(parts, landed, merged):
+    def reduce(parts, landed, merged, group):
         if line:
-            return line_reduce(parts, landed, merged)
-        transfer = over_z(lambda t: parts.at[t], landed.at[z])
+            return line_reduce(parts, landed, merged, group)
+        transfer = over(
+            z_peer, nz, lambda t: parts.at[t], landed.at[z], landed.at[0 : nz - 1], group[0]
+        )
         landed[z] = parts[z]
 
         def total():
@@ -264,72 +292,66 @@
 
         return SimpleNamespace(merge=lambda: None, total=total)
 
-    def over_x(src, dst):
-        base = sems(1)
-        transfer = Transfer(lambda k: remote(src, dst, base, (s, z * nx + 1 - x)), 0, 1).start()
-        pending.append(transfer)
-        return transfer
-
-    local_used = {"n": 0}
-
-    def local(src, dst):
-        sem = local_used["n"]
-        local_used["n"] += 1
-        copy = pltpu.make_async_copy(src, dst, sc.local.at[sem])
-        copy.start()
-        return copy
-
-    small_loads = [
-        local(i.agg_wq.at[:, own_cols], sc.wq),
-        local(i.agg_wk.at[:, own_cols], sc.wk),
-        local(i.agg_wv.at[:, own_cols], sc.wv),
-    ]
+    local(i.agg_wq.at[:, own_cols], sc.wq, 0)
+    local(i.agg_wk.at[:, own_cols], sc.wk, 0)
+    local(i.agg_wv.at[:, own_cols], sc.wv, 0)
     sources = [(i.agg_wo, sc.awo_c, 0, s * wl)]
     sources += [(i.attn_wqkv, sc.qkv_w, j * wl, j * D + s * wl) for j in range(3)]
     sources += [(i.attn_wo, sc.two_c, 0, s * wl)]
     sources += [(i.mlp_up, sc.up_w, j * CHUNK, s * fl + j * CHUNK) for j in range(fl // CHUNK)]
     sources += [(i.mlp_down, sc.down_w, j * CHUNK, s * fl + j * CHUNK) for j in range(fl // CHUNK)]
     pieces = [(dst, pl.ds(at, CHUNK)) for _, dst, at, _ in sources]
-    piece_loads = [
-        local(src.at[:, pl.ds(pl.multiple_of(col, LANES), CHUNK)], dst.at[z, x, :, pl.ds(at, CHUNK)])
-        for src, dst, at, col in sources
-    ]
-    n_pieces = len(pieces)
+    for src, dst, at, col in sources:
+        local(src.at[:, pl.ds(pl.multiple_of(col, LANES), CHUNK)], dst.at[z, x, :, pl.ds(at, CHUNK)], 1)
     from_z, from_x, own_x = {}, {}, {}
+    late = range(n_pieces - crossing, n_pieces)
+    own_order = [*range(6), *late, *range(6, n_pieces - crossing)] if line else []
+    from_own, from_others = send_sem(), send_sem()
+    if line:
+        all_sent(blocks.at[:, 0], from_own)
+        all_sent(blocks.at[0 : n_pieces - crossing, 0 : nz - 1], from_others)
+    else:
+        all_sent(blocks, from_others)
+    x_landed = [recv_sem() for _ in range(n_pieces)]
+
+    def issue_own(count):
+        for c in own_order[len(own_x) : len(own_x) + count]:
+            dst, cols = pieces[c]
+            block = dst.at[z, x, :, cols]
+            own_x[c] = over_x(block, block, from_own, x_landed[c])
 
     def issue_z(count):
         for c in range(len(from_z), min(len(from_z) + count, n_pieces)):
             dst, cols = pieces[c]
-            from_z[c] = spread(lambda t, dst=dst, cols=cols: dst.at[t, x, :, cols])
-
-    def issue_own(count):
-        for c in range(len(own_x), min(len(own_x) + count, n_pieces if line else 0)):
-            dst, cols = pieces[c]
-            block = dst.at[z, x, :, cols]
-            own_x[c] = over_x(block, block)
+            from_z[c] = [spread(lambda t, dst=dst, cols=cols: dst.at[t, x, :, cols])]
+            if c in late:
+                own_x[c].wait_recv()
+                other = lambda t, dst=dst, cols=cols: dst.at[t, 1 - x, :, cols]
+                from_z[c].append(spread(other, second_spread))
 
     def forward(count):
         for c in range(len(from_x), min(len(from_x) + count, n_pieces)):
-            if c >= len(own_x):
+            while line and c not in own_x:
                 issue_own(1)
             dst, cols = pieces[c]
-            if line:
-                from_x[c] = []
-                for k in range(nz - 1):
-                    t = from_z[c](k)
-                    block = dst.at[t, x, :, cols]
-                    from_x[c].append(over_x(block, block))
-            else:
-                from_z[c]()
+            from_x[c] = True
+            if not line:
+                from_z[c][0]()
                 half = dst.at[:, x, :, cols]
-                from_x[c] = [over_x(half, half)]
+                over_x(half, half, from_others, x_landed[c])
+            for k in range(nz - 1 if line else 0):
+                for arrived in from_z[c]:
+                    block = dst.at[arrived(k), x, :, cols]
+                if c not in late:
+                    over_x(block, block, from_others, x_landed[c])
             issue_z(1)
 
     def landed_x(c):
-        for transfer in from_x[c] + ([own_x[c]] if line else []):
-            transfer.wait_recv()
-
-    cot_load = local(i.cotangent, sc.g_full.at[:, own_cols])
+        dst, cols = pieces[c]
+        if c not in late:
+            await_landed(dst.at[:, 0, :, cols], x_landed[c])
+
+    local(i.cotangent, sc.g_full.at[:, own_cols], 2)
 
     barrier = pltpu.get_barrier_semaphore()
     for k in range(1, ns):
@@ -373,16 +395,14 @@
     sc.vecs[...] = jnp.zeros_like(sc.vecs)
     sc.bup[...] = jnp.zeros_like(sc.bup)
 
-    for copy in small_loads:
-        copy.wait()
+    await_local(blocks.at[0:3, 0], 0)
     sc.q_src[...] = nn(query_rows, sc.wq[...])[0:8]
     value_part = tn(sc.basis[...], sc.wv[...])
     blk = CHUNK // nd
     for t in range(nd):
         sc.bv_src[t] = value_part[t * blk : (t + 1) * blk].astype(sc.bv_src.dtype)
-    cot_load.wait()
-    for copy in piece_loads:
-        copy.wait()
+    await_local(sc.g_full.at[:, own_cols], 2)
+    await_local(blocks.at[:, 0], 1)
 
     pl.semaphore_wait(barrier, ns - 1 + nd - 1)
 
@@ -391,13 +411,13 @@
 
     def scatter(part, landed, value):
         part[...] = value.astype(BF)
-        transfer = over_section(lambda t: part.at[pl.ds(pl.multiple_of(t * shard, 16), shard)], landed.at[s])
+        transfer = over_section(lambda t: part.at[pl.ds(pl.multiple_of(t * shard, 16), shard)], landed.at[s], landed.at[0 : ns - 1])
         landed[s] = part[own_rows, :]
         return transfer
 
     def gather(full, value):
         full[own_rows, :] = value.astype(BF)
-        return over_section(lambda t: full.at[own_rows], full.at[own_rows])
+        return over_section(lambda t: full.at[own_rows], full.at[own_rows], full.at[0 : (ns - 1) * shard])
 
     def landed_sum(landed):
         total = landed[0].astype(F32)
@@ -440,14 +460,18 @@
         at = pl.ds(s * zq, zq)
         dst[:, :, :, own_cols] = cols[at]
         return over_section(
-            lambda t: cols.at[pl.ds(t * zq, zq)], dst.at[:, :, :, own_cols]
+            lambda t: cols.at[pl.ds(t * zq, zq)], dst.at[:, :, :, own_cols], dst.at[:, :, :, 0 : (ns - 1) * wl]
         )
+
+    def gather_cols(full):
+        block = full.at[:, own_cols]
+        return over_section(lambda t: block, block, full.at[:, 0 : (ns - 1) * wl])
 
     def columns(ref, j):
         return ref[:, :, :, j * CHUNK : (j + 1) * CHUNK].reshape(D, CHUNK)
 
     def push(src, dst):
-        transfer = over_dp(lambda t: src, dst.at[r])
+        transfer = over_dp(lambda t: src, dst.at[r], dst.at[0 : nd - 1])
         dst[r] = src[...]
         return transfer
 
@@ -458,10 +482,11 @@
         return total
 
     q_push = push(sc.q_src, sc.q_recv)
-    bv_rs = over_dp(lambda t: sc.bv_src.at[t], sc.bv_recv.at[r])
+    bv_rs = over_dp(lambda t: sc.bv_src.at[t], sc.bv_recv.at[r], sc.bv_recv.at[0 : nd - 1])
     sc.bv_recv[r] = sc.bv_src[r]
-    g_gather = over_section(lambda t: sc.g_full.at[:, own_cols], sc.g_full.at[:, own_cols])
-
+    g_gather = gather_cols(sc.g_full)
+
+    issue_own(2)
     q_push.wait_recv()
     query_proj = summed(sc.q_recv, nd)[0:1] + i.agg_bq[:, own_cols]
     sc.query_proj[...] = query_proj
@@ -475,7 +500,7 @@
     sc.bv_own[...] = summed(sc.bv_recv, nd).astype(sc.bv_own.dtype)
     bv_ag = push(sc.bv_own, sc.bv_all)
     issue_z(3)
-    issue_own(6)
+    issue_own(4)
 
     s_push.wait_recv()
     score_rows = summed(sc.s_recv, nd)
@@ -504,7 +529,7 @@
     for h in range(hl):
         context = context + jnp.where(head_of == h, nn(sc.mixed[h], value_basis), 0.0)
     sc.context_full[:, own_cols] = context.astype(BF)
-    context_gather = over_section(lambda t: sc.context_full.at[:, own_cols], sc.context_full.at[:, own_cols])
+    context_gather = gather_cols(sc.context_full)
     g_gather.wait_recv()
     transposed(sc.g_full, sc.gT)
     issue_own(2)
@@ -514,7 +539,7 @@
     landed_x(0)
     part = nn(sc.context_full[...], weight(sc.awo_c)) + i.agg_bo[:, own_cols]
     sc.agg_full[:, own_cols] = part.astype(BF)
-    agg_gather = over_section(lambda t: sc.agg_full.at[:, own_cols], sc.agg_full.at[:, own_cols])
+    agg_gather = gather_cols(sc.agg_full)
     transposed(sc.context_full, sc.contextT)
     forward(1)
     agg_gather.wait_recv()
@@ -560,16 +585,14 @@
             nn(probs.astype(BF), v)
         ).astype(BF)
     sc.attended_full[:, own_cols] = sc.attended[...]
-    attended_gather = over_section(
-        lambda t: sc.attended_full.at[:, own_cols], sc.attended_full.at[:, own_cols]
-    )
+    attended_gather = gather_cols(sc.attended_full)
     forward(1)
     attended_gather.wait_recv()
     forward(1)
     landed_x(4)
     part = nn(sc.attended_full[...], weight(sc.two_c)) + i.attn_bo[:, own_cols]
     sc.mid_full[:, own_cols] = (part + sc.agg_full[:, own_cols].astype(F32)).astype(BF)
-    mid_gather = over_section(lambda t: sc.mid_full.at[:, own_cols], sc.mid_full.at[:, own_cols])
+    mid_gather = gather_cols(sc.mid_full)
     transposed(sc.attended_full, sc.attendedT)
     forward(1)
     mid_gather.wait_recv()
@@ -602,7 +625,13 @@
         + [(o.agg_wo, s * wl)]
     )
     to_x, to_z, made, done = {}, {}, [], []
-    out_copies, out_sends = [], []
+    published = [(send_sem(), recv_sem()) for _ in range(ns)]
+    early = 2
+    chunk_x, early_x = send_sem(), send_sem()
+    all_sent(blocks.at[early:], chunk_x)
+    all_sent(blocks.at[0:early, 0], early_x)
+    chunk_z = reduce_group(n_pieces - early, sc.z_recv)
+    early_z = reduce_group(early, sc.e_recv)
 
     def produce(c, left, right):
         def half(side):
@@ -616,9 +645,8 @@
     def issue_x(count):
         fresh = [c for c in made if c >= early and c not in to_x]
         for c in fresh[:count]:
-            to_x[c] = over_x(sc.x_send.at[c], sc.x_recv.at[c])
-
-    early = 2
+            to_x[c] = over_x(sc.x_send.at[c], sc.x_recv.at[c], chunk_x)
+
     merged = [early - 1]
 
     def produce_early(c, left, right):
@@ -626,12 +654,12 @@
             part = nn(left[:, side].reshape(nz * rows, tokens), right)
             sc.e_send[c, :, side] = part.reshape(nz, rows, CHUNK).astype(BF)
         made.append(c)
-        to_z[c] = reduce(sc.e_send.at[c], sc.e_recv.at[c], sc.e_merged.at[c])
+        to_z[c] = reduce(sc.e_send.at[c], sc.e_recv.at[c], sc.e_merged.at[c], early_z)
 
     def middle_early(c):
         sc.e_sum[c] = to_z[c].total()
         sc.e_out[c] = sc.e_sum[c, 1 - x].astype(BF)
-        to_x[c] = over_x(sc.e_out.at[c], sc.e_in.at[c])
+        to_x[c] = over_x(sc.e_out.at[c], sc.e_in.at[c], early_x)
 
     def finish_early(c):
         to_x[c].wait_recv()
@@ -640,40 +668,35 @@
 
     def middle(c):
         to_x[c].wait_recv()
-        if c >= 6:
-            issue_x(1)
+        issue_x(1)
         sc.z_send[c] = (sc.keep[c] + sc.x_recv[c].astype(F32)).astype(BF)
-        to_z[c] = reduce(sc.z_send.at[c], sc.z_recv.at[c], sc.z_merged.at[c])
+        to_z[c] = reduce(sc.z_send.at[c], sc.z_recv.at[c], sc.z_merged.at[c], chunk_z)
 
     def publish(c, array, start):
         dst = array.at[:, pl.ds(pl.multiple_of(start, LANES), CHUNK)]
-        out_sends.append(over_section(lambda t: sc.final.at[c], dst))
-        out_copies.append(local(sc.final.at[c], dst))
+        for k in range(1, ns):
+            remote(sc.final.at[c], dst, *published[k], section_peer(k)[1]).start()
+        local(sc.final.at[c], dst, 3)
 
     def finish(c):
         sc.final[c] = to_z[c].total().astype(BF)
         publish(c, *names[c])
 
-    order = list(range(early, 8)) + list(range(early)) + list(range(8, len(names)))
+    def finish_up_to(last):
+        for c in range(early, last + 1):
+            if c not in done:
+                finish(c)
+                done.append(c)
 
     def pump(count):
         for _ in range(count):
             c = len(to_z)
-            if c < len(names):
-                middle(c)
-            if early < c <= len(names) and merged[-1] < c - 1:
-                merged.append(c - 1)
+            middle(c)
+            if c > early:
                 to_z[c - 1].merge()
-            if c == len(names) and merged[-1] < c - 1:
-                merged.append(c - 1)
-                to_z[c - 1].merge()
-            n = order[len(done)] if len(done) < len(names) else len(names)
-            if n < early:
-                finish_early(n)
-                done.append(n)
-            elif n < len(names) and (c == len(names) or n < c - 2):
-                finish(n)
-                done.append(n)
+            if early + 3 <= c < 2 * early + 3:
+                finish_early(c - early - 3)
+            finish_up_to(c - 3)
 
     for j in range(fl // CHUNK):
         make_part = produce_early if j < early else produce
@@ -694,7 +717,7 @@
         at = slice(j * CHUNK, (j + 1) * CHUNK)
         produce(nmlp + j, sc.mnormedT, sc.d_hidden[:, at])
     sc.bup[:, own_ff] = colsum(sc.d_hidden[...])
-    issue_x(4)
+    issue_x(1)
     rs3.wait_recv()
     g_shard = sc.g_full[own_rows, :].astype(F32)
     sc.vecs[0:1, :] = colsum(g_shard)
@@ -709,7 +732,9 @@
     sc.out_part[own_rows, :] = sc.out_part[own_rows, :] + sc.mid_full[own_rows, :].astype(F32) + i.mlp_bdown[...]
     sc.out_low[...] = sc.out_part[...].astype(BF)
     out_rs = over_section(
-        lambda t: sc.out_low.at[:, pl.ds(pl.multiple_of(t * wl, LANES), wl)], sc.out_recv.at[s]
+        lambda t: sc.out_low.at[:, pl.ds(pl.multiple_of(t * wl, LANES), wl)],
+        sc.out_recv.at[s],
+        sc.out_recv.at[0 : ns - 1],
     )
     sc.out_recv[s] = sc.out_low[:, own_cols]
     pump(2)
@@ -769,20 +794,20 @@
     key_push = push(sc.key_src, sc.key_recv)
     for t in range(nd):
         sc.m_src[t] = cross[t * blk : (t + 1) * blk].astype(sc.m_src.dtype)
-    m_rs = over_dp(lambda t: sc.m_src.at[t], sc.m_recv.at[r])
+    m_rs = over_dp(lambda t: sc.m_src.at[t], sc.m_recv.at[r], sc.m_recv.at[0 : nd - 1])
     sc.m_recv[r] = sc.m_src[r]
     grad_pix = grad_pix.astype(BF)
     pw = CP // ns
     for t in range(ns):
         sc.pix_src[t] = nt(sc.place[t * pw : (t + 1) * pw, :], grad_pix).astype(BF)
-    pix_rs = over_section(lambda t: sc.pix_src.at[t], sc.pix_recv.at[s])
+    pix_rs = over_section(lambda t: sc.pix_src.at[t], sc.pix_recv.at[s], sc.pix_recv.at[0 : ns - 1])
     sc.pix_recv[s] = sc.pix_src[s]
     for t in range(nd):
         sc.small_src[t, 0:10] = sc.vecs[0:10, t * rows : (t + 1) * rows]
         for j in range(FF // D):
             start = (t * (FF // D) + j) * rows
             sc.small_src[t, 10 + j : 11 + j] = sc.bup[:, start : start + rows]
-    small_rs = over_dp(lambda t: sc.small_src.at[t], sc.small_recv.at[r])
+    small_rs = over_dp(lambda t: sc.small_src.at[t], sc.small_recv.at[r], sc.small_recv.at[0 : nd - 1])
     sc.small_recv[r] = sc.small_src[r]
 
     issue_x(1)
@@ -803,7 +828,7 @@
     pump(2)
     small_rs.wait_recv()
     sc.sec_small[s] = summed(sc.small_recv, nd)
-    small_ag = over_section(lambda t: sc.sec_small.at[s], sc.sec_small.at[s])
+    small_ag = over_section(lambda t: sc.sec_small.at[s], sc.sec_small.at[s], sc.sec_small.at[0 : ns - 1])
     pump(1)
     m_ag.wait_recv()
     for t in range(nd):
@@ -814,11 +839,12 @@
     key_low = jnp.concatenate([key_terms, jnp.zeros_like(key_terms)], axis=0).astype(BF)
     grad_basis = nt(cross, sc.wv[...]) + tn(key_low, sc.key_query[...])
     sc.basis_recv[s] = grad_basis.astype(BF)
-    basis_sum = over_section(lambda t: sc.basis_recv.at[s], sc.basis_recv.at[s])
-    pump(1)
+    basis_sum = over_section(lambda t: sc.basis_recv.at[s], sc.basis_recv.at[s], sc.basis_recv.at[0 : ns - 1])
+    finish_up_to(len(names) - 3)
+    to_z[len(names) - 1].merge()
     dq_push.wait_recv()
     o.d_query[s] = summed(sc.dq_recv, nd)
-    dq_gather = over_section(lambda t: o.d_query.at[s], o.d_query.at[s])
+    dq_gather = over_section(lambda t: o.d_query.at[s], o.d_query.at[s], o.d_query.at[0 : ns - 1])
 
     def section_total(ref):
         total = ref[0].astype(F32)
@@ -832,18 +858,17 @@
     o.patches[...] = section_total(sc.pix_recv).astype(BF)
     small_ag.wait_recv()
     o.small[...] = summed(sc.sec_small, ns)
-    pump(20)
+    finish_up_to(len(names) - 1)
     basis_sum.wait_recv()
     o.basis[...] = section_total(sc.basis_recv)
     dq_gather.wait_recv()
-    for transfer in out_sends:
-        transfer.wait_recv()
-    for copy in out_copies:
-        copy.wait()
-    for transfer in pending:
-        transfer.wait_send()
-    assert used["n"] <= send.shape[0], used["n"]
-    assert local_used["n"] <= sc.local.shape[0]
+    for k in range(1, ns):
+        await_landed(sc.final, published[k][1])
+        await_sent(sc.final, published[k][0])
+    await_local(sc.final, 3)
+    for wait in pending:
+        wait()
+    assert used.send <= send.shape[0] and used.recv <= recv.shape[0], used
 
 
 def scratch(ns, nd, tokens):
@@ -936,10 +961,8 @@
     shapes.update(bv_src=part, bv_recv=part, bv_all=part, m_src=part, m_recv=part, m_all=part)
     part = v((blk, CHUNK), kind)
     shapes.update(bv_own=part, m_own=part)
-    spread, reduced = (8, 5) if nz == 4 else (nz, nz)
-    count = 9 * nd + 32 * ns + chunks * (spread + reduced + 6)
     dma = pltpu.SemaphoreType.DMA
-    shapes.update(send=dma((count,)), recv=dma((count,)), local=dma((8 + 2 * chunks + 4,)))
+    shapes.update(send=dma((48,)), recv=dma((160,)), local=dma((4,)))
     return shapes
 
 

time: 203 us -> 191 us (0.941); the launches traced: 203 us -> 187 us
  Pallas kernels: 202 us -> 186 us
    pallas_call x1, Pallas kernels: 194 us -> 179 us  [fused(): pl.pallas_call(body, out_shape=[jax.ShapeDtypeStruct(shape, kind) for sha...]
where the time goes in v6:
time: 191 us; the launch traced here: 187 us
  Pallas kernels  186 us (97%)
    pallas_call x1, Pallas kernels, fused(): pl.pallas_call(body, out_shape=[jax.ShapeDtypeStruct(shape, kind) for sha...  179 us
    pallas_call x1, Pallas kernels, widen(): pl.pallas_call(body, grid=(rows // step,), out_shape=shaped, in_specs=[by...  7.2 us

profile of v6, /device:TPU:0, one launch (start us, length us, event | category | flops | bytes accessed | tf_op | source)
XLA Modules:
  0.0 186.9 jit_solution(8327906572873293816)
XLA Ops:
  0.7 178.9 %block.1 = (bf16[256,256]{1,0:T(8,128)(2,1)}, bf16[48,256]{1,0:T(8,128)(2,1)}, f32[256,128]{1,0:T(8,128)}, bf16[16,128]{1,0:T(8,128)(2,1)}, f32[4,8,256]{2,1,0:T...) custom-call(bf16[192,256]{1,0:T(8,128)(2,1)} %bitcast.31, ...), custom_call_target="tpu_custom_call" | custom-call | tf_op jit(solution)/shard_map/block/pallas_call | solution.py:1002
  179.6 7.2 %widen.1 = (f32[128,4096]{1,0:T(8,128)}, f32[128,4096]{1,0:T(8,128)}, f32[128,3072]{1,0:T(8,128)}, f32[128,1024]{1,0:T(8,128)}, f32[128,1024]{1,0:T(8,128)}, /*i...) custom-call(bf16[128,4096]{1,0:T(8,128)(2,1)} %get-tuple-element.63., ...), custom_call_target="tpu_custom_call" | custom-call | tf_op jit(solution)/shard_map/widen/pallas_call | solution.py:1090

commit v7 on v6

--- a/solution.py
+++ b/solution.py
@@ -249,15 +249,24 @@
         pending.append(sent)
         return near, far, across
 
-    def line_reduce(parts, landed, merged, group):
+    def line_reduce(parts, landed, merged, group, hold):
         near, far, across = group
         base = recv_sem(3)
-        remote(parts.at[partner], landed.at[0], near, base, at_z(partner)).start()
+
+        def first():
+            remote(parts.at[partner], landed.at[0], near, base, at_z(partner)).start()
+
+        def begin():
+            pl.when(inner)(first)
 
         @pl.when(outer)
         def _():
+            first()
             for j in range(2):
                 remote(parts.at[beyond[j]], landed.at[2 + j], far, base + 1, at_z(partner)).start()
+
+        if not hold:
+            begin()
 
         def merge():
             @pl.when(inner)
@@ -273,11 +282,11 @@
             await_landed(landed.at[1], base + 2)
             return parts[z].astype(F32) + landed[0].astype(F32) + landed[1].astype(F32)
 
-        return SimpleNamespace(merge=merge, total=total)
-
-    def reduce(parts, landed, merged, group):
+        return SimpleNamespace(begin=begin, merge=merge, total=total)
+
+    def reduce(parts, landed, merged, group, hold=False):
         if line:
-            return line_reduce(parts, landed, merged, group)
+            return line_reduce(parts, landed, merged, group, hold)
         transfer = over(
             z_peer, nz, lambda t: parts.at[t], landed.at[z], landed.at[0 : nz - 1], group[0]
         )
@@ -290,7 +299,7 @@
                 value = value + landed[k].astype(F32)
             return value
 
-        return SimpleNamespace(merge=lambda: None, total=total)
+        return SimpleNamespace(begin=lambda: None, merge=lambda: None, total=total)
 
     local(i.agg_wq.at[:, own_cols], sc.wq, 0)
     local(i.agg_wk.at[:, own_cols], sc.wk, 0)
@@ -487,6 +496,7 @@
     g_gather = gather_cols(sc.g_full)
 
     issue_own(2)
+    issue_z(1)
     q_push.wait_recv()
     query_proj = summed(sc.q_recv, nd)[0:1] + i.agg_bq[:, own_cols]
     sc.query_proj[...] = query_proj
@@ -499,7 +509,7 @@
     bv_rs.wait_recv()
     sc.bv_own[...] = summed(sc.bv_recv, nd).astype(sc.bv_own.dtype)
     bv_ag = push(sc.bv_own, sc.bv_all)
-    issue_z(3)
+    issue_z(2)
     issue_own(4)
 
     s_push.wait_recv()
@@ -616,14 +626,19 @@
             forward(1)
         if j == 2:
             forward(1)
-    forward(2)
-    names = (
-        [(o.mlp_down, s * fl + j * CHUNK) for j in range(fl // CHUNK)]
-        + [(o.mlp_up, s * fl + j * CHUNK) for j in range(fl // CHUNK)]
-        + [(o.attn_wo, s * wl)]
-        + [(o.attn_wqkv, j * D + s * wl) for j in range(3)]
-        + [(o.agg_wo, s * wl)]
-    )
+    names = [(o.mlp_down, lambda q, j=j: q * fl + j * CHUNK) for j in range(fl // CHUNK)]
+    names += [(o.mlp_up, lambda q, j=j: q * fl + j * CHUNK) for j in range(fl // CHUNK)]
+    names += [(o.attn_wo, lambda q: q * wl)]
+    names += [(o.attn_wqkv, lambda q, j=j: j * D + q * wl) for j in range(3)]
+    names += [(o.agg_wo, lambda q: q * wl)]
+    steps = [(c, 0, CHUNK) for c in range(n_pieces - 1)]
+    steps += [(n_pieces - 1, 0, CHUNK // 2), (n_pieces - 1, CHUNK // 2, CHUNK // 2)]
+    last = len(steps)
+
+    def view(ref, n):
+        c, at, width = steps[n]
+        return ref.at[c] if width == CHUNK else ref.at[c, :, :, pl.ds(at, width)]
+
     to_x, to_z, made, done = {}, {}, [], []
     published = [(send_sem(), recv_sem()) for _ in range(ns)]
     early = 2
@@ -639,13 +654,13 @@
             return nn(block, right).reshape(nz, rows, CHUNK)
 
         sc.x_send[c] = half(1 - x).astype(BF)
-        made.append(c)
+        made.extend(n for n in range(last) if steps[n][0] == c)
         sc.keep[c] = half(x)
 
     def issue_x(count):
         fresh = [c for c in made if c >= early and c not in to_x]
         for c in fresh[:count]:
-            to_x[c] = over_x(sc.x_send.at[c], sc.x_recv.at[c], chunk_x)
+            to_x[c] = over_x(view(sc.x_send, c), view(sc.x_recv, c), chunk_x)
 
     merged = [early - 1]
 
@@ -654,7 +669,7 @@
             part = nn(left[:, side].reshape(nz * rows, tokens), right)
             sc.e_send[c, :, side] = part.reshape(nz, rows, CHUNK).astype(BF)
         made.append(c)
-        to_z[c] = reduce(sc.e_send.at[c], sc.e_recv.at[c], sc.e_merged.at[c], early_z)
+        to_z[c] = reduce(sc.e_send.at[c], sc.e_recv.at[c], sc.e_merged.at[c], early_z, True)
 
     def middle_early(c):
         sc.e_sum[c] = to_z[c].total()
@@ -664,26 +679,47 @@
     def finish_early(c):
         to_x[c].wait_recv()
         sc.final[c] = (sc.e_sum[c, x] + sc.e_in[c].astype(F32)).astype(BF)
-        publish(c, *names[c])
-
-    def middle(c):
-        to_x[c].wait_recv()
-        issue_x(1)
-        sc.z_send[c] = (sc.keep[c] + sc.x_recv[c].astype(F32)).astype(BF)
-        to_z[c] = reduce(sc.z_send.at[c], sc.z_recv.at[c], sc.z_merged.at[c], chunk_z)
-
-    def publish(c, array, start):
-        dst = array.at[:, pl.ds(pl.multiple_of(start, LANES), CHUNK)]
-        for k in range(1, ns):
-            remote(sc.final.at[c], dst, *published[k], section_peer(k)[1]).start()
-        local(sc.final.at[c], dst, 3)
-
-    def finish(c):
-        sc.final[c] = to_z[c].total().astype(BF)
-        publish(c, *names[c])
-
-    def finish_up_to(last):
-        for c in range(early, last + 1):
+        publish(sc.final.at[c], *names[c])
+
+    def middle(n):
+        to_x[n].wait_recv()
+        issue_x({2: 2, 5: 0, 6: 0, 8: 2}.get(n, 1))
+        merged_x = view(sc.keep, n)[...] + view(sc.x_recv, n)[...].astype(F32)
+        view(sc.z_send, n)[...] = merged_x.astype(BF)
+        to_z[n] = reduce(view(sc.z_send, n), view(sc.z_recv, n), view(sc.z_merged, n), chunk_z)
+
+    mate = s + 1 - 2 * lax.rem(s, 2)
+    other = lax.rem(s + ns // 2, ns)
+    relayed = []
+
+    def publish(block, array, col, at=0, width=CHUNK):
+        def cols(q):
+            return array.at[:, pl.ds(pl.multiple_of(col(q) + at, LANES), width)]
+
+        (near, landed), (across, _), (passed, landed_passed) = published[0:3]
+        arrival = recv_sem()
+        remote(block, cols(s), near, landed, (mate, r)).start()
+        remote(block, cols(s), across, arrival, (other, r)).start()
+        local(block, cols(s), 3)
+
+        def relay():
+            await_landed(cols(other), arrival)
+            remote(cols(other), cols(other), passed, landed_passed, (mate, r)).start()
+
+        relayed.append(relay)
+
+    def relay_until(left):
+        while len(relayed) > left:
+            relayed.pop(0)()
+
+    def finish(n):
+        c, at, width = steps[n]
+        block = sc.final.at[c] if width == CHUNK else sc.final.at[c, :, pl.ds(at, width)]
+        block[...] = to_z[n].total().astype(BF)
+        publish(block, *names[c], at, width)
+
+    def finish_up_to(to):
+        for c in range(early, to + 1):
             if c not in done:
                 finish(c)
                 done.append(c)
@@ -692,16 +728,20 @@
         for _ in range(count):
             c = len(to_z)
             middle(c)
-            if c > early:
-                to_z[c - 1].merge()
-            if early + 3 <= c < 2 * early + 3:
-                finish_early(c - early - 3)
-            finish_up_to(c - 3)
+            if c > early + 1:
+                to_z[c - 2].merge()
+            if early + 6 <= c < 2 * early + 6:
+                finish_early(c - early - 6)
+            relay_until(1)
+            finish_up_to(c - 4)
 
     for j in range(fl // CHUNK):
         make_part = produce_early if j < early else produce
         make_part(j, sc.gT, sc.act[:, j * CHUNK : (j + 1) * CHUNK])
     issue_x(2)
+    forward(2)
+    for c in range(early):
+        to_z[c].begin()
     g_full = sc.g_full[...]
     nmlp = fl // CHUNK
     for j in range(fl // CHUNK):
@@ -709,15 +749,13 @@
         landed_x(5 + nmlp + j)
         d_hidden = nn(g_full, columns(sc.down_w, j)) * sc.slope[:, at]
         sc.d_hidden[:, at] = d_hidden.astype(BF)
-    for c in range(early):
-        to_z[c].merge()
     up_w = weight(sc.up_w)
     rs3 = scatter(sc.rs3_part, sc.rs3_recv, nt(sc.d_hidden[...], up_w))
     for j in range(nmlp):
         at = slice(j * CHUNK, (j + 1) * CHUNK)
         produce(nmlp + j, sc.mnormedT, sc.d_hidden[:, at])
     sc.bup[:, own_ff] = colsum(sc.d_hidden[...])
-    issue_x(1)
+    issue_x(2)
     rs3.wait_recv()
     g_shard = sc.g_full[own_rows, :].astype(F32)
     sc.vecs[0:1, :] = colsum(g_shard)
@@ -726,8 +764,6 @@
     sc.vecs[3:4, :] = colsum(d_mid)
     ag3 = gather(sc.d_mid, d_mid)
     d_mid = d_mid.astype(F32)
-    for c in range(early):
-        middle_early(c)
     sc.out_part[...] = nt(sc.act[...], weight(sc.down_w))
     sc.out_part[own_rows, :] = sc.out_part[own_rows, :] + sc.mid_full[own_rows, :].astype(F32) + i.mlp_bdown[...]
     sc.out_low[...] = sc.out_part[...].astype(BF)
@@ -737,10 +773,12 @@
         sc.out_recv.at[0 : ns - 1],
     )
     sc.out_recv[s] = sc.out_low[:, own_cols]
+    to_z[0].merge()
+    pump(1)
+    to_z[1].merge()
+    ag3.wait_recv()
+
     pump(2)
-    ag3.wait_recv()
-
-    pump(1)
     two_rows.wait_recv()
     d_att = nt(sc.d_mid[...], weight(sc.two)).astype(BF)
     sc.d_att[...] = d_att
@@ -761,12 +799,14 @@
         produce(2 * nmlp + 1 + j, sc.normedT, sc.d_qkv[:, j * wl : (j + 1) * wl])
     sc.vecs[7:8, own_cols] = colsum(sc.d_qkv[:, 0:wl])
     sc.vecs[8:9, own_cols] = colsum(sc.d_qkv[:, 2 * wl : 3 * wl])
+    middle_early(0)
     pump(1)
     rs4.wait_recv()
     d_agg = norm_back(landed_sum(sc.rs4_recv), i.attn_norm_gain, sc.hat1, sc.rstd1, 4, 5)
     d_agg = (sc.d_mid[own_rows, :].astype(F32) + d_agg).astype(BF)
     sc.vecs[6:7, :] = colsum(d_agg)
     ag4 = gather(sc.d_agg, d_agg)
+    middle_early(1)
     pump(2)
     ag4.wait_recv()
 
@@ -824,24 +864,27 @@
     dq_push = push(sc.dq_src, sc.dq_recv)
     count = len(names)
     sc.final[count] = (d_key * (sc.query_proj[...] * scale)).astype(BF)
-    publish(count, o.agg_wk, s * wl)
+    publish(sc.final.at[count], o.agg_wk, lambda q: q * wl)
     pump(2)
     small_rs.wait_recv()
     sc.sec_small[s] = summed(sc.small_recv, nd)
     small_ag = over_section(lambda t: sc.sec_small.at[s], sc.sec_small.at[s], sc.sec_small.at[0 : ns - 1])
-    pump(1)
+    pump(2)
     m_ag.wait_recv()
     for t in range(nd):
         sc.cross[t * blk : (t + 1) * blk] = sc.m_all[t].astype(F32)
     cross = sc.cross[...].astype(BF)
     sc.final[count + 1] = nn(sc.basis[...], cross).astype(BF)
-    publish(count + 1, o.agg_wv, s * wl)
+    publish(sc.final.at[count + 1], o.agg_wv, lambda q: q * wl)
     key_low = jnp.concatenate([key_terms, jnp.zeros_like(key_terms)], axis=0).astype(BF)
     grad_basis = nt(cross, sc.wv[...]) + tn(key_low, sc.key_query[...])
     sc.basis_recv[s] = grad_basis.astype(BF)
     basis_sum = over_section(lambda t: sc.basis_recv.at[s], sc.basis_recv.at[s], sc.basis_recv.at[0 : ns - 1])
-    finish_up_to(len(names) - 3)
-    to_z[len(names) - 1].merge()
+    to_z[last - 2].merge()
+    finish_up_to(last - 4)
+    relay_until(2)
+    to_z[last - 1].merge()
+    finish_up_to(last - 3)
     dq_push.wait_recv()
     o.d_query[s] = summed(sc.dq_recv, nd)
     dq_gather = over_section(lambda t: o.d_query.at[s], o.d_query.at[s], o.d_query.at[0 : ns - 1])
@@ -858,13 +901,16 @@
     o.patches[...] = section_total(sc.pix_recv).astype(BF)
     small_ag.wait_recv()
     o.small[...] = summed(sc.sec_small, ns)
-    finish_up_to(len(names) - 1)
+    finish_up_to(last - 1)
+    relay_until(2)
     basis_sum.wait_recv()
     o.basis[...] = section_total(sc.basis_recv)
     dq_gather.wait_recv()
-    for k in range(1, ns):
-        await_landed(sc.final, published[k][1])
-        await_sent(sc.final, published[k][0])
+    relay_until(0)
+    await_landed(sc.final, published[0][1])
+    await_landed(sc.final, published[2][1])
+    for out, _ in published[0:3]:
+        await_sent(sc.final, out)
     await_local(sc.final, 3)
     for wait in pending:
         wait()
@@ -962,7 +1008,7 @@
     part = v((blk, CHUNK), kind)
     shapes.update(bv_own=part, m_own=part)
     dma = pltpu.SemaphoreType.DMA
-    shapes.update(send=dma((48,)), recv=dma((160,)), local=dma((4,)))
+    shapes.update(send=dma((48,)), recv=dma((180,)), local=dma((4,)))
     return shapes
 
 
@@ -1015,7 +1061,7 @@
 
 def widen(nd, got, agg_wq):
     rows = D // nd
-    step = min(rows, 32)
+    step = min(rows, 64)
     big = dict(
         mlp_up=got.mlp_up,
         mlp_down=got.mlp_down,

time: 191 us -> 176 us (0.921); the launches traced: 187 us -> 175 us
  Pallas kernels: 186 us -> 175 us
    pallas_call x1, Pallas kernels: 179 us -> 168 us  [fused(): pl.pallas_call(body, out_shape=[jax.ShapeDtypeStruct(shape, kind) for sha...]
where the time goes in v7:
time: 176 us; the launch traced here: 175 us
  Pallas kernels  175 us (99%)
    pallas_call x1, Pallas kernels, fused(): pl.pallas_call(body, out_shape=[jax.ShapeDtypeStruct(shape, kind) for sha...  168 us
    pallas_call x1, Pallas kernels, widen(): pl.pallas_call(body, grid=(rows // step,), out_shape=shaped, in_specs=[by...  6.5 us

profile of v7, /device:TPU:0, one launch (start us, length us, event | category | flops | bytes accessed | tf_op | source)
XLA Modules:
  0.0 175.5 jit_solution(12003001785532512740)
XLA Ops:
  0.7 168.1 %block.1 = (bf16[256,256]{1,0:T(8,128)(2,1)}, bf16[48,256]{1,0:T(8,128)(2,1)}, f32[256,128]{1,0:T(8,128)}, bf16[16,128]{1,0:T(8,128)(2,1)}, f32[4,8,256]{2,1,0:T...) custom-call(bf16[192,256]{1,0:T(8,128)(2,1)} %bitcast.31, ...), custom_call_target="tpu_custom_call" | custom-call | tf_op jit(solution)/shard_map/block/pallas_call | solution.py:1048
  168.8 6.5 %widen.1 = (f32[128,4096]{1,0:T(8,128)}, f32[128,4096]{1,0:T(8,128)}, f32[128,3072]{1,0:T(8,128)}, f32[128,1024]{1,0:T(8,128)}, f32[128,1024]{1,0:T(8,128)}, /*i...) custom-call(bf16[128,4096]{1,0:T(8,128)(2,1)} %get-tuple-element.63., ...), custom_call_target="tpu_custom_call" | custom-call | tf_op jit(solution)/shard_map/widen/pallas_call | solution.py:1136

commit v8 on v7

--- a/solution.py
+++ b/solution.py
@@ -80,13 +80,14 @@
         self.whole().wait_send()
 
 
-def kernel(ns, nd, refs_in, refs_out, sc):
+def kernel(ns, nd, refs_in, refs_out, sc, near_names, near):
     s = lax.axis_index("section")
     r = lax.axis_index("dp")
     nx = 2
     nz = nd // nx
     z, x = lax.div(r, nx), lax.rem(r, nx)
-    i, o = refs_in, refs_out
+    o = refs_out
+    i = SimpleNamespace(**{**vars(refs_in), **dict(zip(near_names, near))})
     rows = D // nd
     tokens = i.patches.shape[1]
     shard = tokens // ns
@@ -211,17 +212,29 @@
         remote(block(z), block(z), out, base, at_z(partner)).start()
         remote(block(z), block(z), out, mine_beyond, at_z(gate)).start()
 
-        def arrived(k):
+        def pass_on(k):
+            t = beyond[k - 1]
+
+            @pl.when(inner)
+            def _():
+                await_landed(block(t), base + k)
+                remote(block(t), block(t), out_passed, base + k, at_z(partner)).start()
+
+        def arrived(k, passed=False):
             t = [partner, *beyond][k]
-            await_landed(block(t), base + k)
-            if k > 0:
-
-                @pl.when(inner)
-                def _():
-                    remote(block(t), block(t), out_passed, base + k, at_z(partner)).start()
+            if k == 0:
+                await_landed(block(t), base)
+                return t
+            if not passed:
+                pass_on(k)
+
+            @pl.when(outer)
+            def _():
+                await_landed(block(t), base + k)
 
             return t
 
+        arrived.pass_on = pass_on
         return arrived
 
     def spread(block, group=first_spread):
@@ -285,11 +298,10 @@
         return SimpleNamespace(begin=begin, merge=merge, total=total)
 
     def reduce(parts, landed, merged, group, hold=False):
-        if line:
+        if line and group is not None:
             return line_reduce(parts, landed, merged, group, hold)
-        transfer = over(
-            z_peer, nz, lambda t: parts.at[t], landed.at[z], landed.at[0 : nz - 1], group[0]
-        )
+        out = None if group is None else group[0]
+        transfer = over(z_peer, nz, lambda t: parts.at[t], landed.at[z], landed.at[0 : nz - 1], out)
         landed[z] = parts[z]
 
         def total():
@@ -300,6 +312,17 @@
             return value
 
         return SimpleNamespace(begin=lambda: None, merge=lambda: None, total=total)
+
+    barrier = pltpu.get_barrier_semaphore()
+    for k in range(1, ns):
+        pl.semaphore_signal(barrier, inc=1, device_id=(lax.rem(s + k, ns), r), device_id_type=MESH)
+    each(
+        1,
+        nd,
+        lambda k: pl.semaphore_signal(
+            barrier, inc=1, device_id=(s, lax.rem(r + k, nd)), device_id_type=MESH
+        ),
+    )
 
     local(i.agg_wq.at[:, own_cols], sc.wq, 0)
     local(i.agg_wk.at[:, own_cols], sc.wk, 0)
@@ -312,7 +335,16 @@
     pieces = [(dst, pl.ds(at, CHUNK)) for _, dst, at, _ in sources]
     for src, dst, at, col in sources:
         local(src.at[:, pl.ds(pl.multiple_of(col, LANES), CHUNK)], dst.at[z, x, :, pl.ds(at, CHUNK)], 1)
-    from_z, from_x, own_x = {}, {}, {}
+    from_z, from_x, own_x, early_passed = {}, {}, {}, set()
+
+    def pass_next():
+        c = max([-1, *early_passed, *from_x]) + 1
+        if line:
+            early_passed.add(c)
+            for k in range(1, nz - 1):
+                for arrived in from_z[c]:
+                    arrived.pass_on(k)
+
     late = range(n_pieces - crossing, n_pieces)
     own_order = [*range(6), *late, *range(6, n_pieces - crossing)] if line else []
     from_own, from_others = send_sem(), send_sem()
@@ -350,7 +382,8 @@
                 over_x(half, half, from_others, x_landed[c])
             for k in range(nz - 1 if line else 0):
                 for arrived in from_z[c]:
-                    block = dst.at[arrived(k), x, :, cols]
+                    t = arrived(k, c in early_passed)
+                    block = dst.at[t, x, :, cols]
                 if c not in late:
                     over_x(block, block, from_others, x_landed[c])
             issue_z(1)
@@ -362,16 +395,10 @@
 
     local(i.cotangent, sc.g_full.at[:, own_cols], 2)
 
-    barrier = pltpu.get_barrier_semaphore()
-    for k in range(1, ns):
-        pl.semaphore_signal(barrier, inc=1, device_id=(lax.rem(s + k, ns), r), device_id_type=MESH)
-    each(
-        1,
-        nd,
-        lambda k: pl.semaphore_signal(
-            barrier, inc=1, device_id=(s, lax.rem(r + k, nd)), device_id_type=MESH
-        ),
-    )
+    for n, name in enumerate(near_names):
+        local(getattr(refs_in, name), near[n], 10 + n)
+    for n, ref in enumerate(near):
+        await_local(ref, 10 + n)
 
     chan = (iota((CP, VARS), 0) >> 2 == iota((CP, VARS), 1)).astype(F32).astype(BF)
     ids = jnp.broadcast_to(i.var_ids[...].astype(F32), (CHUNK, VARS)).astype(BF)
@@ -400,12 +427,13 @@
     query = jnp.broadcast_to(i.agg_query[...].astype(BF).astype(F32), (16, D))
     query = jnp.where(iota((16, D), 0) == 0, query, 0.0).astype(BF)
     query_rows = nt(query, chosen).astype(BF)
-    o.query_rows[...] = query_rows
+    sc.query_rows[...] = query_rows
+    local(sc.query_rows, o.query_rows, 4)
     sc.vecs[...] = jnp.zeros_like(sc.vecs)
     sc.bup[...] = jnp.zeros_like(sc.bup)
 
     await_local(blocks.at[0:3, 0], 0)
-    sc.q_src[...] = nn(query_rows, sc.wq[...])[0:8]
+    sc.q_src[...] = nn(query_rows, sc.wq[...])[0:1]
     value_part = tn(sc.basis[...], sc.wv[...])
     blk = CHUNK // nd
     for t in range(nd):
@@ -495,10 +523,10 @@
     sc.bv_recv[r] = sc.bv_src[r]
     g_gather = gather_cols(sc.g_full)
 
-    issue_own(2)
+    issue_own(4)
     issue_z(1)
     q_push.wait_recv()
-    query_proj = summed(sc.q_recv, nd)[0:1] + i.agg_bq[:, own_cols]
+    query_proj = summed(sc.q_recv, nd) + i.agg_bq[:, own_cols]
     sc.query_proj[...] = query_proj
     head_rows = (iota((16, wl), 1) >> 6 == iota((16, wl), 0)).astype(F32)
     high, low = split(head_rows * (query_proj * scale))
@@ -509,8 +537,8 @@
     bv_rs.wait_recv()
     sc.bv_own[...] = summed(sc.bv_recv, nd).astype(sc.bv_own.dtype)
     bv_ag = push(sc.bv_own, sc.bv_all)
-    issue_z(2)
-    issue_own(4)
+    issue_z(4)
+    issue_own(2)
 
     s_push.wait_recv()
     score_rows = summed(sc.s_recv, nd)
@@ -528,8 +556,9 @@
         wrep = nt(probs.astype(BF), fold)
         sc.wrep[h] = wrep.astype(BF)
         sc.mixed[h] = (wrep * pix).astype(BF)
-    issue_z(2)
+    issue_z(1)
     forward(1)
+    issue_own(2)
     bv_ag.wait_recv()
     for t in range(nd):
         sc.bv[t * blk : (t + 1) * blk] = sc.bv_all[t].astype(F32)
@@ -546,16 +575,19 @@
     forward(1)
     issue_own(1)
     context_gather.wait_recv()
+    pass_next()
     landed_x(0)
     part = nn(sc.context_full[...], weight(sc.awo_c)) + i.agg_bo[:, own_cols]
     sc.agg_full[:, own_cols] = part.astype(BF)
     agg_gather = gather_cols(sc.agg_full)
     transposed(sc.context_full, sc.contextT)
     forward(1)
+    pass_next()
     agg_gather.wait_recv()
     whole_norm(sc.agg_full, i.attn_norm_gain, i.attn_norm_bias, sc.normed)
     kept_norm(sc.agg_full, sc.hat1, sc.rstd1)
     transposed(sc.normed, sc.normedT)
+    pass_next()
     forward(1)
     normed = sc.normed[...]
     for j in range(3):
@@ -566,6 +598,8 @@
         if j == 2:
             part = part + i.attn_bv[:, own_cols]
         sc.qkv[:, j * wl : (j + 1) * wl] = part.astype(BF)
+        if j < 2:
+            pass_next()
         if j == 1:
             forward(1)
     lo = (iota((1, LANES), 1) < HEAD).astype(F32)
@@ -597,21 +631,25 @@
     sc.attended_full[:, own_cols] = sc.attended[...]
     attended_gather = gather_cols(sc.attended_full)
     forward(1)
+    pass_next()
     attended_gather.wait_recv()
     forward(1)
+    pass_next()
     landed_x(4)
     part = nn(sc.attended_full[...], weight(sc.two_c)) + i.attn_bo[:, own_cols]
     sc.mid_full[:, own_cols] = (part + sc.agg_full[:, own_cols].astype(F32)).astype(BF)
     mid_gather = gather_cols(sc.mid_full)
     transposed(sc.attended_full, sc.attendedT)
     forward(1)
+    pass_next()
     mid_gather.wait_recv()
     awo_rows = by_rows(sc.awo_c, sc.awo)
     two_rows = by_rows(sc.two_c, sc.two)
     whole_norm(sc.mid_full, i.mlp_norm_gain, i.mlp_norm_bias, sc.mnormed)
     kept_norm(sc.mid_full, sc.hat2, sc.rstd2)
     transposed(sc.mnormed, sc.mnormedT)
-    forward(1)
+    pass_next()
+    forward(3)
     mnormed = sc.mnormed[...]
     for j in range(fl // CHUNK):
         at = slice(j * CHUNK, (j + 1) * CHUNK)
@@ -622,15 +660,13 @@
         density = jnp.exp(hidden * hidden * -0.5) * 0.3989422804014327
         sc.act[:, at] = (hidden * phi).astype(BF)
         sc.slope[:, at] = phi + hidden * density
-        if j == 0:
-            forward(1)
-        if j == 2:
-            forward(1)
+        if 0 < j <= crossing:
+            pass_next()
     names = [(o.mlp_down, lambda q, j=j: q * fl + j * CHUNK) for j in range(fl // CHUNK)]
     names += [(o.mlp_up, lambda q, j=j: q * fl + j * CHUNK) for j in range(fl // CHUNK)]
-    names += [(o.attn_wo, lambda q: q * wl)]
+    names += [(o.singles, lambda q: 3 * D + q * wl)]
     names += [(o.attn_wqkv, lambda q, j=j: j * D + q * wl) for j in range(3)]
-    names += [(o.agg_wo, lambda q: q * wl)]
+    names += [(o.singles, lambda q: 2 * D + q * wl)]
     steps = [(c, 0, CHUNK) for c in range(n_pieces - 1)]
     steps += [(n_pieces - 1, 0, CHUNK // 2), (n_pieces - 1, CHUNK // 2, CHUNK // 2)]
     last = len(steps)
@@ -645,7 +681,7 @@
     chunk_x, early_x = send_sem(), send_sem()
     all_sent(blocks.at[early:], chunk_x)
     all_sent(blocks.at[0:early, 0], early_x)
-    chunk_z = reduce_group(n_pieces - early, sc.z_recv)
+    chunk_z = reduce_group(n_pieces - early - 1, sc.z_recv)
     early_z = reduce_group(early, sc.e_recv)
 
     def produce(c, left, right):
@@ -657,12 +693,11 @@
         made.extend(n for n in range(last) if steps[n][0] == c)
         sc.keep[c] = half(x)
 
-    def issue_x(count):
-        fresh = [c for c in made if c >= early and c not in to_x]
-        for c in fresh[:count]:
+    def issue_x(until):
+        for c in [c for c in made if early <= c <= until and c not in to_x]:
             to_x[c] = over_x(view(sc.x_send, c), view(sc.x_recv, c), chunk_x)
 
-    merged = [early - 1]
+    unmerged = list(range(early, last))
 
     def produce_early(c, left, right):
         for side in range(nx):
@@ -683,10 +718,11 @@
 
     def middle(n):
         to_x[n].wait_recv()
-        issue_x({2: 2, 5: 0, 6: 0, 8: 2}.get(n, 1))
+        issue_x({2: 7, 5: 9, 8: 11}.get(n, 0))
         merged_x = view(sc.keep, n)[...] + view(sc.x_recv, n)[...].astype(F32)
         view(sc.z_send, n)[...] = merged_x.astype(BF)
-        to_z[n] = reduce(view(sc.z_send, n), view(sc.z_recv, n), view(sc.z_merged, n), chunk_z)
+        group = chunk_z if steps[n][2] == CHUNK else None
+        to_z[n] = reduce(view(sc.z_send, n), view(sc.z_recv, n), view(sc.z_merged, n), group)
 
     mate = s + 1 - 2 * lax.rem(s, 2)
     other = lax.rem(s + ns // 2, ns)
@@ -728,17 +764,19 @@
         for _ in range(count):
             c = len(to_z)
             middle(c)
-            if c > early + 1:
+            if c - 2 in unmerged:
+                unmerged.remove(c - 2)
                 to_z[c - 2].merge()
-            if early + 6 <= c < 2 * early + 6:
-                finish_early(c - early - 6)
+            if 8 <= c < last - 2 and c - 1 in unmerged:
+                unmerged.remove(c - 1)
+                to_z[c - 1].merge()
             relay_until(1)
-            finish_up_to(c - 4)
+            finish_up_to(c - (3 if c > 9 else 4))
 
     for j in range(fl // CHUNK):
         make_part = produce_early if j < early else produce
         make_part(j, sc.gT, sc.act[:, j * CHUNK : (j + 1) * CHUNK])
-    issue_x(2)
+    issue_x(3)
     forward(2)
     for c in range(early):
         to_z[c].begin()
@@ -755,7 +793,7 @@
         at = slice(j * CHUNK, (j + 1) * CHUNK)
         produce(nmlp + j, sc.mnormedT, sc.d_hidden[:, at])
     sc.bup[:, own_ff] = colsum(sc.d_hidden[...])
-    issue_x(2)
+    issue_x(5)
     rs3.wait_recv()
     g_shard = sc.g_full[own_rows, :].astype(F32)
     sc.vecs[0:1, :] = colsum(g_shard)
@@ -799,14 +837,13 @@
         produce(2 * nmlp + 1 + j, sc.normedT, sc.d_qkv[:, j * wl : (j + 1) * wl])
     sc.vecs[7:8, own_cols] = colsum(sc.d_qkv[:, 0:wl])
     sc.vecs[8:9, own_cols] = colsum(sc.d_qkv[:, 2 * wl : 3 * wl])
-    middle_early(0)
+    issue_x(8)
     pump(1)
     rs4.wait_recv()
     d_agg = norm_back(landed_sum(sc.rs4_recv), i.attn_norm_gain, sc.hat1, sc.rstd1, 4, 5)
     d_agg = (sc.d_mid[own_rows, :].astype(F32) + d_agg).astype(BF)
     sc.vecs[6:7, :] = colsum(d_agg)
     ag4 = gather(sc.d_agg, d_agg)
-    middle_early(1)
     pump(2)
     ag4.wait_recv()
 
@@ -850,7 +887,7 @@
     small_rs = over_dp(lambda t: sc.small_src.at[t], sc.small_recv.at[r], sc.small_recv.at[0 : nd - 1])
     sc.small_recv[r] = sc.small_src[r]
 
-    issue_x(1)
+    issue_x(10)
     pump(2)
     m_rs.wait_recv()
     sc.m_own[...] = summed(sc.m_recv, nd).astype(sc.m_own.dtype)
@@ -860,34 +897,32 @@
     wide = jnp.concatenate([jnp.broadcast_to(key_terms[h : h + 1], (HEAD, CHUNK)) for h in range(hl)], axis=0)
     d_key = nt(sc.basis[...], wide.astype(BF))
     d_query = jnp.sum(sc.wk[...].astype(F32) * d_key, axis=0, keepdims=True) * scale
-    sc.dq_src[...] = jnp.broadcast_to(d_query, sc.dq_src.shape)
+    sc.dq_src[...] = d_query
     dq_push = push(sc.dq_src, sc.dq_recv)
     count = len(names)
     sc.final[count] = (d_key * (sc.query_proj[...] * scale)).astype(BF)
-    publish(sc.final.at[count], o.agg_wk, lambda q: q * wl)
+    publish(sc.final.at[count], o.singles, lambda q: q * wl)
+    issue_x(last)
+    for c in range(early):
+        middle_early(c)
     pump(2)
     small_rs.wait_recv()
     sc.sec_small[s] = summed(sc.small_recv, nd)
     small_ag = over_section(lambda t: sc.sec_small.at[s], sc.sec_small.at[s], sc.sec_small.at[0 : ns - 1])
-    pump(2)
     m_ag.wait_recv()
     for t in range(nd):
         sc.cross[t * blk : (t + 1) * blk] = sc.m_all[t].astype(F32)
     cross = sc.cross[...].astype(BF)
     sc.final[count + 1] = nn(sc.basis[...], cross).astype(BF)
-    publish(sc.final.at[count + 1], o.agg_wv, lambda q: q * wl)
+    publish(sc.final.at[count + 1], o.singles, lambda q: 1 * D + q * wl)
     key_low = jnp.concatenate([key_terms, jnp.zeros_like(key_terms)], axis=0).astype(BF)
     grad_basis = nt(cross, sc.wv[...]) + tn(key_low, sc.key_query[...])
     sc.basis_recv[s] = grad_basis.astype(BF)
     basis_sum = over_section(lambda t: sc.basis_recv.at[s], sc.basis_recv.at[s], sc.basis_recv.at[0 : ns - 1])
-    to_z[last - 2].merge()
-    finish_up_to(last - 4)
-    relay_until(2)
-    to_z[last - 1].merge()
-    finish_up_to(last - 3)
     dq_push.wait_recv()
-    o.d_query[s] = summed(sc.dq_recv, nd)
-    dq_gather = over_section(lambda t: o.d_query.at[s], o.d_query.at[s], o.d_query.at[0 : ns - 1])
+    sc.d_query[...] = jnp.broadcast_to(summed(sc.dq_recv, nd), sc.d_query.shape)
+    dq_gather = over_section(lambda t: sc.d_query, o.d_query.at[s], o.d_query.at[0 : ns - 1])
+    local(sc.d_query, o.d_query.at[s], 5)
 
     def section_total(ref):
         total = ref[0].astype(F32)
@@ -895,16 +930,28 @@
             total = total + ref[k].astype(F32)
         return total
 
+    pump(2)
+    finish_up_to(last - 4)
+    to_z[last - 2].merge()
+    to_z[last - 1].merge()
+    for c in range(early):
+        finish_early(c)
+    finish_up_to(last - 3)
+    finish_up_to(last - 2)
+    finish_up_to(last - 1)
     out_rs.wait_recv()
-    o.activations[...] = section_total(sc.out_recv).astype(BF)
+    sc.activations[...] = section_total(sc.out_recv).astype(BF)
+    local(sc.activations, o.activations, 6)
     pix_rs.wait_recv()
-    o.patches[...] = section_total(sc.pix_recv).astype(BF)
+    sc.patches_out[...] = section_total(sc.pix_recv).astype(BF)
+    local(sc.patches_out, o.patches, 7)
     small_ag.wait_recv()
-    o.small[...] = summed(sc.sec_small, ns)
-    finish_up_to(last - 1)
+    sc.small_out[...] = summed(sc.sec_small, ns)
+    local(sc.small_out, o.small, 8)
     relay_until(2)
     basis_sum.wait_recv()
-    o.basis[...] = section_total(sc.basis_recv)
+    sc.basis_out[...] = section_total(sc.basis_recv)
+    local(sc.basis_out, o.basis, 9)
     dq_gather.wait_recv()
     relay_until(0)
     await_landed(sc.final, published[0][1])
@@ -912,6 +959,12 @@
     for out, _ in published[0:3]:
         await_sent(sc.final, out)
     await_local(sc.final, 3)
+    await_local(sc.query_rows, 4)
+    await_local(sc.d_query, 5)
+    await_local(sc.activations, 6)
+    await_local(sc.patches_out, 7)
+    await_local(sc.small_out, 8)
+    await_local(sc.basis_out, 9)
     for wait in pending:
         wait()
     assert used.send <= send.shape[0] and used.recv <= recv.shape[0], used
@@ -999,16 +1052,27 @@
     part = v((ns, shard, D), BF)
     shapes.update(rs3_recv=part, rs4_recv=part)
     part = v((8, CHUNK), F32)
-    shapes.update(q_src=part, s_src=part, key_src=part, dq_src=part)
+    shapes.update(s_src=part, key_src=part)
     part = v((nd, 8, CHUNK), F32)
-    shapes.update(q_recv=part, s_recv=part, key_recv=part, dq_recv=part)
+    shapes.update(s_recv=part, key_recv=part)
+    shapes.update(q_src=v((1, CHUNK), F32), dq_src=v((1, CHUNK), F32))
+    part = v((nd, 1, CHUNK), F32)
+    shapes.update(q_recv=part, dq_recv=part)
     kind = BF if blk % 16 == 0 else F32
     part = v((nd, blk, CHUNK), kind)
     shapes.update(bv_src=part, bv_recv=part, bv_all=part, m_src=part, m_recv=part, m_all=part)
     part = v((blk, CHUNK), kind)
     shapes.update(bv_own=part, m_own=part)
+    shapes.update(
+        query_rows=v((16, rows), BF),
+        d_query=v((8, wl), F32),
+        activations=v((tokens, wl), BF),
+        patches_out=v((CP // ns, tokens), BF),
+        small_out=v((16, rows), F32),
+        basis_out=v((CHUNK, rows), F32),
+    )
     dma = pltpu.SemaphoreType.DMA
-    shapes.update(send=dma((48,)), recv=dma((180,)), local=dma((4,)))
+    shapes.update(send=dma((48,)), recv=dma((180,)), local=dma((40,)))
     return shapes
 
 
@@ -1018,21 +1082,17 @@
     shapes = scratch(ns, nd, tokens)
     arrays = {**near, **far}
     hbm = pl.BlockSpec(memory_space=pl.ANY)
-    vmem = pl.BlockSpec(memory_space=pltpu.VMEM)
     outs = dict(
-        activations=((tokens, D // ns), BF, vmem),
-        patches=((CP // ns, tokens), BF, vmem),
-        basis=((CHUNK, rows), F32, vmem),
-        query_rows=((16, rows), BF, vmem),
-        d_query=((ns, 8, D // ns), F32, vmem),
-        small=((16, rows), F32, vmem),
-        mlp_up=((rows, FF), BF, hbm),
-        mlp_down=((rows, FF), BF, hbm),
-        attn_wqkv=((rows, 3 * D), BF, hbm),
-        attn_wo=((rows, D), BF, hbm),
-        agg_wo=((rows, D), BF, hbm),
-        agg_wv=((rows, D), BF, hbm),
-        agg_wk=((rows, D), BF, hbm),
+        activations=((tokens, D // ns), BF),
+        patches=((CP // ns, tokens), BF),
+        basis=((CHUNK, rows), F32),
+        query_rows=((16, rows), BF),
+        d_query=((ns, 8, D // ns), F32),
+        small=((16, rows), F32),
+        mlp_up=((rows, FF), BF),
+        mlp_down=((rows, FF), BF),
+        attn_wqkv=((rows, 3 * D), BF),
+        singles=((rows, 4 * D), BF),
     )
 
     def body(*refs):
@@ -1043,14 +1103,16 @@
             SimpleNamespace(**dict(zip(arrays, refs[:n_in]))),
             SimpleNamespace(**dict(zip(outs, refs[n_in : n_in + n_out]))),
             SimpleNamespace(**dict(zip(shapes, refs[n_in + n_out :]))),
+            list(near),
+            refs[n_in + n_out + len(shapes) :],
         )
 
     result = pl.pallas_call(
         body,
-        out_shape=[jax.ShapeDtypeStruct(shape, kind) for shape, kind, _ in outs.values()],
-        in_specs=[vmem] * len(near) + [hbm] * len(far),
-        out_specs=[spec for _, _, spec in outs.values()],
-        scratch_shapes=list(shapes.values()),
+        out_shape=[jax.ShapeDtypeStruct(*a) for a in outs.values()],
+        in_specs=[hbm] * len(arrays),
+        out_specs=[hbm] * len(outs),
+        scratch_shapes=list(shapes.values()) + [pltpu.VMEM(a.shape, a.dtype) for a in near.values()],
         compiler_params=pltpu.CompilerParams(
             collective_id=0, has_side_effects=True, vmem_limit_bytes=60 * 1024 * 1024
         ),
@@ -1061,16 +1123,7 @@
 
 def widen(nd, got, agg_wq):
     rows = D // nd
-    step = min(rows, 64)
-    big = dict(
-        mlp_up=got.mlp_up,
-        mlp_down=got.mlp_down,
-        attn_wqkv=got.attn_wqkv,
-        attn_wo=got.attn_wo,
-        agg_wo=got.agg_wo,
-        agg_wv=got.agg_wv,
-        agg_wk=got.agg_wk,
-    )
+    arrays = [got.mlp_up, got.mlp_down, got.attn_wqkv, got.singles]
     rest = dict(
         activations=got.activations,
         patches=got.patches,
@@ -1092,57 +1145,109 @@
         bup=((1, rows * (FF // D)), F32),
     )
     lines = tuple(range(10))
+    wide = dict(
+        mlp_up=((rows, FF), F32),
+        mlp_down=((rows, FF), F32),
+        attn_wqkv=((rows, 3 * D), F32),
+        agg_wk=((rows, D), F32),
+        agg_wv=((rows, D), F32),
+        agg_wo=((rows, D), F32),
+        attn_wo=((rows, D), F32),
+    )
+    half, third = FF // 2, 3 * D // 2
+    tiles = [(0, at, half, 0, at) for at in (0, half)]
+    tiles += [(1, at, half, 1, at) for at in (0, half)]
+    tiles += [(2, at, third, 2, at) for at in (0, third)]
+    tiles += [(3, n * D, D, 3 + n, 0) for n in range(4)]
+    everything = {**wide, **outs}
+    shaped = [jax.ShapeDtypeStruct(*a) for a in everything.values()]
+    shaped += [jax.ShapeDtypeStruct(line, F32) for _ in lines]
+    slim = shaped[len(wide) :]
 
     def body(*refs):
-        n = len(big)
-        for src, dst in zip(refs[:n], refs[n + len(rest) : 2 * n + len(rest)]):
-            dst[...] = src[...].astype(F32)
-        i = SimpleNamespace(**dict(zip(rest, refs[n : n + len(rest)])))
-        left = refs[2 * n + len(rest) :]
-        o = SimpleNamespace(**dict(zip(outs, left)))
-        left = left[len(outs) :]
+        sources, refs = refs[: len(arrays)], refs[len(arrays) :]
+        rest_in, refs = refs[: len(rest)], refs[len(rest) :]
+        targets, refs = refs[: len(wide)], refs[len(wide) :]
+        slim_out, refs = refs[: len(slim)], refs[len(slim) :]
+        near, refs = refs[: len(arrays)], refs[len(arrays) :]
+        far, refs = refs[: len(wide)], refs[len(wide) :]
+        rest_near, refs = refs[: len(rest)], refs[len(rest) :]
+        slim_near, (ins, outgoing) = refs[: len(slim)], refs[len(slim) :]
+
+        def load(t):
+            m, at, width, _, _ = tiles[t]
+            cols = pl.ds(at, width)
+            return pltpu.make_async_copy(sources[m].at[:, cols], near[m].at[:, cols], ins.at[t])
+
+        def store(t):
+            _, _, width, m, at = tiles[t]
+            cols = pl.ds(at, width)
+            return pltpu.make_async_copy(far[m].at[:, cols], targets[m].at[:, cols], outgoing.at[t])
+
+        def load_rest(n):
+            return pltpu.make_async_copy(rest_in[n], rest_near[n], ins.at[len(tiles) + n])
+
+        def store_slim(n):
+            return pltpu.make_async_copy(slim_near[n], slim_out[n], outgoing.at[len(tiles) + n])
+
+        def widen_tile(t):
+            load(t).wait()
+            m, at, width, to, start = tiles[t]
+            far[to][:, start : start + width] = near[m][:, at : at + width].astype(F32)
+            store(t).start()
+
+        for t in range(len(tiles)):
+            load(t).start()
+        for n in range(len(rest)):
+            load_rest(n).start()
+        for t in range(len(tiles) // 2):
+            widen_tile(t)
+        for n in range(len(rest)):
+            load_rest(n).wait()
+        i = SimpleNamespace(**dict(zip(rest, rest_near)))
+        o = SimpleNamespace(**dict(zip(outs, slim_near)))
+        left = slim_near[len(outs) :]
         r = lax.axis_index("dp")
-
-        @pl.when(pl.program_id(0) == 0)
-        def _():
-            o.activations[...] = i.activations[...]
-            o.patches[...] = i.patches[...]
-            o.embed[...] = i.basis[0:CP]
-            o.var[...] = i.basis[CP : CP + VARS]
-            d_query = jnp.concatenate([i.d_query[k] for k in range(i.d_query.shape[0])], axis=1)
-            d_query = jnp.concatenate([d_query, d_query], axis=0)
-            d_query = jnp.where(iota(d_query.shape, 0) == 0, d_query, 0.0)
-            high, low = split(d_query)
-            low, rest_low = split(d_query - high.astype(F32))
-            chosen = (iota((rows, D), 1) == iota((rows, D), 0) + r * rows).astype(F32).astype(BF)
-            o.bq[...] = (nt(high, chosen) + nt(low, chosen) + nt(rest_low, chosen))[0:1]
-            weight = i.agg_wq[...]
-            o.query[...] = (nt(high, weight) + nt(low, weight) + nt(rest_low, weight))[0:1]
-            first = i.query_rows[...]
-            o.wq[...] = tn(first, high) + tn(first, low) + tn(first, rest_low)
-            o.bup[...] = jnp.concatenate([i.small[10 + k : 11 + k] for k in range(FF // D)], axis=1)
-            for k in lines:
-                left[k][...] = i.small[k : k + 1]
-
-    def by_step(a):
-        return pl.BlockSpec((step, a.shape[1]), lambda g: (g, 0))
-
-    def fixed(shape):
-        return pl.BlockSpec(shape, lambda g: (0,) * len(shape))
-
-    shaped = [jax.ShapeDtypeStruct(a.shape, F32) for a in big.values()]
-    shaped += [jax.ShapeDtypeStruct(*a) for a in outs.values()]
-    shaped += [jax.ShapeDtypeStruct(line, F32) for _ in lines]
+        o.activations[...] = i.activations[...]
+        o.patches[...] = i.patches[...]
+        o.embed[...] = i.basis[0:CP]
+        o.var[...] = i.basis[CP : CP + VARS]
+        d_query = jnp.concatenate([i.d_query[k] for k in range(i.d_query.shape[0])], axis=1)
+        d_query = jnp.concatenate([d_query, d_query], axis=0)
+        d_query = jnp.where(iota(d_query.shape, 0) == 0, d_query, 0.0)
+        high, low = split(d_query)
+        low, rest_low = split(d_query - high.astype(F32))
+        chosen = (iota((rows, D), 1) == iota((rows, D), 0) + r * rows).astype(F32).astype(BF)
+        o.bq[...] = (nt(high, chosen) + nt(low, chosen) + nt(rest_low, chosen))[0:1]
+        weight = i.agg_wq[...]
+        o.query[...] = (nt(high, weight) + nt(low, weight) + nt(rest_low, weight))[0:1]
+        first = i.query_rows[...]
+        o.wq[...] = tn(first, high) + tn(first, low) + tn(first, rest_low)
+        o.bup[...] = jnp.concatenate([i.small[10 + k : 11 + k] for k in range(FF // D)], axis=1)
+        for k in lines:
+            left[k][...] = i.small[k : k + 1]
+        for n in range(len(slim)):
+            store_slim(n).start()
+        for t in range(len(tiles) // 2, len(tiles)):
+            widen_tile(t)
+        for t in range(len(tiles)):
+            store(t).wait()
+        for n in range(len(slim)):
+            store_slim(n).wait()
+
+    hbm = pl.BlockSpec(memory_space=pl.ANY)
+    dma = pltpu.SemaphoreType.DMA
     result = pl.pallas_call(
         body,
-        grid=(rows // step,),
         out_shape=shaped,
-        in_specs=[by_step(a) for a in big.values()] + [fixed(a.shape) for a in rest.values()],
-        out_specs=[by_step(a) for a in big.values()] + [fixed(a.shape) for a in shaped[len(big) :]],
+        in_specs=[hbm] * (len(arrays) + len(rest)),
+        out_specs=[hbm] * len(shaped),
+        scratch_shapes=[pltpu.VMEM(a.shape, a.dtype) for a in [*arrays, *shaped[: len(wide)], *rest.values(), *slim]]
+        + [dma((len(tiles) + len(rest),)), dma((len(tiles) + len(slim),))],
         compiler_params=pltpu.CompilerParams(vmem_limit_bytes=60 * 1024 * 1024),
         name="widen",
-    )(*big.values(), *rest.values())
-    names = list(big) + list(outs)
+    )(*arrays, *rest.values())
+    names = list(everything)
     return SimpleNamespace(**dict(zip(names, result))), [a.reshape(-1) for a in result[len(names) :]]
 
 

time: 176 us -> 167 us (0.949)
  Pallas kernels: 175 us -> 166 us
    pallas_call x2, Pallas kernels: 175 us -> 166 us  [the longest x1 160 us: fused(): pl.pallas_call(body, out_shape=[jax.ShapeDtypeStruct(*a) for a in outs.va...]
where the time goes in v8:
time: 167 us; the launch traced here: 166 us
  Pallas kernels  166 us (99%)
    pallas_call x1, Pallas kernels, fused(): pl.pallas_call(body, out_shape=[jax.ShapeDtypeStruct(*a) for a in outs.va...  160 us
    pallas_call x1, Pallas kernels, widen(): pl.pallas_call(body, out_shape=shaped, in_specs=[hbm] * (len(arrays) + le...  5.84 us

profile of v8, /device:TPU:0, one launch (start us, length us, event | category | flops | bytes accessed | tf_op | source)
XLA Modules:
  0.0 166.5 jit_solution(10353060788794617161)
XLA Ops:
  0.7 159.8 %block.1 = (bf16[256,256]{1,0:T(8,128)(2,1)}, bf16[48,256]{1,0:T(8,128)(2,1)}, f32[256,128]{1,0:T(8,128)}, bf16[16,128]{1,0:T(8,128)(2,1)}, f32[4,8,256]{2,1,0:T...) custom-call(bf16[192,256]{1,0:T(8,128)(2,1)} %bitcast.31, ...), custom_call_target="tpu_custom_call" | custom-call | tf_op jit(solution)/shard_map/block/pallas_call | solution.py:1110
  160.5 5.8 %widen.1 = (f32[128,4096]{1,0:T(8,128)}, f32[128,4096]{1,0:T(8,128)}, f32[128,3072]{1,0:T(8,128)}, f32[128,1024]{1,0:T(8,128)}, f32[128,1024]{1,0:T(8,128)}, /*i...) custom-call(bf16[128,4096]{1,0:T(8,128)(2,1)} %get-tuple-element.60., ...), custom_call_target="tpu_custom_call" | custom-call | tf_op jit(solution)/shard_map/widen/pallas_call | solution.py:1240

commit v9 on v8

--- a/solution.py
+++ b/solution.py
@@ -532,13 +532,14 @@
     high, low = split(head_rows * (query_proj * scale))
     key_query = (nt(high, sc.wk[...]) + nt(low, sc.wk[...])).astype(BF)
     sc.key_query[...] = key_query
-    sc.s_src[...] = nn(key_query, sc.basis[...])[0:8]
+    sc.s_src[...] = nn(key_query, sc.basis[...])[0:hl]
     s_push = push(sc.s_src, sc.s_recv)
     bv_rs.wait_recv()
     sc.bv_own[...] = summed(sc.bv_recv, nd).astype(sc.bv_own.dtype)
     bv_ag = push(sc.bv_own, sc.bv_all)
     issue_z(4)
-    issue_own(2)
+    issue_own(4)
+    pass_next()
 
     s_push.wait_recv()
     score_rows = summed(sc.s_recv, nd)
@@ -559,6 +560,7 @@
     issue_z(1)
     forward(1)
     issue_own(2)
+    pass_next()
     bv_ag.wait_recv()
     for t in range(nd):
         sc.bv[t * blk : (t + 1) * blk] = sc.bv_all[t].astype(F32)
@@ -667,8 +669,9 @@
     names += [(o.singles, lambda q: 3 * D + q * wl)]
     names += [(o.attn_wqkv, lambda q, j=j: j * D + q * wl) for j in range(3)]
     names += [(o.singles, lambda q: 2 * D + q * wl)]
-    steps = [(c, 0, CHUNK) for c in range(n_pieces - 1)]
-    steps += [(n_pieces - 1, 0, CHUNK // 2), (n_pieces - 1, CHUNK // 2, CHUNK // 2)]
+    halved = 2
+    steps = [(c, 0, CHUNK) for c in range(n_pieces - halved)]
+    steps += [(c, at, CHUNK // 2) for c in range(n_pieces - halved, n_pieces) for at in (0, CHUNK // 2)]
     last = len(steps)
 
     def view(ref, n):
@@ -681,7 +684,7 @@
     chunk_x, early_x = send_sem(), send_sem()
     all_sent(blocks.at[early:], chunk_x)
     all_sent(blocks.at[0:early, 0], early_x)
-    chunk_z = reduce_group(n_pieces - early - 1, sc.z_recv)
+    chunk_z = reduce_group(n_pieces - early - halved, sc.z_recv)
     early_z = reduce_group(early, sc.e_recv)
 
     def produce(c, left, right):
@@ -718,7 +721,7 @@
 
     def middle(n):
         to_x[n].wait_recv()
-        issue_x({2: 7, 5: 9, 8: 11}.get(n, 0))
+        issue_x({2: 7, 5: 9, 8: 12}.get(n, 0))
         merged_x = view(sc.keep, n)[...] + view(sc.x_recv, n)[...].astype(F32)
         view(sc.z_send, n)[...] = merged_x.astype(BF)
         group = chunk_z if steps[n][2] == CHUNK else None
@@ -767,11 +770,11 @@
             if c - 2 in unmerged:
                 unmerged.remove(c - 2)
                 to_z[c - 2].merge()
-            if 8 <= c < last - 2 and c - 1 in unmerged:
+            if c >= 8 and c - 1 in unmerged:
                 unmerged.remove(c - 1)
                 to_z[c - 1].merge()
             relay_until(1)
-            finish_up_to(c - (3 if c > 9 else 4))
+            finish_up_to(min(c - (3 if c > 9 else 4), last - 2 * halved - 1))
 
     for j in range(fl // CHUNK):
         make_part = produce_early if j < early else produce
@@ -854,7 +857,6 @@
     value_basis = sc.bv[...].astype(BF)
     cross = jnp.zeros((CHUNK, wl), F32)
     grad_pix = jnp.zeros((tokens, CHUNK), F32)
-    sc.key_src[...] = jnp.zeros_like(sc.key_src)
     for h in range(hl):
         masked = d_context * (head_of == h).astype(F32).astype(BF)
         pulled = nt(masked, value_basis)
@@ -915,7 +917,7 @@
     cross = sc.cross[...].astype(BF)
     sc.final[count + 1] = nn(sc.basis[...], cross).astype(BF)
     publish(sc.final.at[count + 1], o.singles, lambda q: 1 * D + q * wl)
-    key_low = jnp.concatenate([key_terms, jnp.zeros_like(key_terms)], axis=0).astype(BF)
+    key_low = jnp.concatenate([key_terms, jnp.zeros((16 - hl, CHUNK), F32)], axis=0).astype(BF)
     grad_basis = nt(cross, sc.wv[...]) + tn(key_low, sc.key_query[...])
     sc.basis_recv[s] = grad_basis.astype(BF)
     basis_sum = over_section(lambda t: sc.basis_recv.at[s], sc.basis_recv.at[s], sc.basis_recv.at[0 : ns - 1])
@@ -930,10 +932,8 @@
             total = total + ref[k].astype(F32)
         return total
 
-    pump(2)
-    finish_up_to(last - 4)
-    to_z[last - 2].merge()
-    to_z[last - 1].merge()
+    pump(3)
+    finish_up_to(last - 2 * halved)
     for c in range(early):
         finish_early(c)
     finish_up_to(last - 3)
@@ -996,7 +996,7 @@
         bup=v((1, FF), F32),
         query_proj=v((1, wl), F32),
         key_query=v((16, rows), BF),
-        score_rows=v((8, CHUNK), F32),
+        score_rows=v((hl, CHUNK), F32),
         bv=v((CHUNK, CHUNK), F32),
         cross=v((CHUNK, CHUNK), F32),
         e_send=v((2, nz, 2, rows, CHUNK), BF),
@@ -1051,9 +1051,9 @@
     shapes.update(rs3_part=part, rs4_part=part)
     part = v((ns, shard, D), BF)
     shapes.update(rs3_recv=part, rs4_recv=part)
-    part = v((8, CHUNK), F32)
+    part = v((hl, CHUNK), F32)
     shapes.update(s_src=part, key_src=part)
-    part = v((nd, 8, CHUNK), F32)
+    part = v((nd, hl, CHUNK), F32)
     shapes.update(s_recv=part, key_recv=part)
     shapes.update(q_src=v((1, CHUNK), F32), dq_src=v((1, CHUNK), F32))
     part = v((nd, 1, CHUNK), F32)
@@ -1072,7 +1072,7 @@
         basis_out=v((CHUNK, rows), F32),
     )
     dma = pltpu.SemaphoreType.DMA
-    shapes.update(send=dma((48,)), recv=dma((180,)), local=dma((40,)))
+    shapes.update(send=dma((52,)), recv=dma((160,)), local=dma((28,)))
     return shapes
 
 
@@ -1196,12 +1196,10 @@
             far[to][:, start : start + width] = near[m][:, at : at + width].astype(F32)
             store(t).start()
 
+        for n in range(len(rest)):
+            load_rest(n).start()
         for t in range(len(tiles)):
             load(t).start()
-        for n in range(len(rest)):
-            load_rest(n).start()
-        for t in range(len(tiles) // 2):
-            widen_tile(t)
         for n in range(len(rest)):
             load_rest(n).wait()
         i = SimpleNamespace(**dict(zip(rest, rest_near)))
@@ -1228,7 +1226,7 @@
             left[k][...] = i.small[k : k + 1]
         for n in range(len(slim)):
             store_slim(n).start()
-        for t in range(len(tiles) // 2, len(tiles)):
+        for t in range(len(tiles)):
             widen_tile(t)
         for t in range(len(tiles)):
             store(t).wait()

time: 167 us -> 162 us (0.970)
  Pallas kernels: 166 us -> 161 us
    pallas_call x1, Pallas kernels: 160 us -> 155 us  [fused(): pl.pallas_call(body, out_shape=[jax.ShapeDtypeStruct(*a) for a in outs.va...]
where the time goes in v9:
time: 162 us
  Pallas kernels  161 us (99%)
    pallas_call x1, Pallas kernels, fused(): pl.pallas_call(body, out_shape=[jax.ShapeDtypeStruct(*a) for a in outs.va...  155 us
    pallas_call x1, Pallas kernels, widen(): pl.pallas_call(body, out_shape=shaped, in_specs=[hbm] * (len(arrays) + le...  5.7 us

profile of v9, /device:TPU:0, one launch (start us, length us, event | category | flops | bytes accessed | tf_op | source)
XLA Modules:
  0.0 162.0 jit_solution(5968951004772476702)
XLA Ops:
  0.7 155.5 %block.1 = (bf16[256,256]{1,0:T(8,128)(2,1)}, bf16[48,256]{1,0:T(8,128)(2,1)}, f32[256,128]{1,0:T(8,128)}, bf16[16,128]{1,0:T(8,128)(2,1)}, f32[4,8,256]{2,1,0:T...) custom-call(bf16[192,256]{1,0:T(8,128)(2,1)} %bitcast.31, ...), custom_call_target="tpu_custom_call" | custom-call | tf_op jit(solution)/shard_map/block/pallas_call | solution.py:1110
  156.2 5.7 %widen.1 = (f32[128,4096]{1,0:T(8,128)}, f32[128,4096]{1,0:T(8,128)}, f32[128,3072]{1,0:T(8,128)}, f32[128,1024]{1,0:T(8,128)}, f32[128,1024]{1,0:T(8,128)}, /*i...) custom-call(bf16[128,4096]{1,0:T(8,128)(2,1)} %get-tuple-element.60., ...), custom_call_target="tpu_custom_call" | custom-call | tf_op jit(solution)/shard_map/widen/pallas_call | solution.py:1238

commit v10 on v9

--- a/solution.py
+++ b/solution.py
@@ -911,6 +911,13 @@
     small_rs.wait_recv()
     sc.sec_small[s] = summed(sc.small_recv, nd)
     small_ag = over_section(lambda t: sc.sec_small.at[s], sc.sec_small.at[s], sc.sec_small.at[0 : ns - 1])
+    def section_total(ref):
+        total = ref[0].astype(F32)
+        for k in range(1, ns):
+            total = total + ref[k].astype(F32)
+        return total
+
+    pump(1)
     m_ag.wait_recv()
     for t in range(nd):
         sc.cross[t * blk : (t + 1) * blk] = sc.m_all[t].astype(F32)
@@ -926,13 +933,7 @@
     dq_gather = over_section(lambda t: sc.d_query, o.d_query.at[s], o.d_query.at[0 : ns - 1])
     local(sc.d_query, o.d_query.at[s], 5)
 
-    def section_total(ref):
-        total = ref[0].astype(F32)
-        for k in range(1, ns):
-            total = total + ref[k].astype(F32)
-        return total
-
-    pump(3)
+    pump(2)
     finish_up_to(last - 2 * halved)
     for c in range(early):
         finish_early(c)
@@ -1200,6 +1201,8 @@
             load_rest(n).start()
         for t in range(len(tiles)):
             load(t).start()
+        for t in range(len(tiles) // 2):
+            widen_tile(t)
         for n in range(len(rest)):
             load_rest(n).wait()
         i = SimpleNamespace(**dict(zip(rest, rest_near)))
@@ -1226,7 +1229,7 @@
             left[k][...] = i.small[k : k + 1]
         for n in range(len(slim)):
             store_slim(n).start()
-        for t in range(len(tiles)):
+        for t in range(len(tiles) // 2, len(tiles)):
             widen_tile(t)
         for t in range(len(tiles)):
             store(t).wait()

time: 162 us -> 162 us (level)
  no operation moved by 1% of the time
where the time goes in v10:
time: 162 us; the launch traced here: 161 us
  Pallas kernels  161 us (99%)
    pallas_call x1, Pallas kernels, fused(): pl.pallas_call(body, out_shape=[jax.ShapeDtypeStruct(*a) for a in outs.va...  155 us
    pallas_call x1, Pallas kernels, widen(): pl.pallas_call(body, out_shape=shaped, in_specs=[hbm] * (len(arrays) + le...  5.26 us

profile of v10, /device:TPU:0, one launch (start us, length us, event | category | flops | bytes accessed | tf_op | source)
XLA Modules:
  0.0 161.5 jit_solution(10110644786216727108)
XLA Ops:
  0.7 155.4 %block.1 = (bf16[256,256]{1,0:T(8,128)(2,1)}, bf16[48,256]{1,0:T(8,128)(2,1)}, f32[256,128]{1,0:T(8,128)}, bf16[16,128]{1,0:T(8,128)(2,1)}, f32[4,8,256]{2,1,0:T...) custom-call(bf16[192,256]{1,0:T(8,128)(2,1)} %bitcast.31, ...), custom_call_target="tpu_custom_call" | custom-call | tf_op jit(solution)/shard_map/block/pallas_call | solution.py:1111
  156.0 5.3 %widen.1 = (f32[128,4096]{1,0:T(8,128)}, f32[128,4096]{1,0:T(8,128)}, f32[128,3072]{1,0:T(8,128)}, f32[128,1024]{1,0:T(8,128)}, f32[128,1024]{1,0:T(8,128)}, /*i...) custom-call(bf16[128,4096]{1,0:T(8,128)(2,1)} %get-tuple-element.60., ...), custom_call_target="tpu_custom_call" | custom-call | tf_op jit(solution)/shard_map/widen/pallas_call | solution.py:1241

commit v11 on v10

--- a/solution.py
+++ b/solution.py
@@ -537,7 +537,7 @@
     bv_rs.wait_recv()
     sc.bv_own[...] = summed(sc.bv_recv, nd).astype(sc.bv_own.dtype)
     bv_ag = push(sc.bv_own, sc.bv_all)
-    issue_z(4)
+    issue_z(5)
     issue_own(4)
     pass_next()
 

time: 162 us -> 161 us (level)
  no operation moved by 1% of the time
where the time goes in v11:
time: 161 us; the launch traced here: 160 us
  Pallas kernels  160 us (99%)
    pallas_call x1, Pallas kernels, fused(): pl.pallas_call(body, out_shape=[jax.ShapeDtypeStruct(*a) for a in outs.va...  154 us
    pallas_call x1, Pallas kernels, widen(): pl.pallas_call(body, out_shape=shaped, in_specs=[hbm] * (len(arrays) + le...  5.26 us

profile of v11, /device:TPU:0, one launch (start us, length us, event | category | flops | bytes accessed | tf_op | source)
XLA Modules:
  0.0 160.4 jit_solution(7189612996283340940)
XLA Ops:
  0.7 154.3 %block.1 = (bf16[256,256]{1,0:T(8,128)(2,1)}, bf16[48,256]{1,0:T(8,128)(2,1)}, f32[256,128]{1,0:T(8,128)}, bf16[16,128]{1,0:T(8,128)(2,1)}, f32[4,8,256]{2,1,0:T...) custom-call(bf16[192,256]{1,0:T(8,128)(2,1)} %bitcast.31, ...), custom_call_target="tpu_custom_call" | custom-call | tf_op jit(solution)/shard_map/block/pallas_call | solution.py:1111
  155.0 5.3 %widen.1 = (f32[128,4096]{1,0:T(8,128)}, f32[128,4096]{1,0:T(8,128)}, f32[128,3072]{1,0:T(8,128)}, f32[128,1024]{1,0:T(8,128)}, f32[128,1024]{1,0:T(8,128)}, /*i...) custom-call(bf16[128,4096]{1,0:T(8,128)(2,1)} %get-tuple-element.60., ...), custom_call_target="tpu_custom_call" | custom-call | tf_op jit(solution)/shard_map/widen/pallas_call | solution.py:1241
